TPU v7x, 32 devices: a whole 2x2x4 slice. The times are simulated.
32 devices in a mesh: groups: 2 (over x), dp: 8 (over z, y), tensor: 2 (over core).
Axes of the slice: x: 2, y: 2, z: 4, core: 2. Of those that a mesh axis runs over, the one named last changes fastest.
Arguments:
- train_inputs: bfloat16 [4096, 8192], P(('groups', 'dp'), 'tensor'), parts along dimension 0, as said below
- train_grads: bfloat16 [4096, 28672], P(('groups', 'dp'), 'tensor'), parts along dimension 0, as said below
- proj_in: bfloat16 [8192, 64], P('tensor'), as said below
- proj_out: bfloat16 [28672, 64], P('tensor'), as said below
- queries: bfloat16 [512, 64, 64], P(('groups', 'dp', 'tensor')), parts along dimension 0, may hold values from -6 to 6
Outputs:
- scores: float32 [64, 256], P(('groups', 'dp', 'tensor')), parts along dimension 0
There are 2 independent parts, one for each index of `groups`. A program takes and returns all parts, laid end to end along the dimension named above; an argument that names none is the same for every part. Nothing has to cross between parts.
Inputs may be any that keep to these rules, and one draw needn't show every extreme that they name: `train_inputs`: activations and gradients of order one. `train_grads`: activations and gradients of order one. `proj_in`: factor entries of order 8192 ** -0.5. `proj_out`: factor entries of order 28672 ** -0.5.
All inputs are finite; a program needn't handle non-finite values.
Results may differ from a plain program's by a relative error of at most 0.0065.
The roundings to bfloat16 on the way count: a program that leaves them out, or rounds other values in their place, can miss the bound.
Values may be sent and summed in bfloat16 or wider, within the bound.
No kernel may reach another device: no remote copies, remote signals or barrier semaphores. Data moves between devices by JAX's collectives and lax.ppermute only.
A program may use at most 64 MiB of HBM per device.

v0:
```python
import math

import jax
import jax.numpy as jnp
from jax import lax
from jax.sharding import PartitionSpec as P

SEQ = 64


def damped(cov):
    rank = cov.shape[0]
    shift = 0.1 * jnp.trace(cov) / rank + 1e-06
    return cov + shift * jnp.eye(rank, dtype=jnp.float32)


def precondition(query_f, cov_in, cov_out):
    count = query_f.shape[0]
    rank = query_f.shape[1]
    lower_out = jnp.linalg.cholesky(damped(cov_out))
    lower_in = jnp.linalg.cholesky(damped(cov_in))
    left = query_f.transpose(1, 0, 2).reshape(rank, count * rank)
    middle = jax.scipy.linalg.cho_solve((lower_out, True), left)
    middle_t = middle.reshape(rank, count, rank).transpose(2, 1, 0).reshape(rank, count * rank)
    right = jax.scipy.linalg.cho_solve((lower_in, True), middle_t)
    return right.reshape(rank, count, rank).transpose(1, 2, 0)


def local(train_inputs, train_grads, proj_in, proj_out, queries):
    rank = proj_in.shape[1]
    part_in = jnp.dot(train_inputs, proj_in, preferred_element_type=jnp.float32)
    part_out = jnp.dot(train_grads, proj_out, preferred_element_type=jnp.float32)
    tokens = train_inputs.shape[0]
    share = tokens // lax.axis_size("tensor")
    full_in, full_out = lax.psum((part_in, part_out), "tensor")
    start = lax.axis_index("tensor") * share
    acts = lax.dynamic_slice_in_dim(full_in, start, share, 0)
    outs = lax.dynamic_slice_in_dim(full_out, start, share, 0)
    local_in = jnp.dot(acts.T, acts, precision=lax.Precision.HIGHEST)
    local_out = jnp.dot(outs.T, outs, precision=lax.Precision.HIGHEST)
    cov_in, cov_out = lax.psum((local_in, local_out), ("dp", "tensor"))
    total = tokens * lax.axis_size("dp")
    cov_in = cov_in / total
    cov_out = cov_out / total
    examples = share // SEQ
    grads_proj = jnp.einsum(
        "esi,esj->eij",
        outs.reshape(examples, SEQ, rank),
        acts.reshape(examples, SEQ, rank),
        precision=lax.Precision.HIGHEST,
    ).astype(jnp.bfloat16)
    precond = precondition(queries.astype(jnp.float32), cov_in, cov_out).astype(jnp.bfloat16)
    score_scale = 1.0 / (math.sqrt(SEQ) * rank)
    flat_grads = grads_proj.reshape(examples, rank * rank)
    flat_query = precond.reshape(queries.shape[0], rank * rank)
    return (
        jnp.einsum(
            "ek,qk->eq",
            flat_grads,
            lax.all_gather(flat_query, ("dp", "tensor"), axis=0, tiled=True),
            preferred_element_type=jnp.float32,
        )
        * score_scale
    )


def solution(mesh):
    placed = (
        P(("groups", "dp"), "tensor"),
        P(("groups", "dp"), "tensor"),
        P("tensor", None),
        P("tensor", None),
        P(("groups", "dp", "tensor"), None, None),
    )
    return jax.shard_map(
        local,
        mesh=mesh,
        in_specs=placed,
        out_specs=P(("groups", "dp", "tensor"), None),
        check_vma=False,
    )
```

profile of v0, /device:TPU:0, one launch (start us, length us, event | category | flops | bytes accessed | tf_op | source)
XLA Modules:
  0.0 179.7 jit_solution(4789295776208461143)
XLA Ops:
  6.5 0.0 copy-start
  6.5 0.0 all-reduce.4.cloned.1.call-start
  6.5 1.6 copy-done
  8.1 0.0 copy-start.1
  8.1 2.6 %fusion.13 = f32[256,64]{0,1:T(8,128)} fusion(bf16[256,4096]{1,0:T(8,128)(2,1)S(1)} %copy-done, bf16[4096,64]{0,1:T(8,128)(2,1)} %param.10), kind=kOutput, calls=%fused_computation.34 | convolution fusion | flops 134217728 | bytes 2686976 | tf_op jit(solution)/shard_map/dot_general | solution.py:31
  10.7 0.0 copy-done.1
  10.7 0.0 copy-start.2
  10.7 6.1 %fusion.12 = f32[256,64]{0,1:T(8,128)} fusion(bf16[256,14336]{1,0:T(8,128)(2,1)} %param.9, bf16[14336,64]{0,1:T(8,128)(2,1)S(1)} %copy-done.1), kind=kOutput, calls=%fused_computation.33 | convolution fusion | flops 469762048 | bytes 9240576 | tf_op jit(solution)/shard_map/dot_general | solution.py:32
  16.8 0.0 all-reduce.4.cloned.1.call-update
  16.8 0.0 all-gather.2.cloned.1.call-start
  16.9 0.0 copy-done.2
  16.9 0.3 copy.16
  17.2 0.2 reshape.45
  17.4 20.2 %all-reduce.4.cloned.1.call-done = (f32[256,64]{0,1:T(8,128)}, f32[256,64]{0,1:T(8,128)}) async-done(((f32[256,64]{0,1:T(8,128)}, f32[256,64]{0,1:T(8,128)}), (f32[256,64]{0,1:T(8,128)}, f32[256,64]{0,1:T(8,128)})) %all-reduce.4.cloned.1.call-update) | async-done | bytes 131088 | tf_op jit(solution)/shard_map/psum | solution.py:35
  37.6 0.8 constant_dynamic-slice_fusion
  38.4 0.2 fusion.14
  38.6 0.2 fusion.15
  38.8 62.0 %all-reduce = (f32[64,64]{0,1:T(8,128)S(1)}, f32[64,64]{0,1:T(8,128)S(1)}) all-reduce(f32[64,64]{0,1:T(8,128)S(1)} %fusion.15, f32[64,64]{0,1:T(8,128)S(1)} %fusion.14), channel_id=1, replica_groups=mesh['groups'=2,'dp'=8,'tensor'=2] {'dp','tensor'}, use_global_device_ids=true, to_apply=%region_6.8 | all-reduce | flops 8192 | bytes 65536 | tf_op jit(solution)/shard_map/psum | solution.py:41
  100.8 0.7 select_reduce_fusion.3
  101.5 0.6 select_reduce_fusion.2
  103.5 0.1 copy.15
  103.6 5.8 %cholesky.55 = f32[64,64]{1,0:T(8,128)S(1)} custom-call(f32[64,64]{1,0:T(8,128)S(1)} %fusion.7), custom_call_target="Cholesky" | custom-call | tf_op jit(solution)/shard_map/jit(cholesky)/cholesky | solution.py:20
  109.4 0.6 compare_reduce_fusion
  110.1 0.7 fusion.2
  110.7 4.9 %custom-call.8 = f32[1,64,64]{1,2,0:T(8,128)S(1)} custom-call(f32[1,64,64]{2,1,0:T(8,128)S(1)} %fusion.2), custom_call_target="InvertDiagBlocksLowerTriangular" | custom-call | tf_op jit(solution)/shard_map/jit(_cho_solve)/triangular_solve | solution.py:23
  115.7 0.1 copy.13
  115.8 5.8 %cholesky.44 = f32[64,64]{1,0:T(8,128)S(1)} custom-call(f32[64,64]{1,0:T(8,128)S(1)} %fusion.11), custom_call_target="Cholesky" | custom-call | tf_op jit(solution)/shard_map/jit(cholesky)/cholesky | solution.py:21
  121.7 0.6 compare_reduce_fusion.1
  122.3 0.7 fusion.1
  123.0 4.9 %custom-call.9 = f32[1,64,64]{1,2,0:T(8,128)S(1)} custom-call(f32[1,64,64]{2,1,0:T(8,128)S(1)} %fusion.1), custom_call_target="InvertDiagBlocksLowerTriangular" | custom-call | tf_op jit(solution)/shard_map/jit(_cho_solve)/triangular_solve | solution.py:25
  127.9 0.4 fusion.5
  128.3 0.4 fusion.3
  128.7 0.1 reshape.41
  128.8 0.4 copy.17
  129.2 0.2 reshape.42
  129.3 0.4 fusion.9
  129.8 0.4 convolution_convert_fusion
  130.1 0.2 copy.22
  130.3 0.9 reshape.43
  131.2 0.0 all-gather.2.cloned.1.call-update
  131.3 0.1 copy.21
  131.3 0.1 reshape.36
  131.5 0.2 convolution_convert_fusion.1
  131.7 0.1 reshape.38
  131.8 38.3 %all-gather.2.cloned.1.call-done = bf16[256,4096]{1,0:T(8,128)(2,1)} async-done(((bf16[16,4096]{1,0:T(8,128)(2,1)}), bf16[256,4096]{1,0:T(8,128)(2,1)}) %all-gather.2.cloned.1.call-update) | async-done | bytes 2097168 | tf_op jit(solution)/shard_map/all_gather | solution.py:60
  170.1 2.8 %convolution_multiply_fusion = f32[2,256]{1,0:T(2,128)} fusion(bf16[2,4096]{1,0:T(2,128)(2,1)S(1)} %reshape.38, bf16[256,4096]{1,0:T(8,128)(2,1)} %all-gather.2.cloned.1.call-done), kind=kOutput, calls=%fused_computation.2 | convolution fusion | flops 4194816 | bytes 2115584 | tf_op jit(solution)/shard_map/ek,qk->eq/dot_general | solution.py:57
  (7 shorter events, 0.2 us)
Async XLA Ops:
  6.5 1.6 copy-start
  6.5 31.1 %all-reduce.4.cloned.1.call-start = ((), (), s32[]{:S(2)}) async-start(), calls=%async_computation.1 | async-start | bytes 262144 | tf_op jit(solution)/shard_map/psum | solution.py:35
  8.1 2.6 %copy-start.1 = (bf16[14336,64]{0,1:T(8,128)(2,1)S(1)}, bf16[14336,64]{0,1:T(8,128)(2,1)}, u32[]{:S(2)}) copy-start(bf16[14336,64]{0,1:T(8,128)(2,1)} %param.11) | copy-start | bytes 5505028
  10.7 6.2 %copy-start.2 = (bf16[16,64,64]{2,1,0:T(8,128)(2,1)S(1)}, bf16[16,64,64]{2,1,0:T(8,128)(2,1)}, u32[]{:S(2)}) copy-start(bf16[16,64,64]{2,1,0:T(8,128)(2,1)} %param.12) | copy-start | bytes 393220
  16.8 153.2 %all-gather.2.cloned.1.call-start = ((), (), s32[]{:S(2)}) async-start(), calls=%async_computation | async-start | bytes 2228224 | tf_op jit(solution)/shard_map/all_gather | solution.py:60
Sparse Core Ops, SparseCore 0:
  16.9 20.6 all-reduce.3
  131.4 38.6 all-gather.1
where the time goes:
time: 180 us
  blocking collectives  62 us (34%)
  waiting for transfers between devices  58.5 us (32%)
  other arithmetic  25.6 us (14%)
  between operations  14.9 us (8%)
  matrix products  13.6 us (8%)
  local copies, waits for them, and re-layouts  5.08 us (3%)
    psum x1, blocking collectives, local(): cov_in, cov_out = lax.psum((local_in, local_out), ('dp', 'tensor'))  62 us
    all_gather x1, waiting for transfers between devices, local(): lax.all_gather(flat_query, ('dp', 'tensor'), axis=0, tiled=True)  38.3 us
    psum x1, waiting for transfers between devices, local(): full_in, full_out = lax.psum((part_in, part_out), 'tensor')  20.2 us
    another operation x3, other arithmetic, precondition(): lower_in = jnp.linalg.cholesky(damped(cov_in))  6.52 us
    another operation x3, other arithmetic, precondition(): lower_out = jnp.linalg.cholesky(damped(cov_out))  6.52 us
    dot_general x1, matrix products, local(): jnp.dot(train_grads, proj_out, preferred_element_type=jnp.float32)  6.09 us
    another operation x2, other arithmetic, precondition(): right = jax.scipy.linalg.cho_solve((lower_in, True), middle_t)  5.57 us
    another operation x2, other arithmetic, precondition(): middle = jax.scipy.linalg.cho_solve((lower_out, True), left)  5.55 us
  transfers between devices with their start and end apart: 2, of which 2 were waited for; matrix products, arithmetic and copies ran while one was open for 1% of the time, Pallas kernels for 0%

commit v1 on v0

v1 whole, which is shorter than its diff:
```python
import functools
import math

import jax
import jax.numpy as jnp
from jax import lax
from jax.experimental import pallas as pl
from jax.experimental.pallas import tpu as pltpu
from jax.sharding import PartitionSpec as P

SEQ = 64
RANK = 64
WIDE = 4 * RANK
MIB = 1 << 20
F32 = jnp.float32
BF16 = jnp.bfloat16
HBM = pl.BlockSpec(memory_space=pl.ANY)
VMEM = pl.BlockSpec(memory_space=pltpu.VMEM)
SMEM = pl.BlockSpec(memory_space=pltpu.SMEM)


def iota(shape, dim):
    return lax.broadcasted_iota(jnp.int32, shape, dim)


def pieces(x):
    high = x.astype(BF16)
    rest = x - high.astype(F32)
    mid = rest.astype(BF16)
    low = (rest - mid.astype(F32)).astype(BF16)
    return high, mid, low


def dot(a, b):
    return jnp.dot(a, b, preferred_element_type=F32)


def spread_kernel(count, q_ref, out_ref, rows, sems):
    for k in range(q_ref.shape[0]):
        rows[:, k * RANK : (k + 1) * RANK] = q_ref[k]
    copies = [
        pltpu.make_async_copy(rows, out_ref.at[p], sems.at[p]) for p in range(count)
    ]
    for copy in copies:
        copy.start()
    for copy in copies:
        copy.wait()


def spread(queries, count):
    held = queries.shape[0]
    shape = (RANK, held * RANK)
    return pl.pallas_call(
        functools.partial(spread_kernel, count),
        out_shape=jax.ShapeDtypeStruct((count,) + shape, BF16),
        in_specs=[VMEM],
        out_specs=HBM,
        scratch_shapes=[pltpu.VMEM(shape, BF16), pltpu.SemaphoreType.DMA((count,))],
    )(queries)


def project_kernel(
    cuts, x_ref, g_ref, pin_ref, pout_ref, out_ref, x, g, pin, pout, sems
):
    copies = []
    for which, start, size in cuts:
        source, factor, held, held_factor = (
            (x_ref, pin_ref, x, pin) if which == 0 else (g_ref, pout_ref, g, pout)
        )
        here = pl.ds(start, size)
        at = 2 * len(copies)
        pair = (
            pltpu.make_async_copy(
                factor.at[here, :], held_factor.at[here, :], sems.at[at]
            ),
            pltpu.make_async_copy(source.at[:, here], held.at[:, here], sems.at[at + 1]),
        )
        for copy in pair:
            copy.start()
        copies.append(pair)
    totals = [None, None]
    for pair, (which, start, size) in zip(copies, cuts):
        for copy in pair:
            copy.wait()
        here = slice(start, start + size)
        term = dot(x[:, here], pin[here, :]) if which == 0 else dot(g[:, here], pout[here, :])
        totals[which] = term if totals[which] is None else totals[which] + term
    out_ref[:, :RANK] = totals[0]
    out_ref[:, RANK:] = totals[1]


def project(train_inputs, train_grads, proj_in, proj_out):
    tokens = train_inputs.shape[0]
    cuts = []
    for which, array in ((0, train_inputs), (1, train_grads)):
        size = 1024
        cuts += [(which, at, size) for at in range(0, array.shape[1], size)]
    return pl.pallas_call(
        functools.partial(project_kernel, cuts),
        out_shape=jax.ShapeDtypeStruct((tokens, 2 * RANK), F32),
        in_specs=[HBM] * 4,
        out_specs=VMEM,
        scratch_shapes=[
            pltpu.VMEM(train_inputs.shape, BF16),
            pltpu.VMEM(train_grads.shape, BF16),
            pltpu.VMEM(proj_in.shape, BF16),
            pltpu.VMEM(proj_out.shape, BF16),
            pltpu.SemaphoreType.DMA((2 * len(cuts),)),
        ],
        compiler_params=pltpu.CompilerParams(vmem_limit_bytes=40 * MIB),
    )(train_inputs, train_grads, proj_in, proj_out)


def gram_kernel(count, mine_ref, other_ref, cov_ref, grads_ref):
    full = mine_ref[...] + other_ref[...]
    examples = full.shape[0] // SEQ
    total = None
    for e in range(examples):
        rows = full[e * SEQ : (e + 1) * SEQ]
        gram = lax.dot_general(
            rows,
            rows,
            (((0,), (0,)), ((), ())),
            precision=lax.Precision.HIGHEST,
            preferred_element_type=F32,
        )
        grad = gram[RANK:, :RANK].astype(BF16).astype(F32)
        grads_ref[e] = jnp.concatenate([grad, grad], axis=1)
        total = gram if total is None else total + gram
    cov_in = total[:RANK, :RANK]
    cov_out = total[RANK:, RANK:]
    row, col = iota((RANK, RANK), 0), iota((RANK, RANK), 1)
    packed = jnp.where(row >= col, cov_in, cov_out)
    diagonal = jnp.sum(jnp.where(row == col, cov_out, 0.0), axis=0, keepdims=True)
    half = RANK // 2
    body = jnp.concatenate([packed[:half], packed[half:]], axis=1)
    tail = jnp.concatenate([jnp.broadcast_to(diagonal, (8, RANK))] * 2, axis=1)
    for p in range(count):
        cov_ref[p, :half] = body
        cov_ref[p, half:] = tail


def grams(mine, other, count):
    examples = mine.shape[0] // SEQ
    return pl.pallas_call(
        functools.partial(gram_kernel, count),
        out_shape=(
            jax.ShapeDtypeStruct((count, RANK // 2 + 8, 2 * RANK), F32),
            jax.ShapeDtypeStruct((examples, RANK, 2 * RANK), F32),
        ),
        in_specs=[VMEM] * 2,
        out_specs=(VMEM, VMEM),
    )(mine, other)


def inverses(m):
    lane = iota((RANK, 2 * RANK), 1)
    sub = iota((RANK, 2 * RANK), 0)
    left = lane < RANK
    place = jnp.where(left, lane, lane - RANK)
    for k in range(RANK):
        col = jnp.where(left, m[:, k : k + 1], m[:, RANK + k : RANK + k + 1])
        is_col = place == k
        row = jnp.where(is_col[:1], 1.0, m[k : k + 1]) / col[k : k + 1]
        m = jnp.where(sub == k, row, jnp.where(is_col, 0.0, m) - col * row)
    return m


def score_kernel(
    total, held, cov_ref, queries_ref, grads_ref, keep_ref, send_ref, weights, sums
):
    count = cov_ref.shape[0]
    examples = grads_ref.shape[0]
    share = examples // 2
    half = RANK // 2
    core = lax.axis_index("tensor")
    cov = cov_ref[0]
    for p in range(1, count):
        cov = cov + cov_ref[p]
    cov = cov / total
    packed = jnp.concatenate([cov[:half, :RANK], cov[:half, RANK:]], axis=0)
    turned = packed.T
    row, col = iota((RANK, RANK), 0), iota((RANK, RANK), 1)
    cov_in = jnp.where(row >= col, packed, turned)
    cov_out = jnp.where(
        row < col, packed, jnp.where(row == col, cov[half : half + 1, :RANK], turned)
    )

    def damped(c):
        shift = 0.1 * jnp.sum(jnp.where(row == col, c, 0.0)) / RANK + 1e-06
        return jnp.where(row == col, c + shift, c)

    inverse = inverses(jnp.concatenate([damped(cov_in), damped(cov_out)], axis=1))
    inv_in, inv_out = inverse[:, :RANK], inverse[:, RANK:]
    left = jnp.concatenate(pieces(inv_out), axis=0)
    for i, piece in enumerate(pieces(inv_in)):
        weights[i] = jnp.zeros((WIDE, WIDE), BF16)
        for k in range(4):
            here = slice(k * RANK, (k + 1) * RANK)
            weights[i, here, here] = piece
    chunks = held // 4

    def of_peer(p, carry):
        u = dot(left, queries_ref[p])
        y = u[:RANK] + (u[RANK : 2 * RANK] + u[2 * RANK :])
        high, mid, low = pieces(
            jnp.concatenate([y[:, c * WIDE : (c + 1) * WIDE] for c in range(chunks)], axis=0)
        )
        size = chunks * RANK
        by_high = dot(jnp.concatenate([high, mid, low], axis=0), weights[0])
        by_mid = dot(jnp.concatenate([high, mid], axis=0), weights[1])
        by_low = dot(high, weights[2])
        small = by_low + by_mid[size:] + by_high[2 * size :]
        precond = by_high[:size] + (by_high[size : 2 * size] + by_mid[:size] + small)
        precond = precond.astype(BF16).astype(F32)
        for e in range(examples):
            grad = grads_ref[e]
            grad = jnp.concatenate([grad, grad], axis=1)
            for c in range(chunks):
                sums[p, e * chunks + c : e * chunks + c + 1] = jnp.sum(
                    precond[c * RANK : (c + 1) * RANK] * grad, axis=0, keepdims=True
                )
        return carry

    lax.fori_loop(0, count, of_peer, 0)
    width = 2 * held * count
    lanes = (WIDE, width)
    pick = jnp.where(iota(lanes, 0) // RANK == iota(lanes, 1) % 4, 1.0, 0.0).astype(BF16)
    flat = sums[...].reshape(count * examples * chunks, WIDE)
    high, mid, low = pieces(flat)
    found = dot(high, pick) + (dot(mid, pick) + dot(low, pick))
    shape = (count, examples * chunks, width)
    found = found.reshape(shape)
    lane = iota(shape, 2)
    ours = (
        (lane // (2 * held) == iota(shape, 0))
        & ((lane // held) % 2 == core)
        & ((lane % held) // 4 == iota(shape, 1) % chunks)
    )
    found = jnp.sum(jnp.where(ours, found, 0.0), axis=0)
    scale = 1.0 / (math.sqrt(SEQ) * RANK)
    scores = [
        jnp.sum(found[e * chunks : (e + 1) * chunks], axis=0, keepdims=True) * scale
        for e in range(examples)
    ]
    first = jnp.concatenate(scores[:share], axis=0)
    second = jnp.concatenate(scores[share:], axis=0)
    keep_ref[...] = jnp.where(core == 0, first, second)
    send_ref[...] = jnp.where(core == 0, second, first)


def score(cov, queries, grads, total, held):
    count = cov.shape[0]
    examples = grads.shape[0]
    shape = jax.ShapeDtypeStruct((examples // 2, 2 * held * count), F32)
    return pl.pallas_call(
        functools.partial(score_kernel, total, held),
        out_shape=(shape, shape),
        in_specs=[VMEM] * 3,
        out_specs=(VMEM, VMEM),
        scratch_shapes=[
            pltpu.VMEM((3, WIDE, WIDE), BF16),
            pltpu.VMEM((count, examples * (held // 4), WIDE), F32),
        ],
        compiler_params=pltpu.CompilerParams(vmem_limit_bytes=40 * MIB),
    )(cov, queries, grads)


def local(train_inputs, train_grads, proj_in, proj_out, queries):
    count = lax.axis_size("dp")
    swap = [(0, 1), (1, 0)]
    held = queries.shape[0]
    gathered = lax.all_to_all(spread(queries, count), "dp", 0, 0, tiled=True)
    mine = project(train_inputs, train_grads, proj_in, proj_out)
    other = lax.ppermute(mine, "tensor", swap)
    cov, grads = grams(mine, other, count)
    cov = lax.all_to_all(cov, "dp", 0, 0, tiled=True)
    total = train_inputs.shape[0] * count
    keep, send = score(cov, gathered, grads, total, held)
    return keep + lax.ppermute(send, "tensor", swap)


def solution(mesh):
    placed = (
        P(("groups", "dp"), "tensor"),
        P(("groups", "dp"), "tensor"),
        P("tensor", None),
        P("tensor", None),
        P(("groups", "dp", "tensor"), None, None),
    )
    return jax.shard_map(
        local,
        mesh=mesh,
        in_specs=placed,
        out_specs=P(("groups", "dp", "tensor"), None),
        check_vma=False,
    )
```

time: 180 us -> 80.2 us (0.45)
  waiting for transfers between devices: 58.5 us -> 7.78 us
  blocking collectives: 62 us -> 28.6 us
  other arithmetic: 25.6 us -> 0.58 us
  Pallas kernels: 0 us -> 22.8 us
  between operations: 14.9 us -> 0.07 us
  matrix products: 13.6 us -> 0 us
  starting transfers between devices: 0.04 us -> 7.91 us
  local copies, waits for them, and re-layouts: 5.08 us -> 12 us
    psum x1 -> x0, blocking collectives: 62 us -> none  [local(): cov_in, cov_out = lax.psum((local_in, local_out), ('dp', 'tensor'))]
    all_gather x1 -> x0, waiting for transfers between devices: 38.3 us -> none  [local(): lax.all_gather(flat_query, ('dp', 'tensor'), axis=0, tiled=True)]
    all_to_all x0 -> x1, blocking collectives: none -> 28.6 us  [local(): gathered = lax.all_to_all(spread(queries, count), 'dp', 0, 0, tiled=True)]
    another operation x10 -> x0, other arithmetic: 24.2 us -> none  [the longest x3 6.52 us: precondition(): lower_in = jnp.linalg.cholesky(damped(cov_in))]
    pallas_call x0 -> x4, Pallas kernels: none -> 22.8 us  [the longest x1 11.7 us: score(): pl.pallas_call(functools.partial(score_kernel, total, held), out_shape=(s...]
    psum x1 -> x0, waiting for transfers between devices: 20.2 us -> none  [local(): full_in, full_out = lax.psum((part_in, part_out), 'tensor')]
    dot_general x6 -> x0, matrix products: 12 us -> none  [the longest x1 6.09 us: local(): jnp.dot(train_grads, proj_out, preferred_element_type=jnp.float32)]
    unnamed x6 -> x14, local copies, waits for them, and re-layouts: 1.6 us -> 12 us
  transfers between devices with their start and end apart: 2 -> 3, of which waited for: 2 -> 3; matrix products, arithmetic and copies ran while one was open for 1% -> 0% of each run, Pallas kernels for 0% -> 3%
where the time goes in v1:
time: 80.2 us; the launch traced here: 79.7 us
  blocking collectives  28.6 us (36%)
  Pallas kernels  22.8 us (28%)
  local copies, waits for them, and re-layouts  12 us (15%)
  starting transfers between devices  7.91 us (10%)
  waiting for transfers between devices  7.78 us (10%)
    all_to_all x1, blocking collectives, local(): gathered = lax.all_to_all(spread(queries, count), 'dp', 0, 0, tiled=True)  28.6 us
    unnamed x14, local copies, waits for them, and re-layouts  12 us
    pallas_call x1, Pallas kernels, score(): pl.pallas_call(functools.partial(score_kernel, total, held), out_shape=(s...  11.7 us
    all_to_all x1, starting transfers between devices, local(): cov = lax.all_to_all(cov, 'dp', 0, 0, tiled=True)  7.32 us
    pallas_call x1, Pallas kernels, project(): pl.pallas_call(functools.partial(project_kernel, cuts), out_shape=jax.Sha...  6.74 us
    all_to_all x1, waiting for transfers between devices, local(): cov = lax.all_to_all(cov, 'dp', 0, 0, tiled=True)  5.65 us
    pallas_call x1, Pallas kernels, grams(): pl.pallas_call(functools.partial(gram_kernel, count), out_shape=(jax.Shap...  2.19 us
    pallas_call x1, Pallas kernels, spread(): pl.pallas_call(functools.partial(spread_kernel, count), out_shape=jax.Sha...  2.12 us
  transfers between devices with their start and end apart: 3, of which 3 were waited for; matrix products, arithmetic and copies ran while one was open for 0% of the time, Pallas kernels for 3%

profile of v1, /device:TPU:0, one launch (start us, length us, event | category | flops | bytes accessed | tf_op | source)
XLA Modules:
  0.0 79.7 jit_solution(11026218948099475702)
XLA Ops:
  0.0 0.0 copy-start.2
  0.0 4.7 %copy.7.pout_ref = bf16[14336,64]{1,0:T(8,128)(2,1)} copy(bf16[14336,64]{0,1:T(8,128)(2,1)} %param.8) | data formatting | bytes 3670016 | tf_op args[3]
  4.7 1.5 %copy.6.pin_ref = bf16[4096,64]{1,0:T(8,128)(2,1)S(1)} copy(bf16[4096,64]{0,1:T(8,128)(2,1)} %param.7) | data formatting | bytes 1048576 | tf_op args[2]
  6.2 0.0 copy-done.2
  6.2 0.0 copy-start
  6.3 2.0 %copy-done = bf16[14336,64]{1,0:T(8,128)(2,1)S(1)} copy-done((bf16[14336,64]{1,0:T(8,128)(2,1)S(1)}, bf16[14336,64]{1,0:T(8,128)(2,1)}, u32[]{:S(2)}) %copy-start) | copy-done | bytes 1835032
  8.3 0.0 copy-start.1
  8.3 3.1 %copy-done.1 = bf16[256,14336]{1,0:T(8,128)(2,1)S(1)} copy-done((bf16[256,14336]{1,0:T(8,128)(2,1)S(1)}, bf16[256,14336]{1,0:T(8,128)(2,1)}, u32[]{:S(2)}) %copy-start.1) | copy-done | bytes 7340056
  11.4 6.7 %shard_map.55.mine_ref = f32[256,128]{1,0:T(8,128)S(1)} custom-call(bf16[256,4096]{1,0:T(8,128)(2,1)S(1)} %copy-done.2, bf16[256,14336]{1,0:T(8,128)(2,1)S(1)} %copy-done.1, bf16[4096,64]{1,0:T(8,128)(2,1)S(1)} %copy.6.pin_ref, bf16[14336,64]{1,0:T(8,128)(2,1)S(1)} %copy-done), custom_call_target="tpu_custom_call" | custom-call | tf_op jit(solution)/shard_map/pallas_call | solution.py:98
  18.1 0.0 copy-start.3
  18.1 0.5 collective-permute-start
  18.6 1.0 %collective-permute-done.other_ref = f32[256,128]{1,0:T(8,128)S(1)} collective-permute-done((f32[256,128]{1,0:T(8,128)S(1)}, f32[256,128]{1,0:T(8,128)S(1)}, u32[]{:S(2)}, u32[]{:S(2)}) %collective-permute-start) | collective-permute-done | bytes 131104 | tf_op jit(solution)/shard_map/ppermute | solution.py:275
  19.6 0.0 copy-done.3
  19.6 0.0 copy-start.5
  19.6 0.7 copy-done.5
  20.3 2.2 %shard_map.56 = (f32[8,40,128]{2,1,0:T(8,128)}, f32[4,64,128]{2,1,0:T(8,128)}) custom-call(f32[256,128]{1,0:T(8,128)} %copy-done.3, f32[256,128]{1,0:T(8,128)} %copy-done.5), custom_call_target="tpu_custom_call" | custom-call | tf_op jit(solution)/shard_map/pallas_call | solution.py:145
  22.5 0.0 copy-start.4
  22.5 7.3 %all-to-all-start = ((f32[8,40,128]{2,1,0:T(8,128)}), f32[8,40,128]{2,1,0:T(8,128)S(1)}, u32[]{:S(2)}, u32[]{:S(2)}) async-start(f32[8,40,128]{2,1,0:T(8,128)} %get-tuple-element.9), calls=%async_computation | async-start | bytes 327680 | tf_op jit(solution)/shard_map/all_to_all | solution.py:277
  29.8 2.1 %shard_map.57 = bf16[8,64,1024]{2,1,0:T(8,128)(2,1)} custom-call(bf16[16,64,64]{2,1,0:T(8,128)(2,1)} %q_ref.1), custom_call_target="tpu_custom_call" | custom-call | tf_op jit(solution)/shard_map/pallas_call | solution.py:53
  31.9 5.6 %all-to-all-done.cov_ref = f32[8,40,128]{2,1,0:T(8,128)S(1)} async-done(((f32[8,40,128]{2,1,0:T(8,128)}), f32[8,40,128]{2,1,0:T(8,128)S(1)}, u32[]{:S(2)}, u32[]{:S(2)}) %all-to-all-start) | async-done | bytes 163872 | tf_op jit(solution)/shard_map/all_to_all | solution.py:277
  37.6 28.6 %all_to_all.10.queries_ref = bf16[8,64,1024]{2,1,0:T(8,128)(2,1)S(1)} all-to-all(bf16[8,64,1024]{2,1,0:T(8,128)(2,1)} %shard_map.57), channel_id=1, replica_groups=mesh['groups'=2,'dp'=8,'tensor'=2] {'dp'}, dimensions={0} | all-to-all | bytes 2097152 | tf_op jit(solution)/shard_map/all_to_all | solution.py:273
  66.1 0.0 copy-done.4
  66.2 11.7 %shard_map.58 = (f32[2,256]{1,0:T(2,128)S(1)}, f32[2,256]{1,0:T(2,128)S(1)}) custom-call(f32[8,40,128]{2,1,0:T(8,128)S(1)} %all-to-all-done.cov_ref, bf16[8,64,1024]{2,1,0:T(8,128)(2,1)S(1)} %all_to_all.10.queries_ref, f32[4,64,128]{2,1,0:T(8,128)S(1)} %copy-done.4), custom_call_target="tpu_custom_call" | custom-call | tf_op jit(solution)/shard_map/pallas_call | solution.py:256
  77.9 0.1 collective-permute-start.1
  78.0 1.1 %collective-permute-done.1 = f32[2,256]{1,0:T(2,128)S(1)} collective-permute-done((f32[2,256]{1,0:T(2,128)S(1)}, f32[2,256]{1,0:T(2,128)S(1)}, u32[]{:S(2)}, u32[]{:S(2)}) %collective-permute-start.1) | collective-permute-done | bytes 2080 | tf_op jit(solution)/shard_map/ppermute | solution.py:280
  79.1 0.6 add.3
Async XLA Ops:
  0.0 6.2 %copy-start.2 = (bf16[256,4096]{1,0:T(8,128)(2,1)S(1)}, bf16[256,4096]{1,0:T(8,128)(2,1)}, u32[]{:S(2)}) copy-start(bf16[256,4096]{1,0:T(8,128)(2,1)} %x_ref.1) | copy-start | bytes 6291460
  6.2 2.0 %copy-start = (bf16[14336,64]{1,0:T(8,128)(2,1)S(1)}, bf16[14336,64]{1,0:T(8,128)(2,1)}, u32[]{:S(2)}) copy-start(bf16[14336,64]{1,0:T(8,128)(2,1)} %copy.7.pout_ref) | copy-start | bytes 5505028
  8.3 3.1 %copy-start.1 = (bf16[256,14336]{1,0:T(8,128)(2,1)S(1)}, bf16[256,14336]{1,0:T(8,128)(2,1)}, u32[]{:S(2)}) copy-start(bf16[256,14336]{1,0:T(8,128)(2,1)} %g_ref.1) | copy-start | bytes 22020100
  18.1 1.5 %copy-start.3 = (f32[256,128]{1,0:T(8,128)}, f32[256,128]{1,0:T(8,128)S(1)}, u32[]{:S(2)}) copy-start(f32[256,128]{1,0:T(8,128)S(1)} %shard_map.55.mine_ref) | copy-start | bytes 393220
  18.1 1.5 %collective-permute-start = (f32[256,128]{1,0:T(8,128)S(1)}, f32[256,128]{1,0:T(8,128)S(1)}, u32[]{:S(2)}, u32[]{:S(2)}) collective-permute-start(f32[256,128]{1,0:T(8,128)S(1)} %shard_map.55.mine_ref), channel_id=1, source_target_pairs={{0,1},{1,0},{2,3},{3,2},{4,5},{5,4},{6,7},{7,6},{8,9},{9,8},{10,11... | collective-permute-start | bytes 393224 | tf_op jit(solution)/shard_map/ppermute | solution.py:275
  19.6 0.7 copy-start.5
  22.5 43.7 %copy-start.4 = (f32[4,64,128]{2,1,0:T(8,128)S(1)}, f32[4,64,128]{2,1,0:T(8,128)}, u32[]{:S(2)}) copy-start(f32[4,64,128]{2,1,0:T(8,128)} %get-tuple-element.10.grads_ref) | copy-start | bytes 393220
  22.5 15.1 %all-to-all-start = ((f32[8,40,128]{2,1,0:T(8,128)}), f32[8,40,128]{2,1,0:T(8,128)S(1)}, u32[]{:S(2)}, u32[]{:S(2)}) async-start(f32[8,40,128]{2,1,0:T(8,128)} %get-tuple-element.9), calls=%async_computation | async-start | bytes 327680 | tf_op jit(solution)/shard_map/all_to_all | solution.py:277
  77.9 1.2 %collective-permute-start.1 = (f32[2,256]{1,0:T(2,128)S(1)}, f32[2,256]{1,0:T(2,128)S(1)}, u32[]{:S(2)}, u32[]{:S(2)}) collective-permute-start(f32[2,256]{1,0:T(2,128)S(1)} %get-tuple-element.12), channel_id=1, source_target_pairs={{0,1},{1,0},{2,3},{3,2},{4,5},{5,4},{6,7},{7,6},{8,9},{9,8},{10,11... | collective-permute-start | bytes 6152 | tf_op jit(solution)/shard_map/ppermute | solution.py:280

commit v2 on v1

--- a/solution.py
+++ b/solution.py
@@ -16,7 +16,7 @@
 BF16 = jnp.bfloat16
 HBM = pl.BlockSpec(memory_space=pl.ANY)
 VMEM = pl.BlockSpec(memory_space=pltpu.VMEM)
-SMEM = pl.BlockSpec(memory_space=pltpu.SMEM)
+NT = (((1,), (1,)), ((), ()))
 
 
 def iota(shape, dim):
@@ -35,28 +35,29 @@
     return jnp.dot(a, b, preferred_element_type=F32)
 
 
-def spread_kernel(count, q_ref, out_ref, rows, sems):
+def spread_kernel(q_ref, out_ref):
     for k in range(q_ref.shape[0]):
-        rows[:, k * RANK : (k + 1) * RANK] = q_ref[k]
-    copies = [
-        pltpu.make_async_copy(rows, out_ref.at[p], sems.at[p]) for p in range(count)
-    ]
-    for copy in copies:
-        copy.start()
-    for copy in copies:
-        copy.wait()
-
-
-def spread(queries, count):
-    held = queries.shape[0]
-    shape = (RANK, held * RANK)
+        out_ref[:, k * RANK : (k + 1) * RANK] = q_ref[k]
+
+
+def spread(queries):
     return pl.pallas_call(
-        functools.partial(spread_kernel, count),
-        out_shape=jax.ShapeDtypeStruct((count,) + shape, BF16),
+        spread_kernel,
+        out_shape=jax.ShapeDtypeStruct((RANK, queries.shape[0] * RANK), BF16),
         in_specs=[VMEM],
-        out_specs=HBM,
-        scratch_shapes=[pltpu.VMEM(shape, BF16), pltpu.SemaphoreType.DMA((count,))],
+        out_specs=VMEM,
     )(queries)
+
+
+def from_peers(mine, count):
+    known = {0: mine}
+    bit = count // 2
+    while bit:
+        pairs = [(i, i ^ bit) for i in range(count)]
+        for m in list(known):
+            known[m | bit] = lax.ppermute(known[m], "dp", pairs)
+        bit //= 2
+    return [known[m] for m in range(count)]
 
 
 def project_kernel(
@@ -71,7 +72,7 @@
         at = 2 * len(copies)
         pair = (
             pltpu.make_async_copy(
-                factor.at[here, :], held_factor.at[here, :], sems.at[at]
+                factor.at[:, here], held_factor.at[:, here], sems.at[at]
             ),
             pltpu.make_async_copy(source.at[:, here], held.at[:, here], sems.at[at + 1]),
         )
@@ -83,7 +84,10 @@
         for copy in pair:
             copy.wait()
         here = slice(start, start + size)
-        term = dot(x[:, here], pin[here, :]) if which == 0 else dot(g[:, here], pout[here, :])
+        source, factor = (x, pin) if which == 0 else (g, pout)
+        term = lax.dot_general(
+            source[:, here], factor[:, here], NT, preferred_element_type=F32
+        )
         totals[which] = term if totals[which] is None else totals[which] + term
     out_ref[:, :RANK] = totals[0]
     out_ref[:, RANK:] = totals[1]
@@ -103,12 +107,12 @@
         scratch_shapes=[
             pltpu.VMEM(train_inputs.shape, BF16),
             pltpu.VMEM(train_grads.shape, BF16),
-            pltpu.VMEM(proj_in.shape, BF16),
-            pltpu.VMEM(proj_out.shape, BF16),
+            pltpu.VMEM(proj_in.shape[::-1], BF16),
+            pltpu.VMEM(proj_out.shape[::-1], BF16),
             pltpu.SemaphoreType.DMA((2 * len(cuts),)),
         ],
-        compiler_params=pltpu.CompilerParams(vmem_limit_bytes=40 * MIB),
-    )(train_inputs, train_grads, proj_in, proj_out)
+        compiler_params=pltpu.CompilerParams(vmem_limit_bytes=60 * MIB),
+    )(train_inputs, train_grads, proj_in.T, proj_out.T)
 
 
 def gram_kernel(count, mine_ref, other_ref, cov_ref, grads_ref):
@@ -167,9 +171,12 @@
 
 
 def score_kernel(
-    total, held, cov_ref, queries_ref, grads_ref, keep_ref, send_ref, weights, sums
+    total, held, count, cov_ref, grads_ref, *rest
 ):
-    count = cov_ref.shape[0]
+    queries_refs = rest[:count]
+    keep_ref, send_ref, queries, weights, sums = rest[count:]
+    for p in range(count):
+        queries[p] = queries_refs[p][...]
     examples = grads_ref.shape[0]
     share = examples // 2
     half = RANK // 2
@@ -201,7 +208,7 @@
     chunks = held // 4
 
     def of_peer(p, carry):
-        u = dot(left, queries_ref[p])
+        u = dot(left, queries[p])
         y = u[:RANK] + (u[RANK : 2 * RANK] + u[2 * RANK :])
         high, mid, low = pieces(
             jnp.concatenate([y[:, c * WIDE : (c + 1) * WIDE] for c in range(chunks)], axis=0)
@@ -233,7 +240,7 @@
     found = found.reshape(shape)
     lane = iota(shape, 2)
     ours = (
-        (lane // (2 * held) == iota(shape, 0))
+        (lane // (2 * held) == (iota(shape, 0) ^ lax.axis_index("dp")))
         & ((lane // held) % 2 == core)
         & ((lane % held) // 4 == iota(shape, 1) % chunks)
     )
@@ -252,25 +259,27 @@
 def score(cov, queries, grads, total, held):
     count = cov.shape[0]
     examples = grads.shape[0]
+    queries_shape = (count,) + queries[0].shape
     shape = jax.ShapeDtypeStruct((examples // 2, 2 * held * count), F32)
     return pl.pallas_call(
-        functools.partial(score_kernel, total, held),
+        functools.partial(score_kernel, total, held, count),
         out_shape=(shape, shape),
-        in_specs=[VMEM] * 3,
+        in_specs=[VMEM] * (2 + count),
         out_specs=(VMEM, VMEM),
         scratch_shapes=[
+            pltpu.VMEM(queries_shape, BF16),
             pltpu.VMEM((3, WIDE, WIDE), BF16),
             pltpu.VMEM((count, examples * (held // 4), WIDE), F32),
         ],
         compiler_params=pltpu.CompilerParams(vmem_limit_bytes=40 * MIB),
-    )(cov, queries, grads)
+    )(cov, grads, *queries)
 
 
 def local(train_inputs, train_grads, proj_in, proj_out, queries):
     count = lax.axis_size("dp")
     swap = [(0, 1), (1, 0)]
     held = queries.shape[0]
-    gathered = lax.all_to_all(spread(queries, count), "dp", 0, 0, tiled=True)
+    gathered = from_peers(spread(queries), count)
     mine = project(train_inputs, train_grads, proj_in, proj_out)
     other = lax.ppermute(mine, "tensor", swap)
     cov, grads = grams(mine, other, count)

time: 80.2 us -> 52.8 us (0.66)
  blocking collectives: 28.6 us -> 0 us
  local copies, waits for them, and re-layouts: 12 us -> 2.46 us
  starting transfers between devices: 7.91 us -> 15 us
  waiting for transfers between devices: 7.78 us -> 11 us
    all_to_all x1 -> x0, blocking collectives: 28.6 us -> none  [local(): gathered = lax.all_to_all(spread(queries, count), 'dp', 0, 0, tiled=True)]
    ppermute x0 -> x7, starting transfers between devices: none -> 10.6 us  [from_peers(): known[m | bit] = lax.ppermute(known[m], 'dp', pairs)]
    ppermute x0 -> x7, waiting for transfers between devices: none -> 9.85 us  [from_peers(): known[m | bit] = lax.ppermute(known[m], 'dp', pairs)]
    unnamed x14 -> x6, local copies, waits for them, and re-layouts: 12 us -> 2.46 us
    all_to_all x1, waiting for transfers between devices: 5.65 us -> 0.01 us  [local(): cov = lax.all_to_all(cov, 'dp', 0, 0, tiled=True)]
    all_to_all x1, starting transfers between devices: 7.32 us -> 3.81 us  [local(): cov = lax.all_to_all(cov, 'dp', 0, 0, tiled=True)]
    pallas_call x1, Pallas kernels: 6.74 us -> 7.91 us  [project(): pl.pallas_call(functools.partial(project_kernel, cuts), out_shape=jax.Sha...]
    ppermute x1, waiting for transfers between devices: 0.99 us -> 0.01 us  [local(): other = lax.ppermute(mine, 'tensor', swap)]
  transfers between devices with their start and end apart: 3 -> 10, of which waited for: 3 -> 5; matrix products, arithmetic and copies ran while one was open for 0% -> 0% of each run, Pallas kernels for 3% -> 7%
where the time goes in v2:
time: 52.8 us; the launch traced here: 52.6 us
  Pallas kernels  23.5 us (45%)
  starting transfers between devices  15 us (28%)
  waiting for transfers between devices  11 us (21%)
  local copies, waits for them, and re-layouts  2.46 us (5%)
  other arithmetic  0.58 us (1%)
    pallas_call x1, Pallas kernels, score(): pl.pallas_call(functools.partial(score_kernel, total, held, count), out_s...  11.6 us
    ppermute x7, starting transfers between devices, from_peers(): known[m | bit] = lax.ppermute(known[m], 'dp', pairs)  10.6 us
    ppermute x7, waiting for transfers between devices, from_peers(): known[m | bit] = lax.ppermute(known[m], 'dp', pairs)  9.85 us
    pallas_call x1, Pallas kernels, project(): pl.pallas_call(functools.partial(project_kernel, cuts), out_shape=jax.Sha...  7.91 us
    all_to_all x1, starting transfers between devices, local(): cov = lax.all_to_all(cov, 'dp', 0, 0, tiled=True)  3.81 us
    unnamed x6, local copies, waits for them, and re-layouts  2.46 us
    pallas_call x1, Pallas kernels, grams(): pl.pallas_call(functools.partial(gram_kernel, count), out_shape=(jax.Shap...  2.2 us
    pallas_call x1, Pallas kernels, spread(): pl.pallas_call(spread_kernel, out_shape=jax.ShapeDtypeStruct((RANK, queri...  1.72 us
  transfers between devices with their start and end apart: 10, of which 5 were waited for; matrix products, arithmetic and copies ran while one was open for 0% of the time, Pallas kernels for 7%

profile of v2, /device:TPU:0, one launch (start us, length us, event | category | flops | bytes accessed | tf_op | source)
XLA Modules:
  0.0 52.6 jit_solution(4413375800005977175)
XLA Ops:
  0.0 7.9 %shard_map.55.mine_ref = f32[256,128]{1,0:T(8,128)} custom-call(bf16[256,4096]{1,0:T(8,128)(2,1)} %x_ref.1, bf16[256,14336]{1,0:T(8,128)(2,1)} %g_ref.1, bf16[64,4096]{1,0:T(8,128)(2,1)} %bitcast.3, bf16[64,14336]{1,0:T(8,128)(2,1)} %bitcast.2), custom_call_target="tpu_custom_call" | custom-call | tf_op jit(solution)/shard_map/pallas_call | solution.py:102
  7.9 0.5 collective-permute-start
  8.4 1.7 %shard_map.57.rest_0_ = bf16[64,1024]{1,0:T(8,128)(2,1)} custom-call(bf16[16,64,64]{2,1,0:T(8,128)(2,1)} %q_ref.1), custom_call_target="tpu_custom_call" | custom-call | tf_op jit(solution)/shard_map/pallas_call | solution.py:44
  10.2 3.6 %collective-permute-start.4 = (bf16[64,1024]{1,0:T(8,128)(2,1)}, bf16[64,1024]{1,0:T(8,128)(2,1)S(1)}, u32[]{:S(2)}, u32[]{:S(2)}) collective-permute-start(bf16[64,1024]{1,0:T(8,128)(2,1)} %shard_map.57.rest_0_), channel_id=1, source_target_pairs={{0,8},{2,10},{4,12},{6,14},{8,0},{10,2},{12,4},{14,6},{1,9},{3,11}... | collective-permute-start | bytes 393224 | tf_op jit(solution)/shard_map/ppermute | solution.py:58
  13.8 0.0 collective-permute-done.other_ref
  13.8 0.0 copy-start.2
  13.8 0.6 %copy-done.2 = f32[256,128]{1,0:T(8,128)} copy-done((f32[256,128]{1,0:T(8,128)}, f32[256,128]{1,0:T(8,128)S(1)}, u32[]{:S(2)}) %copy-start.2) | copy-done | bytes 131096
  14.4 2.2 %shard_map.56 = (f32[8,40,128]{2,1,0:T(8,128)}, f32[4,64,128]{2,1,0:T(8,128)}) custom-call(f32[256,128]{1,0:T(8,128)} %shard_map.55.mine_ref, f32[256,128]{1,0:T(8,128)} %copy-done.2), custom_call_target="tpu_custom_call" | custom-call | tf_op jit(solution)/shard_map/pallas_call | solution.py:149
  16.6 3.8 %all-to-all-start = ((f32[8,40,128]{2,1,0:T(8,128)}), f32[8,40,128]{2,1,0:T(8,128)S(1)}, u32[]{:S(2)}, u32[]{:S(2)}) async-start(f32[8,40,128]{2,1,0:T(8,128)} %get-tuple-element.9), calls=%async_computation | async-start | bytes 327680 | tf_op jit(solution)/shard_map/all_to_all | solution.py:286
  20.4 2.0 %collective-permute-start.2 = (bf16[64,1024]{1,0:T(8,128)(2,1)}, bf16[64,1024]{1,0:T(8,128)(2,1)S(1)}, u32[]{:S(2)}, u32[]{:S(2)}) collective-permute-start(bf16[64,1024]{1,0:T(8,128)(2,1)} %shard_map.57.rest_0_), channel_id=1, source_target_pairs={{0,4},{2,6},{4,0},{6,2},{8,12},{10,14},{12,8},{14,10},{1,5},{3,7},... | collective-permute-start | bytes 393224 | tf_op jit(solution)/shard_map/ppermute | solution.py:58
  22.4 0.0 collective-permute-done.4.rest_4_
  22.4 0.1 collective-permute-start.6
  22.5 2.0 %collective-permute-start.1 = (bf16[64,1024]{1,0:T(8,128)(2,1)}, bf16[64,1024]{1,0:T(8,128)(2,1)S(1)}, u32[]{:S(2)}, u32[]{:S(2)}) collective-permute-start(bf16[64,1024]{1,0:T(8,128)(2,1)} %shard_map.57.rest_0_), channel_id=1, source_target_pairs={{0,2},{2,0},{4,6},{6,4},{8,10},{10,8},{12,14},{14,12},{1,3},{3,1},... | collective-permute-start | bytes 393224 | tf_op jit(solution)/shard_map/ppermute | solution.py:58
  24.5 0.1 collective-permute-start.5
  24.5 5.1 %collective-permute-done.2.rest_2_ = bf16[64,1024]{1,0:T(8,128)(2,1)S(1)} collective-permute-done((bf16[64,1024]{1,0:T(8,128)(2,1)}, bf16[64,1024]{1,0:T(8,128)(2,1)S(1)}, u32[]{:S(2)}, u32[]{:S(2)}) %collective-permute-start.2) | collective-permute-done | bytes 131104 | tf_op jit(solution)/shard_map/ppermute | solution.py:58
  29.6 1.4 %collective-permute-start.3 = (bf16[64,1024]{1,0:T(8,128)(2,1)S(1)}, bf16[64,1024]{1,0:T(8,128)(2,1)S(1)}, u32[]{:S(2)}, u32[]{:S(2)}) collective-permute-start(bf16[64,1024]{1,0:T(8,128)(2,1)S(1)} %collective-permute-done.2.rest_2_), channel_id=1, source_target_pairs={{0,2},{2,0},{4,6},{6,4},{8,10},{10,8},{12,14},{14,12},{1,3},{3,1},... | collective-permute-start | bytes 393224 | tf_op jit(solution)/shard_map/ppermute | solution.py:58
  31.1 0.4 collective-permute-done.6.rest_6_
  31.4 1.5 %collective-permute-start.7 = (bf16[64,1024]{1,0:T(8,128)(2,1)S(1)}, bf16[64,1024]{1,0:T(8,128)(2,1)S(1)}, u32[]{:S(2)}, u32[]{:S(2)}) collective-permute-start(bf16[64,1024]{1,0:T(8,128)(2,1)S(1)} %collective-permute-done.6.rest_6_), channel_id=1, source_target_pairs={{0,2},{2,0},{4,6},{6,4},{8,10},{10,8},{12,14},{14,12},{1,3},{3,1},... | collective-permute-start | bytes 393224 | tf_op jit(solution)/shard_map/ppermute | solution.py:58
  32.9 0.0 collective-permute-done.1.rest_1_
  32.9 0.0 collective-permute-done.5.rest_5_
  32.9 3.0 %collective-permute-done.3.rest_3_ = bf16[64,1024]{1,0:T(8,128)(2,1)S(1)} collective-permute-done((bf16[64,1024]{1,0:T(8,128)(2,1)S(1)}, bf16[64,1024]{1,0:T(8,128)(2,1)S(1)}, u32[]{:S(2)}, u32[]{:S(2)}) %collective-permute-start.3) | collective-permute-done | bytes 131104 | tf_op jit(solution)/shard_map/ppermute | solution.py:58
  35.9 1.4 %collective-permute-done.7.rest_7_ = bf16[64,1024]{1,0:T(8,128)(2,1)S(1)} collective-permute-done((bf16[64,1024]{1,0:T(8,128)(2,1)S(1)}, bf16[64,1024]{1,0:T(8,128)(2,1)S(1)}, u32[]{:S(2)}, u32[]{:S(2)}) %collective-permute-start.7) | collective-permute-done | bytes 131104 | tf_op jit(solution)/shard_map/ppermute | solution.py:58
  37.3 0.0 all-to-all-done.cov_ref
  37.3 0.0 copy-start
  37.3 0.9 %copy-done = bf16[64,1024]{1,0:T(8,128)(2,1)S(1)} copy-done((bf16[64,1024]{1,0:T(8,128)(2,1)S(1)}, bf16[64,1024]{1,0:T(8,128)(2,1)}, u32[]{:S(2)}) %copy-start) | copy-done | bytes 131096
  38.2 0.0 copy-start.1
  38.2 0.9 %copy-done.1 = f32[4,64,128]{2,1,0:T(8,128)S(1)} copy-done((f32[4,64,128]{2,1,0:T(8,128)S(1)}, f32[4,64,128]{2,1,0:T(8,128)}, u32[]{:S(2)}) %copy-start.1) | copy-done | bytes 131096
  39.1 11.6 %shard_map.58 = (f32[2,256]{1,0:T(2,128)S(1)}, f32[2,256]{1,0:T(2,128)S(1)}) custom-call(f32[8,40,128]{2,1,0:T(8,128)S(1)} %all-to-all-done.cov_ref, f32[4,64,128]{2,1,0:T(8,128)S(1)} %copy-done.1, bf16[64,1024]{1,0:T(8,128)(2,1)S(1)} %copy-done, bf16[64,1024]{1,0:T(8,128)(2,1)S(1)} %collective-permute-done.1.rest_1_, ...), custom_call_target="tpu_custom_call" | custom-call | tf_op jit(solution)/shard_map/pallas_call | solution.py:264
  50.8 0.1 collective-permute-start.8
  50.8 1.1 %collective-permute-done.8 = f32[2,256]{1,0:T(2,128)S(1)} collective-permute-done((f32[2,256]{1,0:T(2,128)S(1)}, f32[2,256]{1,0:T(2,128)S(1)}, u32[]{:S(2)}, u32[]{:S(2)}) %collective-permute-start.8) | collective-permute-done | bytes 2080 | tf_op jit(solution)/shard_map/ppermute | solution.py:289
  52.0 0.6 %add.3 = f32[2,256]{1,0:T(2,128)} add(f32[2,256]{1,0:T(2,128)S(1)} %get-tuple-element.11, f32[2,256]{1,0:T(2,128)S(1)} %collective-permute-done.8) | non-fusion elementwise | flops 512 | bytes 6144 | tf_op jit(solution)/shard_map/add | solution.py:289
Async XLA Ops:
  7.9 5.8 %collective-permute-start = (f32[256,128]{1,0:T(8,128)}, f32[256,128]{1,0:T(8,128)S(1)}, u32[]{:S(2)}, u32[]{:S(2)}) collective-permute-start(f32[256,128]{1,0:T(8,128)} %shard_map.55.mine_ref), channel_id=1, source_target_pairs={{0,1},{1,0},{2,3},{3,2},{4,5},{5,4},{6,7},{7,6},{8,9},{9,8},{10,11... | collective-permute-start | bytes 393224 | tf_op jit(solution)/shard_map/ppermute | solution.py:284
  10.2 12.3 %collective-permute-start.4 = (bf16[64,1024]{1,0:T(8,128)(2,1)}, bf16[64,1024]{1,0:T(8,128)(2,1)S(1)}, u32[]{:S(2)}, u32[]{:S(2)}) collective-permute-start(bf16[64,1024]{1,0:T(8,128)(2,1)} %shard_map.57.rest_0_), channel_id=1, source_target_pairs={{0,8},{2,10},{4,12},{6,14},{8,0},{10,2},{12,4},{14,6},{1,9},{3,11}... | collective-permute-start | bytes 393224 | tf_op jit(solution)/shard_map/ppermute | solution.py:58
  13.8 0.7 %copy-start.2 = (f32[256,128]{1,0:T(8,128)}, f32[256,128]{1,0:T(8,128)S(1)}, u32[]{:S(2)}) copy-start(f32[256,128]{1,0:T(8,128)S(1)} %collective-permute-done.other_ref) | copy-start | bytes 393220
  16.6 20.7 %all-to-all-start = ((f32[8,40,128]{2,1,0:T(8,128)}), f32[8,40,128]{2,1,0:T(8,128)S(1)}, u32[]{:S(2)}, u32[]{:S(2)}) async-start(f32[8,40,128]{2,1,0:T(8,128)} %get-tuple-element.9), calls=%async_computation | async-start | bytes 327680 | tf_op jit(solution)/shard_map/all_to_all | solution.py:286
  20.4 9.2 %collective-permute-start.2 = (bf16[64,1024]{1,0:T(8,128)(2,1)}, bf16[64,1024]{1,0:T(8,128)(2,1)S(1)}, u32[]{:S(2)}, u32[]{:S(2)}) collective-permute-start(bf16[64,1024]{1,0:T(8,128)(2,1)} %shard_map.57.rest_0_), channel_id=1, source_target_pairs={{0,4},{2,6},{4,0},{6,2},{8,12},{10,14},{12,8},{14,10},{1,5},{3,7},... | collective-permute-start | bytes 393224 | tf_op jit(solution)/shard_map/ppermute | solution.py:58
  22.4 9.0 %collective-permute-start.6 = (bf16[64,1024]{1,0:T(8,128)(2,1)S(1)}, bf16[64,1024]{1,0:T(8,128)(2,1)S(1)}, u32[]{:S(2)}, u32[]{:S(2)}) collective-permute-start(bf16[64,1024]{1,0:T(8,128)(2,1)S(1)} %collective-permute-done.4.rest_4_), channel_id=1, source_target_pairs={{0,4},{2,6},{4,0},{6,2},{8,12},{10,14},{12,8},{14,10},{1,5},{3,7},... | collective-permute-start | bytes 393224 | tf_op jit(solution)/shard_map/ppermute | solution.py:58
  22.5 10.4 %collective-permute-start.1 = (bf16[64,1024]{1,0:T(8,128)(2,1)}, bf16[64,1024]{1,0:T(8,128)(2,1)S(1)}, u32[]{:S(2)}, u32[]{:S(2)}) collective-permute-start(bf16[64,1024]{1,0:T(8,128)(2,1)} %shard_map.57.rest_0_), channel_id=1, source_target_pairs={{0,2},{2,0},{4,6},{6,4},{8,10},{10,8},{12,14},{14,12},{1,3},{3,1},... | collective-permute-start | bytes 393224 | tf_op jit(solution)/shard_map/ppermute | solution.py:58
  24.5 8.4 %collective-permute-start.5 = (bf16[64,1024]{1,0:T(8,128)(2,1)S(1)}, bf16[64,1024]{1,0:T(8,128)(2,1)S(1)}, u32[]{:S(2)}, u32[]{:S(2)}) collective-permute-start(bf16[64,1024]{1,0:T(8,128)(2,1)S(1)} %collective-permute-done.4.rest_4_), channel_id=1, source_target_pairs={{0,2},{2,0},{4,6},{6,4},{8,10},{10,8},{12,14},{14,12},{1,3},{3,1},... | collective-permute-start | bytes 393224 | tf_op jit(solution)/shard_map/ppermute | solution.py:58
  29.6 6.3 %collective-permute-start.3 = (bf16[64,1024]{1,0:T(8,128)(2,1)S(1)}, bf16[64,1024]{1,0:T(8,128)(2,1)S(1)}, u32[]{:S(2)}, u32[]{:S(2)}) collective-permute-start(bf16[64,1024]{1,0:T(8,128)(2,1)S(1)} %collective-permute-done.2.rest_2_), channel_id=1, source_target_pairs={{0,2},{2,0},{4,6},{6,4},{8,10},{10,8},{12,14},{14,12},{1,3},{3,1},... | collective-permute-start | bytes 393224 | tf_op jit(solution)/shard_map/ppermute | solution.py:58
  31.4 5.9 %collective-permute-start.7 = (bf16[64,1024]{1,0:T(8,128)(2,1)S(1)}, bf16[64,1024]{1,0:T(8,128)(2,1)S(1)}, u32[]{:S(2)}, u32[]{:S(2)}) collective-permute-start(bf16[64,1024]{1,0:T(8,128)(2,1)S(1)} %collective-permute-done.6.rest_6_), channel_id=1, source_target_pairs={{0,2},{2,0},{4,6},{6,4},{8,10},{10,8},{12,14},{14,12},{1,3},{3,1},... | collective-permute-start | bytes 393224 | tf_op jit(solution)/shard_map/ppermute | solution.py:58
  37.3 0.9 %copy-start = (bf16[64,1024]{1,0:T(8,128)(2,1)S(1)}, bf16[64,1024]{1,0:T(8,128)(2,1)}, u32[]{:S(2)}) copy-start(bf16[64,1024]{1,0:T(8,128)(2,1)} %shard_map.57.rest_0_) | copy-start | bytes 393220
  38.2 0.9 %copy-start.1 = (f32[4,64,128]{2,1,0:T(8,128)S(1)}, f32[4,64,128]{2,1,0:T(8,128)}, u32[]{:S(2)}) copy-start(f32[4,64,128]{2,1,0:T(8,128)} %get-tuple-element.10.grads_ref) | copy-start | bytes 393220
  50.8 1.2 %collective-permute-start.8 = (f32[2,256]{1,0:T(2,128)S(1)}, f32[2,256]{1,0:T(2,128)S(1)}, u32[]{:S(2)}, u32[]{:S(2)}) collective-permute-start(f32[2,256]{1,0:T(2,128)S(1)} %get-tuple-element.12), channel_id=1, source_target_pairs={{0,1},{1,0},{2,3},{3,2},{4,5},{5,4},{6,7},{7,6},{8,9},{9,8},{10,11... | collective-permute-start | bytes 6152 | tf_op jit(solution)/shard_map/ppermute | solution.py:289

commit v3 on v2

v3 whole, which is shorter than its diff:
```python
import functools
import math

import jax
import jax.numpy as jnp
from jax import lax
from jax.experimental import pallas as pl
from jax.experimental.pallas import tpu as pltpu
from jax.sharding import PartitionSpec as P

SEQ = 64
RANK = 64
WIDE = 4 * RANK
MIB = 1 << 20
F32 = jnp.float32
BF16 = jnp.bfloat16
HBM = pl.BlockSpec(memory_space=pl.ANY)
VMEM = pl.BlockSpec(memory_space=pltpu.VMEM)


def cost(us):
    return pl.CostEstimate(flops=0, bytes_accessed=int(us * 3.7e6), transcendentals=0)


NT = (((1,), (1,)), ((), ()))


SMALL = pltpu.CompilerParams(vmem_limit_bytes=4 * MIB)


def iota(shape, dim):
    return lax.broadcasted_iota(jnp.int32, shape, dim)


def pieces(x):
    high = x.astype(BF16)
    rest = x - high.astype(F32)
    mid = rest.astype(BF16)
    low = (rest - mid.astype(F32)).astype(BF16)
    return high, mid, low


def dot(a, b):
    return jnp.dot(a, b, preferred_element_type=F32)


def spread_kernel(q_ref, out_ref):
    for k in range(q_ref.shape[0]):
        out_ref[:, k * RANK : (k + 1) * RANK] = q_ref[k]


def spread(queries):
    return pl.pallas_call(
        spread_kernel,
        out_shape=jax.ShapeDtypeStruct((RANK, queries.shape[0] * RANK), BF16),
        cost_estimate=cost(2),
        in_specs=[VMEM],
        out_specs=VMEM,
        compiler_params=SMALL,
    )(queries)


def flips(count):
    return list(range(0, count, 2))


def flipped(x, count, flip):
    return lax.ppermute(x, "dp", [(i, i ^ flip) for i in range(count)])


def from_peers(mine, count):
    known = {0: mine}
    bit = count // 2
    while bit > 1:
        for m in list(known):
            known[m | bit] = flipped(known[m], count, bit)
        bit //= 2
    return [known[m] for m in flips(count)]


def project_kernel(
    cuts, x_ref, g_ref, pin_ref, pout_ref, after_ref, first_ref, second_ref, x, g, pin, pout, sems
):
    copies = []
    for which, start, size in cuts:
        source, factor, held, held_factor = (
            (x_ref, pin_ref, x, pin) if which == 0 else (g_ref, pout_ref, g, pout)
        )
        here = pl.ds(start, size)
        at = 2 * len(copies)
        pair = (
            pltpu.make_async_copy(
                factor.at[:, here], held_factor.at[:, here], sems.at[at]
            ),
            pltpu.make_async_copy(source.at[:, here], held.at[:, here], sems.at[at + 1]),
        )
        for copy in pair:
            copy.start()
        copies.append(pair)
    totals = [None, None]
    for pair, (which, start, size) in zip(copies, cuts):
        for copy in pair:
            copy.wait()
        here = slice(start, start + size)
        source, factor = (x, pin) if which == 0 else (g, pout)
        term = lax.dot_general(
            source[:, here], factor[:, here], NT, preferred_element_type=F32
        )
        totals[which] = term if totals[which] is None else totals[which] + term
    half = totals[0].shape[0] // 2
    for part, out_ref in enumerate((first_ref, second_ref)):
        here = slice(part * half, (part + 1) * half)
        out_ref[:, :RANK] = totals[0][here]
        out_ref[:, RANK:] = totals[1][here]


def project(train_inputs, train_grads, proj_in, proj_out, after):
    half = jax.ShapeDtypeStruct((train_inputs.shape[0] // 2, 2 * RANK), F32)
    cuts = []
    for which, array in ((0, train_inputs), (1, train_grads)):
        size = 1024
        cuts += [(which, at, size) for at in range(0, array.shape[1], size)]
    return pl.pallas_call(
        functools.partial(project_kernel, cuts),
        out_shape=(half, half),
        cost_estimate=cost(8),
        in_specs=[HBM] * 5,
        out_specs=(VMEM, VMEM),
        scratch_shapes=[
            pltpu.VMEM(train_inputs.shape, BF16),
            pltpu.VMEM(train_grads.shape, BF16),
            pltpu.VMEM(proj_in.shape[::-1], BF16),
            pltpu.VMEM(proj_out.shape[::-1], BF16),
            pltpu.SemaphoreType.DMA((2 * len(cuts),)),
        ],
        compiler_params=pltpu.CompilerParams(vmem_limit_bytes=58 * MIB),
    )(train_inputs, train_grads, proj_in.T, proj_out.T, after)


def over_rows(a):
    return lax.dot_general(
        a,
        a,
        (((0,), (0,)), ((), ())),
        precision=lax.Precision.HIGHEST,
        preferred_element_type=F32,
    )


def both_halves(refs):
    a, b, c, d = refs
    return jnp.concatenate([a[...] + c[...], b[...] + d[...]], axis=0)


def covariance_kernel(count, *refs):
    cov_ref = refs[-1]
    gram = over_rows(both_halves(refs[:4]))
    cov_in = gram[:RANK, :RANK]
    cov_out = gram[RANK:, RANK:]
    row, col = iota((RANK, RANK), 0), iota((RANK, RANK), 1)
    packed = jnp.where(row >= col, cov_in, cov_out)
    diagonal = jnp.sum(jnp.where(row == col, cov_out, 0.0), axis=0, keepdims=True)
    half = RANK // 2
    body = jnp.concatenate([packed[:half], packed[half:]], axis=1)
    tail = jnp.concatenate([jnp.broadcast_to(diagonal, (8, RANK))] * 2, axis=1)
    for p in range(count):
        cov_ref[p, :half] = body
        cov_ref[p, half:] = tail


def covariances(mine, other, after, count):
    return pl.pallas_call(
        functools.partial(covariance_kernel, count),
        out_shape=jax.ShapeDtypeStruct((count, RANK // 2 + 8, 2 * RANK), F32),
        cost_estimate=cost(2),
        in_specs=[VMEM] * (4 + len(after)),
        out_specs=VMEM,
        compiler_params=SMALL,
    )(*mine, *other, *after)


def gradient_kernel(*refs):
    grads_ref = refs[-1]
    full = both_halves(refs[:4])
    for e in range(full.shape[0] // SEQ):
        gram = over_rows(full[e * SEQ : (e + 1) * SEQ])
        grads_ref[:, e * RANK : (e + 1) * RANK] = gram[RANK:, :RANK].astype(BF16)


def gradients(mine, other):
    examples = 2 * mine[0].shape[0] // SEQ
    return pl.pallas_call(
        gradient_kernel,
        out_shape=jax.ShapeDtypeStruct((RANK, examples * RANK), BF16),
        cost_estimate=cost(2),
        in_specs=[VMEM] * 4,
        out_specs=VMEM,
        compiler_params=SMALL,
    )(*mine, *other)


def inverse_2(m):
    a, b, c, d = m
    scale = 1.0 / (a * d - b * c)
    return d * scale, -b * scale, -c * scale, a * scale


def times_2(m, n):
    a, b, c, d = m
    e, f, g, h = n
    return a * e + b * g, a * f + b * h, c * e + d * g, c * f + d * h


def minus_2(m, n):
    return tuple(i - j for i, j in zip(m, n))


def inverse_4(entry):
    block = lambda i, j: (
        entry(i, j),
        entry(i, j + 1),
        entry(i + 1, j),
        entry(i + 1, j + 1),
    )
    b, c = block(0, 2), block(2, 0)
    first = inverse_2(block(0, 0))
    first_b, c_first = times_2(first, b), times_2(c, first)
    last = inverse_2(minus_2(block(2, 2), times_2(c, first_b)))
    upper = tuple(-i for i in times_2(first_b, last))
    lower = tuple(-i for i in times_2(last, c_first))
    first = minus_2(first, times_2(upper, c_first))
    return (
        (first[0], first[1], upper[0], upper[1]),
        (first[2], first[3], upper[2], upper[3]),
        (lower[0], lower[1], last[0], last[1]),
        (lower[2], lower[3], last[2], last[3]),
    )


def inverses(m):
    lane = iota((RANK, 2 * RANK), 1)
    sub = iota((RANK, 2 * RANK), 0)
    left = lane < RANK
    place = jnp.where(left, lane, lane - RANK)
    for k in range(0, RANK, 4):
        cols = [
            jnp.where(left, m[:, k + i : k + i + 1], m[:, RANK + k + i : RANK + k + i + 1])
            for i in range(4)
        ]
        pivot = inverse_4(lambda i, j: cols[j][k + i : k + i + 1])
        rows = []
        for i in range(4):
            row = m[k + i : k + i + 1]
            for j in range(4):
                row = jnp.where(place[:1] == k + j, 1.0 if i == j else 0.0, row)
            rows.append(row)
        news = [
            (p[0] * rows[0] + p[1] * rows[1]) + (p[2] * rows[2] + p[3] * rows[3])
            for p in pivot
        ]
        m = jnp.where((place >= k) & (place < k + 4), 0.0, m)
        m = (m - cols[0] * news[0] - cols[1] * news[1]) - (
            cols[2] * news[2] + cols[3] * news[3]
        )
        for i in range(4):
            m = jnp.where(sub == k + i, news[i], m)
    return m


def score_kernel(total, held, count, cov_ref, *rest):
    peers = len(flips(count))
    grads_refs, rest = rest[:2], rest[2:]
    queries_refs, rest = rest[:peers], rest[peers:]
    out_refs, (queries, weights, sums) = rest[:4], rest[4:]
    for p in range(peers):
        queries[p] = queries_refs[p][...]
    examples = 2 * grads_refs[0].shape[1] // RANK
    half = RANK // 2
    core = lax.axis_index("tensor")
    cov = cov_ref[0]
    for p in range(1, count):
        cov = cov + cov_ref[p]
    cov = cov / total
    packed = jnp.concatenate([cov[:half, :RANK], cov[:half, RANK:]], axis=0)
    turned = packed.T
    row, col = iota((RANK, RANK), 0), iota((RANK, RANK), 1)
    cov_in = jnp.where(row >= col, packed, turned)
    cov_out = jnp.where(
        row < col, packed, jnp.where(row == col, cov[half : half + 1, :RANK], turned)
    )

    def damped(c):
        shift = 0.1 * jnp.sum(jnp.where(row == col, c, 0.0)) / RANK + 1e-06
        return jnp.where(row == col, c + shift, c)

    inverse = inverses(jnp.concatenate([damped(cov_in), damped(cov_out)], axis=1))
    inv_in, inv_out = inverse[:, :RANK], inverse[:, RANK:]
    left = jnp.concatenate(pieces(inv_out), axis=0)
    for i, piece in enumerate(pieces(inv_in)):
        weights[i] = jnp.zeros((WIDE, WIDE), BF16)
        for k in range(4):
            here = slice(k * RANK, (k + 1) * RANK)
            weights[i, here, here] = piece
    chunks = held // 4
    grads = []
    for ref in grads_refs:
        both = ref[...].astype(F32)
        for e in range(examples // 2):
            grad = both[:, e * RANK : (e + 1) * RANK]
            grads.append(jnp.concatenate([grad] * 4, axis=1))

    def of_peer(p, carry):
        u = dot(left, queries[p])
        y = u[:RANK] + (u[RANK : 2 * RANK] + u[2 * RANK :])
        high, mid, low = pieces(
            jnp.concatenate([y[:, c * WIDE : (c + 1) * WIDE] for c in range(chunks)], axis=0)
        )
        size = chunks * RANK
        by_high = dot(jnp.concatenate([high, mid, low], axis=0), weights[0])
        by_mid = dot(jnp.concatenate([high, mid], axis=0), weights[1])
        by_low = dot(high, weights[2])
        small = by_low + by_mid[size:] + by_high[2 * size :]
        precond = by_high[:size] + (by_high[size : 2 * size] + by_mid[:size] + small)
        precond = precond.astype(BF16).astype(F32)
        for e in range(examples):
            for c in range(chunks):
                sums[p, e * chunks + c : e * chunks + c + 1] = jnp.sum(
                    precond[c * RANK : (c + 1) * RANK] * grads[e], axis=0, keepdims=True
                )
        return carry

    lax.fori_loop(0, peers, of_peer, 0)
    width = 2 * held * count
    lanes = (WIDE, width)
    pick = jnp.where(iota(lanes, 0) // RANK == iota(lanes, 1) % 4, 1.0, 0.0).astype(BF16)
    flat = sums[...].reshape(peers * examples * chunks, WIDE)
    high, mid, low = pieces(flat)
    found = dot(high, pick) + (dot(mid, pick) + dot(low, pick))
    shape = (peers, examples * chunks, width)
    found = found.reshape(shape)
    lane = iota(shape, 2)
    ours = (
        (lane // (2 * held) == ((2 * iota(shape, 0)) ^ lax.axis_index("dp")))
        & ((lane // held) % 2 == core)
        & ((lane % held) // 4 == iota(shape, 1) % chunks)
    )
    found = jnp.sum(jnp.where(ours, found, 0.0), axis=0)
    scale = 1.0 / (math.sqrt(SEQ) * RANK)
    scores = [
        jnp.sum(found[e * chunks : (e + 1) * chunks], axis=0, keepdims=True) * scale
        for e in range(examples)
    ]
    share = examples // 4
    blocks = [
        jnp.concatenate(scores[i * share : (i + 1) * share], axis=0) for i in range(4)
    ]
    for i in (0, 2):
        out_refs[i][...] = jnp.where(core == 0, blocks[i], blocks[i + 1])
        out_refs[i + 1][...] = jnp.where(core == 0, blocks[i + 1], blocks[i])


def score(cov, grads, queries, total, held):
    count = cov.shape[0]
    peers = len(queries)
    examples = 2 * grads[0].shape[1] // RANK
    shape = jax.ShapeDtypeStruct((examples // 4, 2 * held * count), F32)
    return pl.pallas_call(
        functools.partial(score_kernel, total, held, count),
        out_shape=(shape,) * 4,
        cost_estimate=cost(10),
        in_specs=[VMEM] * (3 + peers),
        out_specs=(VMEM,) * 4,
        scratch_shapes=[
            pltpu.VMEM((peers,) + queries[0].shape, BF16),
            pltpu.VMEM((3, WIDE, WIDE), BF16),
            pltpu.VMEM((peers, examples * (held // 4), WIDE), F32),
        ],
        compiler_params=pltpu.CompilerParams(vmem_limit_bytes=24 * MIB),
    )(cov, *grads, *queries)


def local(train_inputs, train_grads, proj_in, proj_out, queries):
    count = lax.axis_size("dp")
    swap = [(0, 1), (1, 0)]
    held = queries.shape[0]
    spread_queries = spread(queries)
    gathered = from_peers(spread_queries, count)
    mine = project(train_inputs, train_grads, proj_in, proj_out, spread_queries)
    other = [lax.ppermute(part, "tensor", swap) for part in mine]
    cov = covariances(mine, other, [gathered[count // 4]], count)
    cov = lax.all_to_all(cov, "dp", 0, 0, tiled=True)
    grads = gradients(mine, other)
    total = train_inputs.shape[0] * count
    pair = (grads, flipped(grads, count, 1))
    keep, to_core, to_chip, to_far = score(cov, pair, gathered, total, held)
    corner = [(i, i ^ 3) for i in range(2 * count)]
    return (
        (keep + lax.ppermute(to_core, "tensor", swap))
        + (flipped(to_chip, count, 1) + lax.ppermute(to_far, ("dp", "tensor"), corner))
    )


def solution(mesh):
    placed = (
        P(("groups", "dp"), "tensor"),
        P(("groups", "dp"), "tensor"),
        P("tensor", None),
        P("tensor", None),
        P(("groups", "dp", "tensor"), None, None),
    )
    return jax.shard_map(
        local,
        mesh=mesh,
        in_specs=placed,
        out_specs=P(("groups", "dp", "tensor"), None),
        check_vma=False,
    )
```

time: 52.8 us -> 45.6 us (0.86)
  Pallas kernels: 23.5 us -> 16.1 us
  local copies, waits for them, and re-layouts: 2.46 us -> 5.22 us
  waiting for transfers between devices: 11 us -> 8.68 us
    pallas_call x1, Pallas kernels: 11.6 us -> 6.52 us  [score(): pl.pallas_call(functools.partial(score_kernel, total, held, count), out_s...]
    unnamed x6 -> x14, local copies, waits for them, and re-layouts: 2.46 us -> 5.22 us
    ppermute x9, waiting for transfers between devices: 11 us -> 8.68 us  [the longest x5 6.68 us: flipped(): return lax.ppermute(x, 'dp', [(i, i ^ flip) for i in range(count)])]
    pallas_call x1, Pallas kernels: 1.72 us -> 0.12 us  [spread(): pl.pallas_call(spread_kernel, out_shape=jax.ShapeDtypeStruct((RANK, queri...]
    pallas_call x2 -> x3, Pallas kernels: 10.1 us -> 9.49 us  [the longest x1 7.88 us: project(): pl.pallas_call(functools.partial(project_kernel, cuts), out_shape=(half,...]
    ppermute x9, starting transfers between devices: 11.2 us -> 10.7 us  [the longest x5 9.69 us: flipped(): return lax.ppermute(x, 'dp', [(i, i ^ flip) for i in range(count)])]
  transfers between devices with their start and end apart: 10 -> 10, of which waited for: 5 -> 7; matrix products, arithmetic and copies ran while one was open for 0% -> 0% of each run, Pallas kernels for 7% -> 19%
where the time goes in v3:
time: 45.6 us; the launch traced here: 45.2 us
  Pallas kernels  16.1 us (35%)
  starting transfers between devices  14.5 us (32%)
  waiting for transfers between devices  8.68 us (19%)
  local copies, waits for them, and re-layouts  5.22 us (11%)
  other arithmetic  0.58 us (1%)
    ppermute x5, starting transfers between devices, flipped(): return lax.ppermute(x, 'dp', [(i, i ^ flip) for i in range(count)])  9.69 us
    pallas_call x1, Pallas kernels, project(): pl.pallas_call(functools.partial(project_kernel, cuts), out_shape=(half,...  7.88 us
    ppermute x5, waiting for transfers between devices, flipped(): return lax.ppermute(x, 'dp', [(i, i ^ flip) for i in range(count)])  6.68 us
    pallas_call x1, Pallas kernels, score(): pl.pallas_call(functools.partial(score_kernel, total, held, count), out_s...  6.52 us
    unnamed x14, local copies, waits for them, and re-layouts  5.22 us
    all_to_all x1, starting transfers between devices, local(): cov = lax.all_to_all(cov, 'dp', 0, 0, tiled=True)  3.82 us
    pallas_call x1, Pallas kernels, covariances(): pl.pallas_call(functools.partial(covariance_kernel, count), out_shape=jax...  1.12 us
    ppermute x2, waiting for transfers between devices, local(): other = [lax.ppermute(part, 'tensor', swap) for part in mine]  1.11 us
  transfers between devices with their start and end apart: 10, of which 7 were waited for; matrix products, arithmetic and copies ran while one was open for 0% of the time, Pallas kernels for 19%

profile of v3, /device:TPU:0, one launch (start us, length us, event | category | flops | bytes accessed | tf_op | source)
XLA Modules:
  0.0 45.2 jit_solution(12132759036071836890)
XLA Ops:
  0.0 0.0 copy-start.2
  0.0 0.9 %copy-done.2 = bf16[16,64,64]{2,1,0:T(8,128)(2,1)S(1)} copy-done((bf16[16,64,64]{2,1,0:T(8,128)(2,1)S(1)}, bf16[16,64,64]{2,1,0:T(8,128)(2,1)}, u32[]{:S(2)}) %copy-start.2) | copy-done | bytes 131096
  1.0 0.1 shard_map.55.after_ref.rest_2_
  1.1 0.0 copy-start
  1.1 4.1 %collective-permute-start.2 = (bf16[64,1024]{1,0:T(8,128)(2,1)S(1)}, bf16[64,1024]{1,0:T(8,128)(2,1)S(1)}, u32[]{:S(2)}, u32[]{:S(2)}) collective-permute-start(bf16[64,1024]{1,0:T(8,128)(2,1)S(1)} %shard_map.55.after_ref.rest_2_), channel_id=1, source_target_pairs={{0,8},{2,10},{4,12},{6,14},{8,0},{10,2},{12,4},{14,6},{1,9},{3,11}... | collective-permute-start | bytes 393224 | tf_op jit(solution)/shard_map/ppermute | solution.py:68
  5.2 0.0 copy-done
  5.2 7.9 %shard_map.56 = (f32[128,128]{1,0:T(8,128)}, f32[128,128]{1,0:T(8,128)}) custom-call(bf16[256,4096]{1,0:T(8,128)(2,1)} %x_ref.1, bf16[256,14336]{1,0:T(8,128)(2,1)} %g_ref.1, bf16[64,4096]{1,0:T(8,128)(2,1)} %bitcast.3, bf16[64,14336]{1,0:T(8,128)(2,1)} %bitcast.2, bf16[64,1024]{1,0:T(8,128)(2,1)} %copy-done), custom_call_target="tpu_custom_call" | custom-call | bytes 29600000 | tf_op jit(solution)/shard_map/pallas_call | solution.py:123
  13.1 0.1 collective-permute-start
  13.2 0.5 %collective-permute-start.1 = (f32[128,128]{1,0:T(8,128)}, f32[128,128]{1,0:T(8,128)S(1)}, u32[]{:S(2)}, u32[]{:S(2)}) collective-permute-start(f32[128,128]{1,0:T(8,128)} %get-tuple-element.12.refs_1_), channel_id=1, source_target_pairs={{0,1},{1,0},{2,3},{3,2},{4,5},{5,4},{6,7},{7,6},{8,9},{9,8},{10,11... | collective-permute-start | bytes 196616 | tf_op jit(solution)/shard_map/ppermute | solution.py:389
  13.7 1.0 %collective-permute-done.refs_2_ = f32[128,128]{1,0:T(8,128)S(1)} collective-permute-done((f32[128,128]{1,0:T(8,128)}, f32[128,128]{1,0:T(8,128)S(1)}, u32[]{:S(2)}, u32[]{:S(2)}) %collective-permute-start) | collective-permute-done | bytes 65568 | tf_op jit(solution)/shard_map/ppermute | solution.py:389
  14.6 0.2 collective-permute-done.1.refs_3_
  14.8 0.0 collective-permute-done.2.refs_4_.rest_4_
  14.8 0.0 copy-start.3
  14.8 0.8 %copy-done.3 = f32[128,128]{1,0:T(8,128)S(1)} copy-done((f32[128,128]{1,0:T(8,128)S(1)}, f32[128,128]{1,0:T(8,128)}, u32[]{:S(2)}) %copy-start.3) | copy-done | bytes 65560
  15.6 0.0 copy-start.5
  15.6 0.8 %copy-done.5 = f32[128,128]{1,0:T(8,128)S(1)} copy-done((f32[128,128]{1,0:T(8,128)S(1)}, f32[128,128]{1,0:T(8,128)}, u32[]{:S(2)}) %copy-start.5) | copy-done | bytes 65560
  16.5 1.1 %shard_map.57 = f32[8,40,128]{2,1,0:T(8,128)} custom-call(f32[128,128]{1,0:T(8,128)S(1)} %copy-done.3, f32[128,128]{1,0:T(8,128)S(1)} %copy-done.5, f32[128,128]{1,0:T(8,128)S(1)} %collective-permute-done.refs_2_, f32[128,128]{1,0:T(8,128)S(1)} %collective-permute-done.1.refs_3_, bf16[64,1024]{1,0:T(8,128)(2,1)S(1)} %collective-permute-done.2.refs_4_.rest_4_), custom_call_target="tpu_custom_call" | custom-call | bytes 7400000 | tf_op jit(solution)/shard_map/pallas_call | solution.py:172
  17.6 3.8 %all-to-all-start = ((f32[8,40,128]{2,1,0:T(8,128)}), f32[8,40,128]{2,1,0:T(8,128)S(1)}, u32[]{:S(2)}, u32[]{:S(2)}) async-start(f32[8,40,128]{2,1,0:T(8,128)} %shard_map.57), calls=%async_computation | async-start | bytes 327680 | tf_op jit(solution)/shard_map/all_to_all | solution.py:391
  21.4 2.0 %collective-permute-start.4 = (bf16[64,1024]{1,0:T(8,128)(2,1)}, bf16[64,1024]{1,0:T(8,128)(2,1)S(1)}, u32[]{:S(2)}, u32[]{:S(2)}) collective-permute-start(bf16[64,1024]{1,0:T(8,128)(2,1)} %copy-done), channel_id=1, source_target_pairs={{0,4},{2,6},{4,0},{6,2},{8,12},{10,14},{12,8},{14,10},{1,5},{3,7},... | collective-permute-start | bytes 393224 | tf_op jit(solution)/shard_map/ppermute | solution.py:68
  23.4 0.0 collective-permute-start.5
  23.5 0.0 copy-start.4
  23.5 0.8 %copy-done.4 = f32[128,128]{1,0:T(8,128)S(1)} copy-done((f32[128,128]{1,0:T(8,128)S(1)}, f32[128,128]{1,0:T(8,128)}, u32[]{:S(2)}) %copy-start.4) | copy-done | bytes 65560
  24.3 0.0 copy-start.6
  24.3 0.8 %copy-done.6 = f32[128,128]{1,0:T(8,128)S(1)} copy-done((f32[128,128]{1,0:T(8,128)S(1)}, f32[128,128]{1,0:T(8,128)}, u32[]{:S(2)}) %copy-start.6) | copy-done | bytes 65560
  25.2 0.5 %shard_map.58.rest_0_ = bf16[64,256]{1,0:T(8,128)(2,1)S(1)} custom-call(f32[128,128]{1,0:T(8,128)S(1)} %copy-done.4, f32[128,128]{1,0:T(8,128)S(1)} %copy-done.6, f32[128,128]{1,0:T(8,128)S(1)} %collective-permute-done.refs_2_, f32[128,128]{1,0:T(8,128)S(1)} %collective-permute-done.1.refs_3_), custom_call_target="tpu_custom_call" | custom-call | bytes 7400000 | tf_op jit(solution)/shard_map/pallas_call | solution.py:192
  25.6 2.0 %collective-permute-start.3 = (bf16[64,256]{1,0:T(8,128)(2,1)S(1)}, bf16[64,256]{1,0:T(8,128)(2,1)S(1)}, u32[]{:S(2)}, u32[]{:S(2)}) collective-permute-start(bf16[64,256]{1,0:T(8,128)(2,1)S(1)} %shard_map.58.rest_0_), channel_id=1, source_target_pairs={{0,2},{2,0},{4,6},{6,4},{8,10},{10,8},{12,14},{14,12},{1,3},{3,1},... | collective-permute-start | bytes 98312 | tf_op jit(solution)/shard_map/ppermute | solution.py:68
  27.6 1.9 %collective-permute-done.3.rest_1_ = bf16[64,256]{1,0:T(8,128)(2,1)S(1)} collective-permute-done((bf16[64,256]{1,0:T(8,128)(2,1)S(1)}, bf16[64,256]{1,0:T(8,128)(2,1)S(1)}, u32[]{:S(2)}, u32[]{:S(2)}) %collective-permute-start.3) | collective-permute-done | bytes 32800 | tf_op jit(solution)/shard_map/ppermute | solution.py:68
  29.6 1.0 %collective-permute-done.4.rest_3_ = bf16[64,1024]{1,0:T(8,128)(2,1)S(1)} collective-permute-done((bf16[64,1024]{1,0:T(8,128)(2,1)}, bf16[64,1024]{1,0:T(8,128)(2,1)S(1)}, u32[]{:S(2)}, u32[]{:S(2)}) %collective-permute-start.4) | collective-permute-done | bytes 131104 | tf_op jit(solution)/shard_map/ppermute | solution.py:68
  30.6 1.9 %collective-permute-done.5.rest_5_ = bf16[64,1024]{1,0:T(8,128)(2,1)S(1)} collective-permute-done((bf16[64,1024]{1,0:T(8,128)(2,1)S(1)}, bf16[64,1024]{1,0:T(8,128)(2,1)S(1)}, u32[]{:S(2)}, u32[]{:S(2)}) %collective-permute-start.5) | collective-permute-done | bytes 131104 | tf_op jit(solution)/shard_map/ppermute | solution.py:68
  32.5 0.0 all-to-all-done.cov_ref
  32.5 0.0 copy-start.1
  32.5 0.9 %copy-done.1 = bf16[64,1024]{1,0:T(8,128)(2,1)S(1)} copy-done((bf16[64,1024]{1,0:T(8,128)(2,1)S(1)}, bf16[64,1024]{1,0:T(8,128)(2,1)}, u32[]{:S(2)}) %copy-start.1) | copy-done | bytes 131096
  33.4 6.5 %shard_map.59 = (f32[2,256]{1,0:T(2,128)S(1)}, f32[2,256]{1,0:T(2,128)S(1)}, f32[2,256]{1,0:T(2,128)S(1)}, f32[2,256]{1,0:T(2,128)S(1)}) custom-call(f32[8,40,128]{2,1,0:T(8,128)S(1)} %all-to-all-done.cov_ref, bf16[64,256]{1,0:T(8,128)(2,1)S(1)} %shard_map.58.rest_0_, bf16[64,256]{1,0:T(8,128)(2,1)S(1)} %collective-permute-done.3.rest_1_, ...), custom_call_target="tpu_custom_call" | custom-call | bytes 37000000 | tf_op jit(solution)/shard_map/pallas_call | solution.py:367
  40.0 0.1 collective-permute-start.6
  40.0 1.5 %collective-permute-start.7 = (f32[2,256]{1,0:T(2,128)S(1)}, f32[2,256]{1,0:T(2,128)S(1)}, u32[]{:S(2)}, u32[]{:S(2)}) collective-permute-start(f32[2,256]{1,0:T(2,128)S(1)} %get-tuple-element.15), channel_id=1, source_target_pairs={{0,2},{2,0},{4,6},{6,4},{8,10},{10,8},{12,14},{14,12},{1,3},{3,1},... | collective-permute-start | bytes 6152 | tf_op jit(solution)/shard_map/ppermute | solution.py:68
  41.6 0.3 collective-permute-start.8
  41.9 0.0 collective-permute-done.6
  41.9 1.8 %collective-permute-done.7 = f32[2,256]{1,0:T(2,128)S(1)} collective-permute-done((f32[2,256]{1,0:T(2,128)S(1)}, f32[2,256]{1,0:T(2,128)S(1)}, u32[]{:S(2)}, u32[]{:S(2)}) %collective-permute-start.7) | collective-permute-done | bytes 2080 | tf_op jit(solution)/shard_map/ppermute | solution.py:68
  43.7 0.9 %collective-permute-done.8 = f32[2,256]{1,0:T(2,128)S(1)} collective-permute-done((f32[2,256]{1,0:T(2,128)S(1)}, f32[2,256]{1,0:T(2,128)S(1)}, u32[]{:S(2)}, u32[]{:S(2)}) %collective-permute-start.8) | collective-permute-done | bytes 2080 | tf_op jit(solution)/shard_map/ppermute | solution.py:399
  44.6 0.6 %add_add_fusion = f32[2,256]{1,0:T(2,128)} fusion(f32[2,256]{1,0:T(2,128)S(1)} %collective-permute-done.7, f32[2,256]{1,0:T(2,128)S(1)} %collective-permute-done.8, f32[2,256]{1,0:T(2,128)S(1)} %get-tuple-element.13, f32[2,256]{1,0:T(2,128)S(1)} %collective-permute-done.6), kind=kLoop, calls=%fused_computation | loop fusion | flops 1536 | bytes 10240 | tf_op jit(solution)/shard_map/add | solution.py:398
Async XLA Ops:
  0.0 0.9 %copy-start.2 = (bf16[16,64,64]{2,1,0:T(8,128)(2,1)S(1)}, bf16[16,64,64]{2,1,0:T(8,128)(2,1)}, u32[]{:S(2)}) copy-start(bf16[16,64,64]{2,1,0:T(8,128)(2,1)} %q_ref.1) | copy-start | bytes 393220
  1.1 4.1 %copy-start = (bf16[64,1024]{1,0:T(8,128)(2,1)}, bf16[64,1024]{1,0:T(8,128)(2,1)S(1)}, u32[]{:S(2)}) copy-start(bf16[64,1024]{1,0:T(8,128)(2,1)S(1)} %shard_map.55.after_ref.rest_2_) | copy-start | bytes 393220
  1.1 13.7 %collective-permute-start.2 = (bf16[64,1024]{1,0:T(8,128)(2,1)S(1)}, bf16[64,1024]{1,0:T(8,128)(2,1)S(1)}, u32[]{:S(2)}, u32[]{:S(2)}) collective-permute-start(bf16[64,1024]{1,0:T(8,128)(2,1)S(1)} %shard_map.55.after_ref.rest_2_), channel_id=1, source_target_pairs={{0,8},{2,10},{4,12},{6,14},{8,0},{10,2},{12,4},{14,6},{1,9},{3,11}... | collective-permute-start | bytes 393224 | tf_op jit(solution)/shard_map/ppermute | solution.py:68
  13.1 1.5 %collective-permute-start = (f32[128,128]{1,0:T(8,128)}, f32[128,128]{1,0:T(8,128)S(1)}, u32[]{:S(2)}, u32[]{:S(2)}) collective-permute-start(f32[128,128]{1,0:T(8,128)} %get-tuple-element.11.refs_0_), channel_id=1, source_target_pairs={{0,1},{1,0},{2,3},{3,2},{4,5},{5,4},{6,7},{7,6},{8,9},{9,8},{10,11... | collective-permute-start | bytes 196616 | tf_op jit(solution)/shard_map/ppermute | solution.py:389
  13.2 1.6 %collective-permute-start.1 = (f32[128,128]{1,0:T(8,128)}, f32[128,128]{1,0:T(8,128)S(1)}, u32[]{:S(2)}, u32[]{:S(2)}) collective-permute-start(f32[128,128]{1,0:T(8,128)} %get-tuple-element.12.refs_1_), channel_id=1, source_target_pairs={{0,1},{1,0},{2,3},{3,2},{4,5},{5,4},{6,7},{7,6},{8,9},{9,8},{10,11... | collective-permute-start | bytes 196616 | tf_op jit(solution)/shard_map/ppermute | solution.py:389
  14.8 0.8 %copy-start.3 = (f32[128,128]{1,0:T(8,128)S(1)}, f32[128,128]{1,0:T(8,128)}, u32[]{:S(2)}) copy-start(f32[128,128]{1,0:T(8,128)} %get-tuple-element.11.refs_0_) | copy-start | bytes 196612
  15.6 0.8 %copy-start.5 = (f32[128,128]{1,0:T(8,128)S(1)}, f32[128,128]{1,0:T(8,128)}, u32[]{:S(2)}) copy-start(f32[128,128]{1,0:T(8,128)} %get-tuple-element.12.refs_1_) | copy-start | bytes 196612
  17.6 14.9 %all-to-all-start = ((f32[8,40,128]{2,1,0:T(8,128)}), f32[8,40,128]{2,1,0:T(8,128)S(1)}, u32[]{:S(2)}, u32[]{:S(2)}) async-start(f32[8,40,128]{2,1,0:T(8,128)} %shard_map.57), calls=%async_computation | async-start | bytes 327680 | tf_op jit(solution)/shard_map/all_to_all | solution.py:391
  21.4 9.2 %collective-permute-start.4 = (bf16[64,1024]{1,0:T(8,128)(2,1)}, bf16[64,1024]{1,0:T(8,128)(2,1)S(1)}, u32[]{:S(2)}, u32[]{:S(2)}) collective-permute-start(bf16[64,1024]{1,0:T(8,128)(2,1)} %copy-done), channel_id=1, source_target_pairs={{0,4},{2,6},{4,0},{6,2},{8,12},{10,14},{12,8},{14,10},{1,5},{3,7},... | collective-permute-start | bytes 393224 | tf_op jit(solution)/shard_map/ppermute | solution.py:68
  23.4 9.1 %collective-permute-start.5 = (bf16[64,1024]{1,0:T(8,128)(2,1)S(1)}, bf16[64,1024]{1,0:T(8,128)(2,1)S(1)}, u32[]{:S(2)}, u32[]{:S(2)}) collective-permute-start(bf16[64,1024]{1,0:T(8,128)(2,1)S(1)} %collective-permute-done.2.refs_4_.rest_4_), channel_id=1, source_target_pairs={{0,4},{2,6},{4,0},{6,2},{8,12},{10,14},{12,8},{14,10},{1,5},{3,7},... | collective-permute-start | bytes 393224 | tf_op jit(solution)/shard_map/ppermute | solution.py:68
  23.5 0.8 %copy-start.4 = (f32[128,128]{1,0:T(8,128)S(1)}, f32[128,128]{1,0:T(8,128)}, u32[]{:S(2)}) copy-start(f32[128,128]{1,0:T(8,128)} %get-tuple-element.11.refs_0_) | copy-start | bytes 196612
  24.3 0.8 %copy-start.6 = (f32[128,128]{1,0:T(8,128)S(1)}, f32[128,128]{1,0:T(8,128)}, u32[]{:S(2)}) copy-start(f32[128,128]{1,0:T(8,128)} %get-tuple-element.12.refs_1_) | copy-start | bytes 196612
  25.6 3.9 %collective-permute-start.3 = (bf16[64,256]{1,0:T(8,128)(2,1)S(1)}, bf16[64,256]{1,0:T(8,128)(2,1)S(1)}, u32[]{:S(2)}, u32[]{:S(2)}) collective-permute-start(bf16[64,256]{1,0:T(8,128)(2,1)S(1)} %shard_map.58.rest_0_), channel_id=1, source_target_pairs={{0,2},{2,0},{4,6},{6,4},{8,10},{10,8},{12,14},{14,12},{1,3},{3,1},... | collective-permute-start | bytes 98312 | tf_op jit(solution)/shard_map/ppermute | solution.py:68
  32.5 0.9 %copy-start.1 = (bf16[64,1024]{1,0:T(8,128)(2,1)S(1)}, bf16[64,1024]{1,0:T(8,128)(2,1)}, u32[]{:S(2)}) copy-start(bf16[64,1024]{1,0:T(8,128)(2,1)} %copy-done) | copy-start | bytes 393220
  40.0 1.9 %collective-permute-start.6 = (f32[2,256]{1,0:T(2,128)S(1)}, f32[2,256]{1,0:T(2,128)S(1)}, u32[]{:S(2)}, u32[]{:S(2)}) collective-permute-start(f32[2,256]{1,0:T(2,128)S(1)} %get-tuple-element.14), channel_id=1, source_target_pairs={{0,1},{1,0},{2,3},{3,2},{4,5},{5,4},{6,7},{7,6},{8,9},{9,8},{10,11... | collective-permute-start | bytes 6152 | tf_op jit(solution)/shard_map/ppermute | solution.py:398
  40.0 3.7 %collective-permute-start.7 = (f32[2,256]{1,0:T(2,128)S(1)}, f32[2,256]{1,0:T(2,128)S(1)}, u32[]{:S(2)}, u32[]{:S(2)}) collective-permute-start(f32[2,256]{1,0:T(2,128)S(1)} %get-tuple-element.15), channel_id=1, source_target_pairs={{0,2},{2,0},{4,6},{6,4},{8,10},{10,8},{12,14},{14,12},{1,3},{3,1},... | collective-permute-start | bytes 6152 | tf_op jit(solution)/shard_map/ppermute | solution.py:68
  41.6 3.0 %collective-permute-start.8 = (f32[2,256]{1,0:T(2,128)S(1)}, f32[2,256]{1,0:T(2,128)S(1)}, u32[]{:S(2)}, u32[]{:S(2)}) collective-permute-start(f32[2,256]{1,0:T(2,128)S(1)} %get-tuple-element.16), channel_id=1, source_target_pairs={{0,3},{1,2},{2,1},{3,0},{4,7},{5,6},{6,5},{7,4},{8,11},{9,10},{10,... | collective-permute-start | bytes 6152 | tf_op jit(solution)/shard_map/ppermute | solution.py:399

commit v4 on v3

--- a/solution.py
+++ b/solution.py
@@ -70,11 +70,15 @@
 
 def from_peers(mine, count):
     known = {0: mine}
-    bit = count // 2
-    while bit > 1:
-        for m in list(known):
-            known[m | bit] = flipped(known[m], count, bit)
-        bit //= 2
+    bits = []
+    while 2 << len(bits) < count:
+        bits.append(2 << len(bits))
+    for bit in reversed(bits[-2:]):
+        known[bit] = flipped(mine, count, bit)
+    for i, bit in enumerate(reversed(bits)):
+        for m in sorted(known):
+            if m & bit == 0 and m | bit not in known and m % (2 * bit) == 0:
+                known[m | bit] = flipped(known[m], count, bit)
     return [known[m] for m in flips(count)]
 
 
@@ -133,7 +137,7 @@
             pltpu.VMEM(proj_out.shape[::-1], BF16),
             pltpu.SemaphoreType.DMA((2 * len(cuts),)),
         ],
-        compiler_params=pltpu.CompilerParams(vmem_limit_bytes=58 * MIB),
+        compiler_params=pltpu.CompilerParams(vmem_limit_bytes=107 * MIB // 2),
     )(train_inputs, train_grads, proj_in.T, proj_out.T, after)
 
 
@@ -387,7 +391,7 @@
     gathered = from_peers(spread_queries, count)
     mine = project(train_inputs, train_grads, proj_in, proj_out, spread_queries)
     other = [lax.ppermute(part, "tensor", swap) for part in mine]
-    cov = covariances(mine, other, [gathered[count // 4]], count)
+    cov = covariances(mine, other, [gathered[count // 4], gathered[count // 8]], count)
     cov = lax.all_to_all(cov, "dp", 0, 0, tiled=True)
     grads = gradients(mine, other)
     total = train_inputs.shape[0] * count

time: 45.6 us -> 40.5 us (0.89)
  local copies, waits for them, and re-layouts: 5.22 us -> 0.95 us
  Pallas kernels: 16.1 us -> 15.5 us
  starting transfers between devices: 14.5 us -> 15 us
  waiting for transfers between devices: 8.68 us -> 8.2 us
    unnamed x14 -> x2, local copies, waits for them, and re-layouts: 5.22 us -> 0.95 us
    ppermute x5, starting transfers between devices: 9.69 us -> 10.6 us  [flipped(): return lax.ppermute(x, 'dp', [(i, i ^ flip) for i in range(count)])]
    pallas_call x1, Pallas kernels: 7.88 us -> 7.25 us  [project(): pl.pallas_call(functools.partial(project_kernel, cuts), out_shape=(half,...]
  transfers between devices with their start and end apart: 10 -> 10, of which waited for: 7 -> 6; matrix products, arithmetic and copies ran while one was open for 0% -> 0% of each run, Pallas kernels for 19% -> 19%
where the time goes in v4:
time: 40.5 us; the launch traced here: 40.3 us
  Pallas kernels  15.5 us (38%)
  starting transfers between devices  15 us (37%)
  waiting for transfers between devices  8.2 us (20%)
  local copies, waits for them, and re-layouts  0.95 us (2%)
  other arithmetic  0.58 us (1%)
    ppermute x5, starting transfers between devices, flipped(): return lax.ppermute(x, 'dp', [(i, i ^ flip) for i in range(count)])  10.6 us
    pallas_call x1, Pallas kernels, project(): pl.pallas_call(functools.partial(project_kernel, cuts), out_shape=(half,...  7.25 us
    pallas_call x1, Pallas kernels, score(): pl.pallas_call(functools.partial(score_kernel, total, held, count), out_s...  6.52 us
    ppermute x5, waiting for transfers between devices, flipped(): return lax.ppermute(x, 'dp', [(i, i ^ flip) for i in range(count)])  6.4 us
    all_to_all x1, starting transfers between devices, local(): cov = lax.all_to_all(cov, 'dp', 0, 0, tiled=True)  3.38 us
    pallas_call x1, Pallas kernels, covariances(): pl.pallas_call(functools.partial(covariance_kernel, count), out_shape=jax...  1.13 us
    unnamed x2, local copies, waits for them, and re-layouts  0.95 us
    ppermute x2, waiting for transfers between devices, local(): other = [lax.ppermute(part, 'tensor', swap) for part in mine]  0.9 us
  transfers between devices with their start and end apart: 10, of which 6 were waited for; matrix products, arithmetic and copies ran while one was open for 0% of the time, Pallas kernels for 19%

profile of v4, /device:TPU:0, one launch (start us, length us, event | category | flops | bytes accessed | tf_op | source)
XLA Modules:
  0.0 40.3 jit_solution(5914609039554795201)
XLA Ops:
  0.0 0.0 copy-start
  0.0 0.9 %copy-done = bf16[16,64,64]{2,1,0:T(8,128)(2,1)S(1)} copy-done((bf16[16,64,64]{2,1,0:T(8,128)(2,1)S(1)}, bf16[16,64,64]{2,1,0:T(8,128)(2,1)}, u32[]{:S(2)}) %copy-start) | copy-done | bytes 131096
  1.0 0.1 shard_map.55.after_ref.rest_2_
  1.1 3.1 %collective-permute-start.3 = (bf16[64,1024]{1,0:T(8,128)(2,1)S(1)}, bf16[64,1024]{1,0:T(8,128)(2,1)S(1)}, u32[]{:S(2)}, u32[]{:S(2)}) collective-permute-start(bf16[64,1024]{1,0:T(8,128)(2,1)S(1)} %shard_map.55.after_ref.rest_2_), channel_id=1, source_target_pairs={{0,4},{2,6},{4,0},{6,2},{8,12},{10,14},{12,8},{14,10},{1,5},{3,7},... | collective-permute-start | bytes 393224 | tf_op jit(solution)/shard_map/ppermute | solution.py:68
  4.2 2.6 %collective-permute-start.2 = (bf16[64,1024]{1,0:T(8,128)(2,1)S(1)}, bf16[64,1024]{1,0:T(8,128)(2,1)S(1)}, u32[]{:S(2)}, u32[]{:S(2)}) collective-permute-start(bf16[64,1024]{1,0:T(8,128)(2,1)S(1)} %shard_map.55.after_ref.rest_2_), channel_id=1, source_target_pairs={{0,8},{2,10},{4,12},{6,14},{8,0},{10,2},{12,4},{14,6},{1,9},{3,11}... | collective-permute-start | bytes 393224 | tf_op jit(solution)/shard_map/ppermute | solution.py:68
  6.8 7.3 %shard_map.56 = (f32[128,128]{1,0:T(8,128)S(1)}, f32[128,128]{1,0:T(8,128)S(1)}) custom-call(bf16[256,4096]{1,0:T(8,128)(2,1)} %x_ref.1, bf16[256,14336]{1,0:T(8,128)(2,1)} %g_ref.1, bf16[64,4096]{1,0:T(8,128)(2,1)} %bitcast.3, bf16[64,14336]{1,0:T(8,128)(2,1)} %bitcast.2, bf16[64,1024]{1,0:T(8,128)(2,1)S(1)} %shard_map.55.after_ref.rest_2_), custom_call_target="tpu_custom_call" | custom-call | bytes 29600000 | tf_op jit(solution)/shard_map/pallas_call | solution.py:127
  14.0 0.1 collective-permute-start
  14.1 0.5 %collective-permute-start.1 = (f32[128,128]{1,0:T(8,128)S(1)}, f32[128,128]{1,0:T(8,128)S(1)}, u32[]{:S(2)}, u32[]{:S(2)}) collective-permute-start(f32[128,128]{1,0:T(8,128)S(1)} %get-tuple-element.12.refs_1_), channel_id=1, source_target_pairs={{0,1},{1,0},{2,3},{3,2},{4,5},{5,4},{6,7},{7,6},{8,9},{9,8},{10,11... | collective-permute-start | bytes 196616 | tf_op jit(solution)/shard_map/ppermute | solution.py:393
  14.6 0.7 %collective-permute-done.refs_2_ = f32[128,128]{1,0:T(8,128)S(1)} collective-permute-done((f32[128,128]{1,0:T(8,128)S(1)}, f32[128,128]{1,0:T(8,128)S(1)}, u32[]{:S(2)}, u32[]{:S(2)}) %collective-permute-start) | collective-permute-done | bytes 65568 | tf_op jit(solution)/shard_map/ppermute | solution.py:393
  15.3 0.2 collective-permute-done.1.refs_3_
  15.5 0.0 collective-permute-done.3.refs_5_.rest_3_
  15.5 0.0 collective-permute-done.2.refs_4_.rest_4_
  15.5 1.1 %shard_map.57 = f32[8,40,128]{2,1,0:T(8,128)} custom-call(f32[128,128]{1,0:T(8,128)S(1)} %get-tuple-element.11.refs_0_, f32[128,128]{1,0:T(8,128)S(1)} %get-tuple-element.12.refs_1_, f32[128,128]{1,0:T(8,128)S(1)} %collective-permute-done.refs_2_, f32[128,128]{1,0:T(8,128)S(1)} %collective-permute-done.1.refs_3_, ...), custom_call_target="tpu_custom_call" | custom-call | bytes 7400000 | tf_op jit(solution)/shard_map/pallas_call | solution.py:176
  16.6 3.4 %all-to-all-start = ((f32[8,40,128]{2,1,0:T(8,128)}), f32[8,40,128]{2,1,0:T(8,128)S(1)}, u32[]{:S(2)}, u32[]{:S(2)}) async-start(f32[8,40,128]{2,1,0:T(8,128)} %shard_map.57), calls=%async_computation | async-start | bytes 327680 | tf_op jit(solution)/shard_map/all_to_all | solution.py:395
  20.0 1.9 %collective-permute-start.5 = (bf16[64,1024]{1,0:T(8,128)(2,1)S(1)}, bf16[64,1024]{1,0:T(8,128)(2,1)S(1)}, u32[]{:S(2)}, u32[]{:S(2)}) collective-permute-start(bf16[64,1024]{1,0:T(8,128)(2,1)S(1)} %collective-permute-done.2.refs_4_.rest_4_), channel_id=1, source_target_pairs={{0,4},{2,6},{4,0},{6,2},{8,12},{10,14},{12,8},{14,10},{1,5},{3,7},... | collective-permute-start | bytes 393224 | tf_op jit(solution)/shard_map/ppermute | solution.py:68
  22.0 0.5 %shard_map.58.rest_0_ = bf16[64,256]{1,0:T(8,128)(2,1)S(1)} custom-call(f32[128,128]{1,0:T(8,128)S(1)} %get-tuple-element.11.refs_0_, f32[128,128]{1,0:T(8,128)S(1)} %get-tuple-element.12.refs_1_, f32[128,128]{1,0:T(8,128)S(1)} %collective-permute-done.refs_2_, f32[128,128]{1,0:T(8,128)S(1)} %collective-permute-done.1.refs_3_), custom_call_target="tpu_custom_call" | custom-call | bytes 7400000 | tf_op jit(solution)/shard_map/pallas_call | solution.py:196
  22.4 1.5 %collective-permute-start.4 = (bf16[64,256]{1,0:T(8,128)(2,1)S(1)}, bf16[64,256]{1,0:T(8,128)(2,1)S(1)}, u32[]{:S(2)}, u32[]{:S(2)}) collective-permute-start(bf16[64,256]{1,0:T(8,128)(2,1)S(1)} %shard_map.58.rest_0_), channel_id=1, source_target_pairs={{0,2},{2,0},{4,6},{6,4},{8,10},{10,8},{12,14},{14,12},{1,3},{3,1},... | collective-permute-start | bytes 98312 | tf_op jit(solution)/shard_map/ppermute | solution.py:68
  23.9 2.4 %collective-permute-done.4.rest_1_ = bf16[64,256]{1,0:T(8,128)(2,1)S(1)} collective-permute-done((bf16[64,256]{1,0:T(8,128)(2,1)S(1)}, bf16[64,256]{1,0:T(8,128)(2,1)S(1)}, u32[]{:S(2)}, u32[]{:S(2)}) %collective-permute-start.4) | collective-permute-done | bytes 32800 | tf_op jit(solution)/shard_map/ppermute | solution.py:68
  26.4 2.2 %collective-permute-done.5.rest_5_ = bf16[64,1024]{1,0:T(8,128)(2,1)S(1)} collective-permute-done((bf16[64,1024]{1,0:T(8,128)(2,1)S(1)}, bf16[64,1024]{1,0:T(8,128)(2,1)S(1)}, u32[]{:S(2)}, u32[]{:S(2)}) %collective-permute-start.5) | collective-permute-done | bytes 131104 | tf_op jit(solution)/shard_map/ppermute | solution.py:68
  28.5 0.0 all-to-all-done.cov_ref
  28.6 6.5 %shard_map.59 = (f32[2,256]{1,0:T(2,128)S(1)}, f32[2,256]{1,0:T(2,128)S(1)}, f32[2,256]{1,0:T(2,128)S(1)}, f32[2,256]{1,0:T(2,128)S(1)}) custom-call(f32[8,40,128]{2,1,0:T(8,128)S(1)} %all-to-all-done.cov_ref, bf16[64,256]{1,0:T(8,128)(2,1)S(1)} %shard_map.58.rest_0_, bf16[64,256]{1,0:T(8,128)(2,1)S(1)} %collective-permute-done.4.rest_1_, ...), custom_call_target="tpu_custom_call" | custom-call | bytes 37000000 | tf_op jit(solution)/shard_map/pallas_call | solution.py:371
  35.1 0.1 collective-permute-start.6
  35.2 1.5 %collective-permute-start.7 = (f32[2,256]{1,0:T(2,128)S(1)}, f32[2,256]{1,0:T(2,128)S(1)}, u32[]{:S(2)}, u32[]{:S(2)}) collective-permute-start(f32[2,256]{1,0:T(2,128)S(1)} %get-tuple-element.15), channel_id=1, source_target_pairs={{0,2},{2,0},{4,6},{6,4},{8,10},{10,8},{12,14},{14,12},{1,3},{3,1},... | collective-permute-start | bytes 6152 | tf_op jit(solution)/shard_map/ppermute | solution.py:68
  36.7 0.4 collective-permute-start.8
  37.0 0.0 collective-permute-done.6
  37.0 1.8 %collective-permute-done.7 = f32[2,256]{1,0:T(2,128)S(1)} collective-permute-done((f32[2,256]{1,0:T(2,128)S(1)}, f32[2,256]{1,0:T(2,128)S(1)}, u32[]{:S(2)}, u32[]{:S(2)}) %collective-permute-start.7) | collective-permute-done | bytes 2080 | tf_op jit(solution)/shard_map/ppermute | solution.py:68
  38.8 0.9 %collective-permute-done.8 = f32[2,256]{1,0:T(2,128)S(1)} collective-permute-done((f32[2,256]{1,0:T(2,128)S(1)}, f32[2,256]{1,0:T(2,128)S(1)}, u32[]{:S(2)}, u32[]{:S(2)}) %collective-permute-start.8) | collective-permute-done | bytes 2080 | tf_op jit(solution)/shard_map/ppermute | solution.py:403
  39.7 0.6 %add_add_fusion = f32[2,256]{1,0:T(2,128)} fusion(f32[2,256]{1,0:T(2,128)S(1)} %collective-permute-done.7, f32[2,256]{1,0:T(2,128)S(1)} %collective-permute-done.8, f32[2,256]{1,0:T(2,128)S(1)} %get-tuple-element.13, f32[2,256]{1,0:T(2,128)S(1)} %collective-permute-done.6), kind=kLoop, calls=%fused_computation | loop fusion | flops 1536 | bytes 10240 | tf_op jit(solution)/shard_map/add | solution.py:402
Async XLA Ops:
  0.0 0.9 %copy-start = (bf16[16,64,64]{2,1,0:T(8,128)(2,1)S(1)}, bf16[16,64,64]{2,1,0:T(8,128)(2,1)}, u32[]{:S(2)}) copy-start(bf16[16,64,64]{2,1,0:T(8,128)(2,1)} %q_ref.1) | copy-start | bytes 393220
  1.1 14.4 %collective-permute-start.3 = (bf16[64,1024]{1,0:T(8,128)(2,1)S(1)}, bf16[64,1024]{1,0:T(8,128)(2,1)S(1)}, u32[]{:S(2)}, u32[]{:S(2)}) collective-permute-start(bf16[64,1024]{1,0:T(8,128)(2,1)S(1)} %shard_map.55.after_ref.rest_2_), channel_id=1, source_target_pairs={{0,4},{2,6},{4,0},{6,2},{8,12},{10,14},{12,8},{14,10},{1,5},{3,7},... | collective-permute-start | bytes 393224 | tf_op jit(solution)/shard_map/ppermute | solution.py:68
  4.2 11.3 %collective-permute-start.2 = (bf16[64,1024]{1,0:T(8,128)(2,1)S(1)}, bf16[64,1024]{1,0:T(8,128)(2,1)S(1)}, u32[]{:S(2)}, u32[]{:S(2)}) collective-permute-start(bf16[64,1024]{1,0:T(8,128)(2,1)S(1)} %shard_map.55.after_ref.rest_2_), channel_id=1, source_target_pairs={{0,8},{2,10},{4,12},{6,14},{8,0},{10,2},{12,4},{14,6},{1,9},{3,11}... | collective-permute-start | bytes 393224 | tf_op jit(solution)/shard_map/ppermute | solution.py:68
  14.0 1.3 %collective-permute-start = (f32[128,128]{1,0:T(8,128)S(1)}, f32[128,128]{1,0:T(8,128)S(1)}, u32[]{:S(2)}, u32[]{:S(2)}) collective-permute-start(f32[128,128]{1,0:T(8,128)S(1)} %get-tuple-element.11.refs_0_), channel_id=1, source_target_pairs={{0,1},{1,0},{2,3},{3,2},{4,5},{5,4},{6,7},{7,6},{8,9},{9,8},{10,11... | collective-permute-start | bytes 196616 | tf_op jit(solution)/shard_map/ppermute | solution.py:393
  14.1 1.4 %collective-permute-start.1 = (f32[128,128]{1,0:T(8,128)S(1)}, f32[128,128]{1,0:T(8,128)S(1)}, u32[]{:S(2)}, u32[]{:S(2)}) collective-permute-start(f32[128,128]{1,0:T(8,128)S(1)} %get-tuple-element.12.refs_1_), channel_id=1, source_target_pairs={{0,1},{1,0},{2,3},{3,2},{4,5},{5,4},{6,7},{7,6},{8,9},{9,8},{10,11... | collective-permute-start | bytes 196616 | tf_op jit(solution)/shard_map/ppermute | solution.py:393
  16.6 11.9 %all-to-all-start = ((f32[8,40,128]{2,1,0:T(8,128)}), f32[8,40,128]{2,1,0:T(8,128)S(1)}, u32[]{:S(2)}, u32[]{:S(2)}) async-start(f32[8,40,128]{2,1,0:T(8,128)} %shard_map.57), calls=%async_computation | async-start | bytes 327680 | tf_op jit(solution)/shard_map/all_to_all | solution.py:395
  20.0 8.5 %collective-permute-start.5 = (bf16[64,1024]{1,0:T(8,128)(2,1)S(1)}, bf16[64,1024]{1,0:T(8,128)(2,1)S(1)}, u32[]{:S(2)}, u32[]{:S(2)}) collective-permute-start(bf16[64,1024]{1,0:T(8,128)(2,1)S(1)} %collective-permute-done.2.refs_4_.rest_4_), channel_id=1, source_target_pairs={{0,4},{2,6},{4,0},{6,2},{8,12},{10,14},{12,8},{14,10},{1,5},{3,7},... | collective-permute-start | bytes 393224 | tf_op jit(solution)/shard_map/ppermute | solution.py:68
  22.4 3.9 %collective-permute-start.4 = (bf16[64,256]{1,0:T(8,128)(2,1)S(1)}, bf16[64,256]{1,0:T(8,128)(2,1)S(1)}, u32[]{:S(2)}, u32[]{:S(2)}) collective-permute-start(bf16[64,256]{1,0:T(8,128)(2,1)S(1)} %shard_map.58.rest_0_), channel_id=1, source_target_pairs={{0,2},{2,0},{4,6},{6,4},{8,10},{10,8},{12,14},{14,12},{1,3},{3,1},... | collective-permute-start | bytes 98312 | tf_op jit(solution)/shard_map/ppermute | solution.py:68
  35.1 1.9 %collective-permute-start.6 = (f32[2,256]{1,0:T(2,128)S(1)}, f32[2,256]{1,0:T(2,128)S(1)}, u32[]{:S(2)}, u32[]{:S(2)}) collective-permute-start(f32[2,256]{1,0:T(2,128)S(1)} %get-tuple-element.14), channel_id=1, source_target_pairs={{0,1},{1,0},{2,3},{3,2},{4,5},{5,4},{6,7},{7,6},{8,9},{9,8},{10,11... | collective-permute-start | bytes 6152 | tf_op jit(solution)/shard_map/ppermute | solution.py:402
  35.2 3.7 %collective-permute-start.7 = (f32[2,256]{1,0:T(2,128)S(1)}, f32[2,256]{1,0:T(2,128)S(1)}, u32[]{:S(2)}, u32[]{:S(2)}) collective-permute-start(f32[2,256]{1,0:T(2,128)S(1)} %get-tuple-element.15), channel_id=1, source_target_pairs={{0,2},{2,0},{4,6},{6,4},{8,10},{10,8},{12,14},{14,12},{1,3},{3,1},... | collective-permute-start | bytes 6152 | tf_op jit(solution)/shard_map/ppermute | solution.py:68
  36.7 3.0 %collective-permute-start.8 = (f32[2,256]{1,0:T(2,128)S(1)}, f32[2,256]{1,0:T(2,128)S(1)}, u32[]{:S(2)}, u32[]{:S(2)}) collective-permute-start(f32[2,256]{1,0:T(2,128)S(1)} %get-tuple-element.16), channel_id=1, source_target_pairs={{0,3},{1,2},{2,1},{3,0},{4,7},{5,6},{6,5},{7,4},{8,11},{9,10},{10,... | collective-permute-start | bytes 6152 | tf_op jit(solution)/shard_map/ppermute | solution.py:403

commit v5 on v4

--- a/solution.py
+++ b/solution.py
@@ -83,60 +83,69 @@
 
 
 def project_kernel(
-    cuts, x_ref, g_ref, pin_ref, pout_ref, after_ref, first_ref, second_ref, x, g, pin, pout, sems
+    x_ref, g_ref, pin_ref, pout_ref, after_ref, first_ref, second_ref, *scratch
 ):
-    copies = []
-    for which, start, size in cuts:
-        source, factor, held, held_factor = (
-            (x_ref, pin_ref, x, pin) if which == 0 else (g_ref, pout_ref, g, pout)
-        )
-        here = pl.ds(start, size)
-        at = 2 * len(copies)
-        pair = (
-            pltpu.make_async_copy(
-                factor.at[:, here], held_factor.at[:, here], sems.at[at]
-            ),
-            pltpu.make_async_copy(source.at[:, here], held.at[:, here], sems.at[at + 1]),
-        )
-        for copy in pair:
-            copy.start()
-        copies.append(pair)
-    totals = [None, None]
-    for pair, (which, start, size) in zip(copies, cuts):
-        for copy in pair:
-            copy.wait()
-        here = slice(start, start + size)
-        source, factor = (x, pin) if which == 0 else (g, pout)
-        term = lax.dot_general(
-            source[:, here], factor[:, here], NT, preferred_element_type=F32
-        )
-        totals[which] = term if totals[which] is None else totals[which] + term
-    half = totals[0].shape[0] // 2
+    sides = (
+        (x_ref, pin_ref) + scratch[:4],
+        (g_ref, pout_ref) + scratch[4:8],
+    )
+
+    def copies(side, i):
+        source, factor, held, held_factor, _, sems = side
+        size = source.shape[1] // sems.shape[0]
+        here = pl.ds(pl.multiple_of(i * size, size), size)
+        return pltpu.make_async_copy(source.at[:, here], held.at[:, here], sems.at[i])
+
+    factors = [
+        pltpu.make_async_copy(side[1], side[3], scratch[8].at[i])
+        for i, side in enumerate(sides)
+    ]
+    for side, factor in zip(sides, factors):
+        factor.start()
+        for i in range(side[5].shape[0]):
+            copies(side, i).start()
+    for side, factor in zip(sides, factors):
+        _, _, held, held_factor, total, sems = side
+        size = held.shape[1] // sems.shape[0]
+        total[...] = jnp.zeros_like(total)
+        factor.wait()
+
+        def block(i, carry):
+            copies(side, i).wait()
+            here = pl.ds(pl.multiple_of(i * size, size), size)
+            total[...] += lax.dot_general(
+                held[:, here], held_factor[:, here], NT, preferred_element_type=F32
+            )
+            return carry
+
+        lax.fori_loop(0, sems.shape[0], block, 0)
+    half = first_ref.shape[0]
     for part, out_ref in enumerate((first_ref, second_ref)):
-        here = slice(part * half, (part + 1) * half)
-        out_ref[:, :RANK] = totals[0][here]
-        out_ref[:, RANK:] = totals[1][here]
+        for i, side in enumerate(sides):
+            out_ref[:, i * RANK : (i + 1) * RANK] = side[4][part * half : (part + 1) * half]
 
 
 def project(train_inputs, train_grads, proj_in, proj_out, after):
-    half = jax.ShapeDtypeStruct((train_inputs.shape[0] // 2, 2 * RANK), F32)
-    cuts = []
-    for which, array in ((0, train_inputs), (1, train_grads)):
-        size = 1024
-        cuts += [(which, at, size) for at in range(0, array.shape[1], size)]
-    return pl.pallas_call(
-        functools.partial(project_kernel, cuts),
+    tokens = train_inputs.shape[0]
+    half = jax.ShapeDtypeStruct((tokens // 2, 2 * RANK), F32)
+    scratch = []
+    for source, factor, blocks in (
+        (train_inputs, proj_in, 2),
+        (train_grads, proj_out, 4),
+    ):
+        scratch += [
+            pltpu.VMEM(source.shape, BF16),
+            pltpu.VMEM(factor.shape[::-1], BF16),
+            pltpu.VMEM((tokens, RANK), F32),
+            pltpu.SemaphoreType.DMA((blocks,)),
+        ]
+    return pl.pallas_call(
+        project_kernel,
         out_shape=(half, half),
         cost_estimate=cost(8),
         in_specs=[HBM] * 5,
         out_specs=(VMEM, VMEM),
-        scratch_shapes=[
-            pltpu.VMEM(train_inputs.shape, BF16),
-            pltpu.VMEM(train_grads.shape, BF16),
-            pltpu.VMEM(proj_in.shape[::-1], BF16),
-            pltpu.VMEM(proj_out.shape[::-1], BF16),
-            pltpu.SemaphoreType.DMA((2 * len(cuts),)),
-        ],
+        scratch_shapes=scratch + [pltpu.SemaphoreType.DMA((2,))],
         compiler_params=pltpu.CompilerParams(vmem_limit_bytes=107 * MIB // 2),
     )(train_inputs, train_grads, proj_in.T, proj_out.T, after)
 
@@ -241,16 +250,42 @@
     )
 
 
+def with_rows(m, k, rows):
+    base = k // 8 * 8
+    group = m[base : base + 8]
+    sub = iota(group.shape, 0)
+    for i, row in enumerate(rows):
+        group = jnp.where(sub == k - base + i, row, group)
+    parts = [m[:base], group, m[base + 8 :]]
+    return jnp.concatenate([p for p in parts if p.shape[0]], axis=0)
+
+
 def inverses(m):
     lane = iota((RANK, 2 * RANK), 1)
-    sub = iota((RANK, 2 * RANK), 0)
     left = lane < RANK
     place = jnp.where(left, lane, lane - RANK)
-    for k in range(0, RANK, 4):
-        cols = [
+
+    def columns(k):
+        return [
             jnp.where(left, m[:, k + i : k + i + 1], m[:, RANK + k + i : RANK + k + i + 1])
             for i in range(4)
         ]
+
+    def combine(weights, rows):
+        return [
+            (w[0] * rows[0] + w[1] * rows[1]) + (w[2] * rows[2] + w[3] * rows[3])
+            for w in weights
+        ]
+
+    def update(a, cols, news, k):
+        a = (a - cols[0] * news[0] - cols[1] * news[1]) - (
+            cols[2] * news[2] + cols[3] * news[3]
+        )
+        return with_rows(a, k, news)
+
+    cols = columns(0)
+    for k in range(0, RANK, 4):
+        later = columns(k + 4) if k + 4 < RANK else []
         pivot = inverse_4(lambda i, j: cols[j][k + i : k + i + 1])
         rows = []
         for i in range(4):
@@ -258,29 +293,18 @@
             for j in range(4):
                 row = jnp.where(place[:1] == k + j, 1.0 if i == j else 0.0, row)
             rows.append(row)
-        news = [
-            (p[0] * rows[0] + p[1] * rows[1]) + (p[2] * rows[2] + p[3] * rows[3])
-            for p in pivot
+        cleared = jnp.where((place >= k) & (place < k + 4), 0.0, m)
+        m = update(cleared, cols, combine(pivot, rows), k)
+        cols = [
+            update(a, cols, combine(pivot, [a[k + i : k + i + 1] for i in range(4)]), k)
+            for a in later
         ]
-        m = jnp.where((place >= k) & (place < k + 4), 0.0, m)
-        m = (m - cols[0] * news[0] - cols[1] * news[1]) - (
-            cols[2] * news[2] + cols[3] * news[3]
-        )
-        for i in range(4):
-            m = jnp.where(sub == k + i, news[i], m)
     return m
 
 
-def score_kernel(total, held, count, cov_ref, *rest):
-    peers = len(flips(count))
-    grads_refs, rest = rest[:2], rest[2:]
-    queries_refs, rest = rest[:peers], rest[peers:]
-    out_refs, (queries, weights, sums) = rest[:4], rest[4:]
-    for p in range(peers):
-        queries[p] = queries_refs[p][...]
-    examples = 2 * grads_refs[0].shape[1] // RANK
+def invert_kernel(total, cov_ref, left_ref, right_ref):
+    count = cov_ref.shape[0]
     half = RANK // 2
-    core = lax.axis_index("tensor")
     cov = cov_ref[0]
     for p in range(1, count):
         cov = cov + cov_ref[p]
@@ -299,12 +323,38 @@
 
     inverse = inverses(jnp.concatenate([damped(cov_in), damped(cov_out)], axis=1))
     inv_in, inv_out = inverse[:, :RANK], inverse[:, RANK:]
-    left = jnp.concatenate(pieces(inv_out), axis=0)
+    left_ref[...] = jnp.concatenate(pieces(inv_out), axis=0)
     for i, piece in enumerate(pieces(inv_in)):
-        weights[i] = jnp.zeros((WIDE, WIDE), BF16)
+        right_ref[i] = jnp.zeros((WIDE, WIDE), BF16)
         for k in range(4):
             here = slice(k * RANK, (k + 1) * RANK)
-            weights[i, here, here] = piece
+            right_ref[i, here, here] = piece
+
+
+def invert(cov, total):
+    return pl.pallas_call(
+        functools.partial(invert_kernel, total),
+        out_shape=(
+            jax.ShapeDtypeStruct((3 * RANK, RANK), BF16),
+            jax.ShapeDtypeStruct((3, WIDE, WIDE), BF16),
+        ),
+        cost_estimate=cost(4),
+        in_specs=[VMEM],
+        out_specs=(VMEM, VMEM),
+        compiler_params=SMALL,
+    )(cov)
+
+
+def score_kernel(held, count, left_ref, weights, *rest):
+    peers = len(flips(count))
+    grads_refs, rest = rest[:2], rest[2:]
+    queries_refs, rest = rest[:peers], rest[peers:]
+    out_refs, (queries, sums) = rest[:4], rest[4:]
+    for p in range(peers):
+        queries[p] = queries_refs[p][...]
+    examples = 2 * grads_refs[0].shape[1] // RANK
+    core = lax.axis_index("tensor")
+    left = left_ref[...]
     chunks = held // 4
     grads = []
     for ref in grads_refs:
@@ -363,24 +413,22 @@
         out_refs[i + 1][...] = jnp.where(core == 0, blocks[i + 1], blocks[i])
 
 
-def score(cov, grads, queries, total, held):
-    count = cov.shape[0]
+def score(left, right, grads, queries, held, count):
     peers = len(queries)
     examples = 2 * grads[0].shape[1] // RANK
     shape = jax.ShapeDtypeStruct((examples // 4, 2 * held * count), F32)
     return pl.pallas_call(
-        functools.partial(score_kernel, total, held, count),
+        functools.partial(score_kernel, held, count),
         out_shape=(shape,) * 4,
-        cost_estimate=cost(10),
-        in_specs=[VMEM] * (3 + peers),
+        cost_estimate=cost(4),
+        in_specs=[VMEM] * (4 + peers),
         out_specs=(VMEM,) * 4,
         scratch_shapes=[
             pltpu.VMEM((peers,) + queries[0].shape, BF16),
-            pltpu.VMEM((3, WIDE, WIDE), BF16),
             pltpu.VMEM((peers, examples * (held // 4), WIDE), F32),
         ],
         compiler_params=pltpu.CompilerParams(vmem_limit_bytes=24 * MIB),
-    )(cov, *grads, *queries)
+    )(left, right, *grads, *queries)
 
 
 def local(train_inputs, train_grads, proj_in, proj_out, queries):
@@ -396,7 +444,9 @@
     grads = gradients(mine, other)
     total = train_inputs.shape[0] * count
     pair = (grads, flipped(grads, count, 1))
-    keep, to_core, to_chip, to_far = score(cov, pair, gathered, total, held)
+    keep, to_core, to_chip, to_far = score(
+        *invert(cov, total), pair, gathered, held, count
+    )
     corner = [(i, i ^ 3) for i in range(2 * count)]
     return (
         (keep + lax.ppermute(to_core, "tensor", swap))

time: 40.5 us -> 38.2 us (0.943)
  Pallas kernels: 15.5 us -> 14 us
  waiting for transfers between devices: 8.2 us -> 7.35 us
    all_to_all x1, waiting for transfers between devices: 0.04 us -> 4.65 us  [local(): cov = lax.all_to_all(cov, 'dp', 0, 0, tiled=True)]
    ppermute x5, waiting for transfers between devices: 6.4 us -> 1.8 us  [flipped(): return lax.ppermute(x, 'dp', [(i, i ^ flip) for i in range(count)])]
    pallas_call x2 -> x3, Pallas kernels: 13.8 us -> 12.3 us  [the longest x1 6.59 us: project(): pl.pallas_call(project_kernel, out_shape=(half, half), cost_estimate=cost...]
    ppermute x1, starting transfers between devices: 0.36 us -> 1.78 us  [local(): lax.ppermute(to_far, ('dp', 'tensor'), corner)]
    ppermute x5, starting transfers between devices: 10.6 us -> 9.17 us  [flipped(): return lax.ppermute(x, 'dp', [(i, i ^ flip) for i in range(count)])]
    ppermute x1, waiting for transfers between devices: 0.86 us -> 0.01 us  [local(): lax.ppermute(to_far, ('dp', 'tensor'), corner)]
  transfers between devices with their start and end apart: 10 -> 10, of which waited for: 6 -> 4; matrix products, arithmetic and copies ran while one was open for 0% -> 0% of each run, Pallas kernels for 19% -> 26%
where the time goes in v5:
time: 38.2 us; the launch traced here: 38 us
  starting transfers between devices  15 us (39%)
  Pallas kernels  14 us (37%)
  waiting for transfers between devices  7.35 us (19%)
  local copies, waits for them, and re-layouts  0.95 us (2%)
  other arithmetic  0.58 us (2%)
    ppermute x5, starting transfers between devices, flipped(): return lax.ppermute(x, 'dp', [(i, i ^ flip) for i in range(count)])  9.17 us
    pallas_call x1, Pallas kernels, project(): pl.pallas_call(project_kernel, out_shape=(half, half), cost_estimate=cost...  6.59 us
    all_to_all x1, waiting for transfers between devices, local(): cov = lax.all_to_all(cov, 'dp', 0, 0, tiled=True)  4.65 us
    all_to_all x1, starting transfers between devices, local(): cov = lax.all_to_all(cov, 'dp', 0, 0, tiled=True)  3.38 us
    pallas_call x1, Pallas kernels, score(): pl.pallas_call(functools.partial(score_kernel, held, count), out_shape=(s...  3.03 us
    pallas_call x1, Pallas kernels, invert(): pl.pallas_call(functools.partial(invert_kernel, total), out_shape=(jax.Sh...  2.66 us
    ppermute x5, waiting for transfers between devices, flipped(): return lax.ppermute(x, 'dp', [(i, i ^ flip) for i in range(count)])  1.8 us
    ppermute x1, starting transfers between devices, local(): lax.ppermute(to_far, ('dp', 'tensor'), corner)  1.78 us
  transfers between devices with their start and end apart: 10, of which 4 were waited for; matrix products, arithmetic and copies ran while one was open for 0% of the time, Pallas kernels for 26%

profile of v5, /device:TPU:0, one launch (start us, length us, event | category | flops | bytes accessed | tf_op | source)
XLA Modules:
  0.0 38.0 jit_solution(13295308403358387732)
XLA Ops:
  0.0 0.0 copy-start
  0.0 0.9 %copy-done = bf16[16,64,64]{2,1,0:T(8,128)(2,1)S(1)} copy-done((bf16[16,64,64]{2,1,0:T(8,128)(2,1)S(1)}, bf16[16,64,64]{2,1,0:T(8,128)(2,1)}, u32[]{:S(2)}) %copy-start) | copy-done | bytes 131096
  1.0 0.1 shard_map.55.after_ref.rest_2_
  1.1 3.1 %collective-permute-start.3 = (bf16[64,1024]{1,0:T(8,128)(2,1)S(1)}, bf16[64,1024]{1,0:T(8,128)(2,1)S(1)}, u32[]{:S(2)}, u32[]{:S(2)}) collective-permute-start(bf16[64,1024]{1,0:T(8,128)(2,1)S(1)} %shard_map.55.after_ref.rest_2_), channel_id=1, source_target_pairs={{0,4},{2,6},{4,0},{6,2},{8,12},{10,14},{12,8},{14,10},{1,5},{3,7},... | collective-permute-start | bytes 393224 | tf_op jit(solution)/shard_map/ppermute | solution.py:68
  4.2 2.6 %collective-permute-start.2 = (bf16[64,1024]{1,0:T(8,128)(2,1)S(1)}, bf16[64,1024]{1,0:T(8,128)(2,1)S(1)}, u32[]{:S(2)}, u32[]{:S(2)}) collective-permute-start(bf16[64,1024]{1,0:T(8,128)(2,1)S(1)} %shard_map.55.after_ref.rest_2_), channel_id=1, source_target_pairs={{0,8},{2,10},{4,12},{6,14},{8,0},{10,2},{12,4},{14,6},{1,9},{3,11}... | collective-permute-start | bytes 393224 | tf_op jit(solution)/shard_map/ppermute | solution.py:68
  6.8 6.6 %shard_map.56 = (f32[128,128]{1,0:T(8,128)S(1)}, f32[128,128]{1,0:T(8,128)S(1)}) custom-call(bf16[256,4096]{1,0:T(8,128)(2,1)} %x_ref.1, bf16[256,14336]{1,0:T(8,128)(2,1)} %g_ref.1, bf16[64,4096]{1,0:T(8,128)(2,1)} %bitcast.3, bf16[64,14336]{1,0:T(8,128)(2,1)} %bitcast.2, bf16[64,1024]{1,0:T(8,128)(2,1)S(1)} %shard_map.55.after_ref.rest_2_), custom_call_target="tpu_custom_call" | custom-call | bytes 29600000 | tf_op jit(solution)/shard_map/pallas_call | solution.py:142
  13.4 0.1 collective-permute-start
  13.4 0.5 %collective-permute-start.1 = (f32[128,128]{1,0:T(8,128)S(1)}, f32[128,128]{1,0:T(8,128)S(1)}, u32[]{:S(2)}, u32[]{:S(2)}) collective-permute-start(f32[128,128]{1,0:T(8,128)S(1)} %get-tuple-element.14.refs_1_), channel_id=1, source_target_pairs={{0,1},{1,0},{2,3},{3,2},{4,5},{5,4},{6,7},{7,6},{8,9},{9,8},{10,11... | collective-permute-start | bytes 196616 | tf_op jit(solution)/shard_map/ppermute | solution.py:441
  13.9 0.7 %collective-permute-done.refs_2_ = f32[128,128]{1,0:T(8,128)S(1)} collective-permute-done((f32[128,128]{1,0:T(8,128)S(1)}, f32[128,128]{1,0:T(8,128)S(1)}, u32[]{:S(2)}, u32[]{:S(2)}) %collective-permute-start) | collective-permute-done | bytes 65568 | tf_op jit(solution)/shard_map/ppermute | solution.py:441
  14.7 0.2 collective-permute-done.1.refs_3_
  14.8 0.0 collective-permute-done.3.refs_5_.rest_3_
  14.8 0.0 collective-permute-done.2.refs_4_.rest_4_
  14.8 1.1 %shard_map.57 = f32[8,40,128]{2,1,0:T(8,128)} custom-call(f32[128,128]{1,0:T(8,128)S(1)} %get-tuple-element.13.refs_0_, f32[128,128]{1,0:T(8,128)S(1)} %get-tuple-element.14.refs_1_, f32[128,128]{1,0:T(8,128)S(1)} %collective-permute-done.refs_2_, f32[128,128]{1,0:T(8,128)S(1)} %collective-permute-done.1.refs_3_, ...), custom_call_target="tpu_custom_call" | custom-call | bytes 7400000 | tf_op jit(solution)/shard_map/pallas_call | solution.py:185
  16.0 3.4 %all-to-all-start = ((f32[8,40,128]{2,1,0:T(8,128)}), f32[8,40,128]{2,1,0:T(8,128)S(1)}, u32[]{:S(2)}, u32[]{:S(2)}) async-start(f32[8,40,128]{2,1,0:T(8,128)} %shard_map.57), calls=%async_computation | async-start | bytes 327680 | tf_op jit(solution)/shard_map/all_to_all | solution.py:443
  19.4 1.9 %collective-permute-start.5 = (bf16[64,1024]{1,0:T(8,128)(2,1)S(1)}, bf16[64,1024]{1,0:T(8,128)(2,1)S(1)}, u32[]{:S(2)}, u32[]{:S(2)}) collective-permute-start(bf16[64,1024]{1,0:T(8,128)(2,1)S(1)} %collective-permute-done.2.refs_4_.rest_4_), channel_id=1, source_target_pairs={{0,4},{2,6},{4,0},{6,2},{8,12},{10,14},{12,8},{14,10},{1,5},{3,7},... | collective-permute-start | bytes 393224 | tf_op jit(solution)/shard_map/ppermute | solution.py:68
  21.3 0.5 %shard_map.59.rest_0_ = bf16[64,256]{1,0:T(8,128)(2,1)S(1)} custom-call(f32[128,128]{1,0:T(8,128)S(1)} %get-tuple-element.13.refs_0_, f32[128,128]{1,0:T(8,128)S(1)} %get-tuple-element.14.refs_1_, f32[128,128]{1,0:T(8,128)S(1)} %collective-permute-done.refs_2_, f32[128,128]{1,0:T(8,128)S(1)} %collective-permute-done.1.refs_3_), custom_call_target="tpu_custom_call" | custom-call | bytes 7400000 | tf_op jit(solution)/shard_map/pallas_call | solution.py:205
  21.8 1.5 %collective-permute-start.4 = (bf16[64,256]{1,0:T(8,128)(2,1)S(1)}, bf16[64,256]{1,0:T(8,128)(2,1)S(1)}, u32[]{:S(2)}, u32[]{:S(2)}) collective-permute-start(bf16[64,256]{1,0:T(8,128)(2,1)S(1)} %shard_map.59.rest_0_), channel_id=1, source_target_pairs={{0,2},{2,0},{4,6},{6,4},{8,10},{10,8},{12,14},{14,12},{1,3},{3,1},... | collective-permute-start | bytes 98312 | tf_op jit(solution)/shard_map/ppermute | solution.py:68
  23.3 4.7 %all-to-all-done.cov_ref = f32[8,40,128]{2,1,0:T(8,128)S(1)} async-done(((f32[8,40,128]{2,1,0:T(8,128)}), f32[8,40,128]{2,1,0:T(8,128)S(1)}, u32[]{:S(2)}, u32[]{:S(2)}) %all-to-all-start) | async-done | bytes 163872 | tf_op jit(solution)/shard_map/all_to_all | solution.py:443
  27.9 2.7 %shard_map.58 = (bf16[192,64]{1,0:T(8,128)(2,1)S(1)}, bf16[3,256,256]{2,1,0:T(8,128)(2,1)S(1)}) custom-call(f32[8,40,128]{2,1,0:T(8,128)S(1)} %all-to-all-done.cov_ref), custom_call_target="tpu_custom_call" | custom-call | bytes 14800000 | tf_op jit(solution)/shard_map/pallas_call | solution.py:335
  30.6 0.0 collective-permute-done.4.rest_1_
  30.6 0.0 collective-permute-done.5.rest_5_
  30.6 3.0 %shard_map.60 = (f32[2,256]{1,0:T(2,128)S(1)}, f32[2,256]{1,0:T(2,128)S(1)}, f32[2,256]{1,0:T(2,128)S(1)}, f32[2,256]{1,0:T(2,128)S(1)}) custom-call(bf16[192,64]{1,0:T(8,128)(2,1)S(1)} %get-tuple-element.15.left_ref, bf16[3,256,256]{2,1,0:T(8,128)(2,1)S(1)} %get-tuple-element.16.weights, bf16[64,256]{1,0:T(8,128)(2,1)S(1)} %shard_map.59.rest_0_, ...), custom_call_target="tpu_custom_call" | custom-call | bytes 14800000 | tf_op jit(solution)/shard_map/pallas_call | solution.py:420
  33.6 0.1 collective-permute-start.6
  33.7 0.1 collective-permute-start.7
  33.8 1.8 %collective-permute-start.8 = (f32[2,256]{1,0:T(2,128)S(1)}, f32[2,256]{1,0:T(2,128)S(1)}, u32[]{:S(2)}, u32[]{:S(2)}) collective-permute-start(f32[2,256]{1,0:T(2,128)S(1)} %get-tuple-element.20), channel_id=1, source_target_pairs={{0,3},{1,2},{2,1},{3,0},{4,7},{5,6},{6,5},{7,4},{8,11},{9,10},{10,... | collective-permute-start | bytes 6152 | tf_op jit(solution)/shard_map/ppermute | solution.py:453
  35.6 0.0 collective-permute-done.6
  35.6 1.8 %collective-permute-done.7 = f32[2,256]{1,0:T(2,128)S(1)} collective-permute-done((f32[2,256]{1,0:T(2,128)S(1)}, f32[2,256]{1,0:T(2,128)S(1)}, u32[]{:S(2)}, u32[]{:S(2)}) %collective-permute-start.7) | collective-permute-done | bytes 2080 | tf_op jit(solution)/shard_map/ppermute | solution.py:68
  37.4 0.0 collective-permute-done.8
  37.4 0.6 %add_add_fusion = f32[2,256]{1,0:T(2,128)} fusion(f32[2,256]{1,0:T(2,128)S(1)} %collective-permute-done.7, f32[2,256]{1,0:T(2,128)S(1)} %collective-permute-done.8, f32[2,256]{1,0:T(2,128)S(1)} %get-tuple-element.17, f32[2,256]{1,0:T(2,128)S(1)} %collective-permute-done.6), kind=kLoop, calls=%fused_computation | loop fusion | flops 1536 | bytes 10240 | tf_op jit(solution)/shard_map/add | solution.py:452
Async XLA Ops:
  0.0 0.9 %copy-start = (bf16[16,64,64]{2,1,0:T(8,128)(2,1)S(1)}, bf16[16,64,64]{2,1,0:T(8,128)(2,1)}, u32[]{:S(2)}) copy-start(bf16[16,64,64]{2,1,0:T(8,128)(2,1)} %q_ref.1) | copy-start | bytes 393220
  1.1 13.8 %collective-permute-start.3 = (bf16[64,1024]{1,0:T(8,128)(2,1)S(1)}, bf16[64,1024]{1,0:T(8,128)(2,1)S(1)}, u32[]{:S(2)}, u32[]{:S(2)}) collective-permute-start(bf16[64,1024]{1,0:T(8,128)(2,1)S(1)} %shard_map.55.after_ref.rest_2_), channel_id=1, source_target_pairs={{0,4},{2,6},{4,0},{6,2},{8,12},{10,14},{12,8},{14,10},{1,5},{3,7},... | collective-permute-start | bytes 393224 | tf_op jit(solution)/shard_map/ppermute | solution.py:68
  4.2 10.7 %collective-permute-start.2 = (bf16[64,1024]{1,0:T(8,128)(2,1)S(1)}, bf16[64,1024]{1,0:T(8,128)(2,1)S(1)}, u32[]{:S(2)}, u32[]{:S(2)}) collective-permute-start(bf16[64,1024]{1,0:T(8,128)(2,1)S(1)} %shard_map.55.after_ref.rest_2_), channel_id=1, source_target_pairs={{0,8},{2,10},{4,12},{6,14},{8,0},{10,2},{12,4},{14,6},{1,9},{3,11}... | collective-permute-start | bytes 393224 | tf_op jit(solution)/shard_map/ppermute | solution.py:68
  13.4 1.3 %collective-permute-start = (f32[128,128]{1,0:T(8,128)S(1)}, f32[128,128]{1,0:T(8,128)S(1)}, u32[]{:S(2)}, u32[]{:S(2)}) collective-permute-start(f32[128,128]{1,0:T(8,128)S(1)} %get-tuple-element.13.refs_0_), channel_id=1, source_target_pairs={{0,1},{1,0},{2,3},{3,2},{4,5},{5,4},{6,7},{7,6},{8,9},{9,8},{10,11... | collective-permute-start | bytes 196616 | tf_op jit(solution)/shard_map/ppermute | solution.py:441
  13.4 1.4 %collective-permute-start.1 = (f32[128,128]{1,0:T(8,128)S(1)}, f32[128,128]{1,0:T(8,128)S(1)}, u32[]{:S(2)}, u32[]{:S(2)}) collective-permute-start(f32[128,128]{1,0:T(8,128)S(1)} %get-tuple-element.14.refs_1_), channel_id=1, source_target_pairs={{0,1},{1,0},{2,3},{3,2},{4,5},{5,4},{6,7},{7,6},{8,9},{9,8},{10,11... | collective-permute-start | bytes 196616 | tf_op jit(solution)/shard_map/ppermute | solution.py:441
  16.0 11.9 %all-to-all-start = ((f32[8,40,128]{2,1,0:T(8,128)}), f32[8,40,128]{2,1,0:T(8,128)S(1)}, u32[]{:S(2)}, u32[]{:S(2)}) async-start(f32[8,40,128]{2,1,0:T(8,128)} %shard_map.57), calls=%async_computation | async-start | bytes 327680 | tf_op jit(solution)/shard_map/all_to_all | solution.py:443
  19.4 11.2 %collective-permute-start.5 = (bf16[64,1024]{1,0:T(8,128)(2,1)S(1)}, bf16[64,1024]{1,0:T(8,128)(2,1)S(1)}, u32[]{:S(2)}, u32[]{:S(2)}) collective-permute-start(bf16[64,1024]{1,0:T(8,128)(2,1)S(1)} %collective-permute-done.2.refs_4_.rest_4_), channel_id=1, source_target_pairs={{0,4},{2,6},{4,0},{6,2},{8,12},{10,14},{12,8},{14,10},{1,5},{3,7},... | collective-permute-start | bytes 393224 | tf_op jit(solution)/shard_map/ppermute | solution.py:68
  21.8 8.8 %collective-permute-start.4 = (bf16[64,256]{1,0:T(8,128)(2,1)S(1)}, bf16[64,256]{1,0:T(8,128)(2,1)S(1)}, u32[]{:S(2)}, u32[]{:S(2)}) collective-permute-start(bf16[64,256]{1,0:T(8,128)(2,1)S(1)} %shard_map.59.rest_0_), channel_id=1, source_target_pairs={{0,2},{2,0},{4,6},{6,4},{8,10},{10,8},{12,14},{14,12},{1,3},{3,1},... | collective-permute-start | bytes 98312 | tf_op jit(solution)/shard_map/ppermute | solution.py:68
  33.6 1.9 %collective-permute-start.6 = (f32[2,256]{1,0:T(2,128)S(1)}, f32[2,256]{1,0:T(2,128)S(1)}, u32[]{:S(2)}, u32[]{:S(2)}) collective-permute-start(f32[2,256]{1,0:T(2,128)S(1)} %get-tuple-element.18), channel_id=1, source_target_pairs={{0,1},{1,0},{2,3},{3,2},{4,5},{5,4},{6,7},{7,6},{8,9},{9,8},{10,11... | collective-permute-start | bytes 6152 | tf_op jit(solution)/shard_map/ppermute | solution.py:452
  33.7 3.7 %collective-permute-start.7 = (f32[2,256]{1,0:T(2,128)S(1)}, f32[2,256]{1,0:T(2,128)S(1)}, u32[]{:S(2)}, u32[]{:S(2)}) collective-permute-start(f32[2,256]{1,0:T(2,128)S(1)} %get-tuple-element.19), channel_id=1, source_target_pairs={{0,2},{2,0},{4,6},{6,4},{8,10},{10,8},{12,14},{14,12},{1,3},{3,1},... | collective-permute-start | bytes 6152 | tf_op jit(solution)/shard_map/ppermute | solution.py:68
  33.8 3.6 %collective-permute-start.8 = (f32[2,256]{1,0:T(2,128)S(1)}, f32[2,256]{1,0:T(2,128)S(1)}, u32[]{:S(2)}, u32[]{:S(2)}) collective-permute-start(f32[2,256]{1,0:T(2,128)S(1)} %get-tuple-element.20), channel_id=1, source_target_pairs={{0,3},{1,2},{2,1},{3,0},{4,7},{5,6},{6,5},{7,4},{8,11},{9,10},{10,... | collective-permute-start | bytes 6152 | tf_op jit(solution)/shard_map/ppermute | solution.py:453

commit v6 on v5

--- a/solution.py
+++ b/solution.py
@@ -68,17 +68,22 @@
     return lax.ppermute(x, "dp", [(i, i ^ flip) for i in range(count)])
 
 
-def from_peers(mine, count):
+def first_from_peers(mine, count):
     known = {0: mine}
-    bits = []
-    while 2 << len(bits) < count:
-        bits.append(2 << len(bits))
-    for bit in reversed(bits[-2:]):
-        known[bit] = flipped(mine, count, bit)
-    for i, bit in enumerate(reversed(bits)):
+    for bit in sorted(flips(count))[1:]:
+        if bit & (bit - 1) == 0 and bit * 8 > count:
+            known[bit] = flipped(mine, count, bit)
+    return known
+
+
+def all_from_peers(known, count):
+    known = dict(known)
+    bit = count // 2
+    while bit > 1:
         for m in sorted(known):
-            if m & bit == 0 and m | bit not in known and m % (2 * bit) == 0:
+            if m % (2 * bit) == 0 and m | bit not in known:
                 known[m | bit] = flipped(known[m], count, bit)
+        bit //= 2
     return [known[m] for m in flips(count)]
 
 
@@ -165,9 +170,14 @@
     return jnp.concatenate([a[...] + c[...], b[...] + d[...]], axis=0)
 
 
-def covariance_kernel(count, *refs):
-    cov_ref = refs[-1]
-    gram = over_rows(both_halves(refs[:4]))
+def gram_kernel(early, *refs):
+    cov_ref, grads_ref = refs[4 + early : 6 + early]
+    full = both_halves(refs[:4])
+    gram = None
+    for e in range(full.shape[0] // SEQ):
+        term = over_rows(full[e * SEQ : (e + 1) * SEQ])
+        grads_ref[:, e * RANK : (e + 1) * RANK] = term[RANK:, :RANK].astype(BF16)
+        gram = term if gram is None else gram + term
     cov_in = gram[:RANK, :RANK]
     cov_out = gram[RANK:, RANK:]
     row, col = iota((RANK, RANK), 0), iota((RANK, RANK), 1)
@@ -176,40 +186,25 @@
     half = RANK // 2
     body = jnp.concatenate([packed[:half], packed[half:]], axis=1)
     tail = jnp.concatenate([jnp.broadcast_to(diagonal, (8, RANK))] * 2, axis=1)
-    for p in range(count):
-        cov_ref[p, :half] = body
-        cov_ref[p, half:] = tail
-
-
-def covariances(mine, other, after, count):
-    return pl.pallas_call(
-        functools.partial(covariance_kernel, count),
-        out_shape=jax.ShapeDtypeStruct((count, RANK // 2 + 8, 2 * RANK), F32),
-        cost_estimate=cost(2),
-        in_specs=[VMEM] * (4 + len(after)),
-        out_specs=VMEM,
+    cov_ref[:half] = body
+    cov_ref[half:] = tail
+
+
+def grams(mine, other, early):
+    examples = 2 * mine[0].shape[0] // SEQ
+    return pl.pallas_call(
+        functools.partial(gram_kernel, len(early)),
+        out_shape=[
+            jax.ShapeDtypeStruct((RANK // 2 + 8, 2 * RANK), F32),
+            jax.ShapeDtypeStruct((RANK, examples * RANK), BF16),
+        ]
+        + [jax.ShapeDtypeStruct(a.shape, a.dtype) for a in early],
+        cost_estimate=cost(1),
+        in_specs=[VMEM] * 4 + [HBM] * len(early),
+        out_specs=[VMEM] * 2 + [HBM] * len(early),
+        input_output_aliases={4 + i: 2 + i for i in range(len(early))},
         compiler_params=SMALL,
-    )(*mine, *other, *after)
-
-
-def gradient_kernel(*refs):
-    grads_ref = refs[-1]
-    full = both_halves(refs[:4])
-    for e in range(full.shape[0] // SEQ):
-        gram = over_rows(full[e * SEQ : (e + 1) * SEQ])
-        grads_ref[:, e * RANK : (e + 1) * RANK] = gram[RANK:, :RANK].astype(BF16)
-
-
-def gradients(mine, other):
-    examples = 2 * mine[0].shape[0] // SEQ
-    return pl.pallas_call(
-        gradient_kernel,
-        out_shape=jax.ShapeDtypeStruct((RANK, examples * RANK), BF16),
-        cost_estimate=cost(2),
-        in_specs=[VMEM] * 4,
-        out_specs=VMEM,
-        compiler_params=SMALL,
-    )(*mine, *other)
+    )(*mine, *other, *early)
 
 
 def inverse_2(m):
@@ -302,12 +297,38 @@
     return m
 
 
-def invert_kernel(total, cov_ref, left_ref, right_ref):
-    count = cov_ref.shape[0]
+def sum_kernel(*refs):
+    refs[-1][...] = functools.reduce(jnp.add, [ref[...] for ref in refs[:-1]])
+
+
+def summed(arrays):
+    if len(arrays) == 1:
+        return arrays[0]
+    return pl.pallas_call(
+        sum_kernel,
+        out_shape=jax.ShapeDtypeStruct(arrays[0].shape, F32),
+        cost_estimate=cost(0.2),
+        in_specs=[VMEM] * len(arrays),
+        out_specs=VMEM,
+        compiler_params=SMALL,
+    )(*arrays)
+
+
+def over_peers(mine, count):
+    arrays = [mine]
+    bit = 1
+    while bit < count:
+        mine = summed(arrays)
+        group = [bit] if bit == 1 or 2 * bit == count else [3 * bit, 2 * bit, bit]
+        arrays = [mine] + [flipped(mine, count, flip) for flip in group]
+        bit *= len(group) + 1
+    return arrays
+
+
+def invert_kernel(total, *refs):
+    left_ref, right_ref = refs[-2:]
     half = RANK // 2
-    cov = cov_ref[0]
-    for p in range(1, count):
-        cov = cov + cov_ref[p]
+    cov = functools.reduce(jnp.add, [ref[...] for ref in refs[:-2]])
     cov = cov / total
     packed = jnp.concatenate([cov[:half, :RANK], cov[:half, RANK:]], axis=0)
     turned = packed.T
@@ -331,7 +352,7 @@
             right_ref[i, here, here] = piece
 
 
-def invert(cov, total):
+def invert(covs, total):
     return pl.pallas_call(
         functools.partial(invert_kernel, total),
         out_shape=(
@@ -339,10 +360,10 @@
             jax.ShapeDtypeStruct((3, WIDE, WIDE), BF16),
         ),
         cost_estimate=cost(4),
-        in_specs=[VMEM],
+        in_specs=[VMEM] * len(covs),
         out_specs=(VMEM, VMEM),
         compiler_params=SMALL,
-    )(cov)
+    )(*covs)
 
 
 def score_kernel(held, count, left_ref, weights, *rest):
@@ -383,7 +404,7 @@
                 )
         return carry
 
-    lax.fori_loop(0, peers, of_peer, 0)
+    lax.fori_loop(0, peers, of_peer, 0, unroll=min(peers, 4))
     width = 2 * held * count
     lanes = (WIDE, width)
     pick = jnp.where(iota(lanes, 0) // RANK == iota(lanes, 1) % 4, 1.0, 0.0).astype(BF16)
@@ -436,16 +457,18 @@
     swap = [(0, 1), (1, 0)]
     held = queries.shape[0]
     spread_queries = spread(queries)
-    gathered = from_peers(spread_queries, count)
+    known = first_from_peers(spread_queries, count)
     mine = project(train_inputs, train_grads, proj_in, proj_out, spread_queries)
     other = [lax.ppermute(part, "tensor", swap) for part in mine]
-    cov = covariances(mine, other, [gathered[count // 4], gathered[count // 8]], count)
-    cov = lax.all_to_all(cov, "dp", 0, 0, tiled=True)
-    grads = gradients(mine, other)
+    early = sorted(set(known) - {0})
+    cov, grads, *arrived = grams(mine, other, [known[m] for m in early])
+    known.update(zip(early, arrived))
+    gathered = all_from_peers(known, count)
+    covs = over_peers(cov, count)
     total = train_inputs.shape[0] * count
     pair = (grads, flipped(grads, count, 1))
     keep, to_core, to_chip, to_far = score(
-        *invert(cov, total), pair, gathered, held, count
+        *invert(covs, total), pair, gathered, held, count
     )
     corner = [(i, i ^ 3) for i in range(2 * count)]
     return (

time: 38.2 us -> 36.8 us (0.963)
  Pallas kernels: 14 us -> 12.2 us
    ppermute x5 -> x9, starting transfers between devices: 9.17 us -> 14.1 us  [flipped(): return lax.ppermute(x, 'dp', [(i, i ^ flip) for i in range(count)])]
    all_to_all x1 -> x0, waiting for transfers between devices: 4.65 us -> none  [local(): cov = lax.all_to_all(cov, 'dp', 0, 0, tiled=True)]
    ppermute x5 -> x9, waiting for transfers between devices: 1.8 us -> 5.64 us  [flipped(): return lax.ppermute(x, 'dp', [(i, i ^ flip) for i in range(count)])]
    all_to_all x1 -> x0, starting transfers between devices: 3.38 us -> none  [local(): cov = lax.all_to_all(cov, 'dp', 0, 0, tiled=True)]
    ppermute x1, starting transfers between devices: 1.78 us -> 0.01 us  [local(): lax.ppermute(to_far, ('dp', 'tensor'), corner)]
    pallas_call x2, Pallas kernels: 1.61 us -> 0.57 us  [the longest x1 0.57 us: grams(): pl.pallas_call(functools.partial(gram_kernel, len(early)), out_shape=[jax...]
    ppermute x1, waiting for transfers between devices: 0.01 us -> 0.95 us  [local(): lax.ppermute(to_far, ('dp', 'tensor'), corner)]
    pallas_call x1, Pallas kernels: 3.03 us -> 2.25 us  [score(): pl.pallas_call(functools.partial(score_kernel, held, count), out_shape=(s...]
  transfers between devices with their start and end apart: 10 -> 13, of which waited for: 4 -> 8; matrix products, arithmetic and copies ran while one was open for 0% -> 0% of each run, Pallas kernels for 26% -> 25%
where the time goes in v6:
time: 36.8 us; the launch traced here: 36.6 us
  starting transfers between devices  15.3 us (42%)
  Pallas kernels  12.2 us (33%)
  waiting for transfers between devices  7.5 us (20%)
  local copies, waits for them, and re-layouts  0.95 us (3%)
  other arithmetic  0.58 us (2%)
    ppermute x9, starting transfers between devices, flipped(): return lax.ppermute(x, 'dp', [(i, i ^ flip) for i in range(count)])  14.1 us
    pallas_call x1, Pallas kernels, project(): pl.pallas_call(project_kernel, out_shape=(half, half), cost_estimate=cost...  6.59 us
    ppermute x9, waiting for transfers between devices, flipped(): return lax.ppermute(x, 'dp', [(i, i ^ flip) for i in range(count)])  5.64 us
    pallas_call x1, Pallas kernels, invert(): pl.pallas_call(functools.partial(invert_kernel, total), out_shape=(jax.Sh...  2.66 us
    pallas_call x1, Pallas kernels, score(): pl.pallas_call(functools.partial(score_kernel, held, count), out_shape=(s...  2.25 us
    ppermute x1, waiting for transfers between devices, local(): lax.ppermute(to_far, ('dp', 'tensor'), corner)  0.95 us
    unnamed x2, local copies, waits for them, and re-layouts  0.95 us
    ppermute x2, waiting for transfers between devices, local(): other = [lax.ppermute(part, 'tensor', swap) for part in mine]  0.9 us
  transfers between devices with their start and end apart: 13, of which 8 were waited for; matrix products, arithmetic and copies ran while one was open for 0% of the time, Pallas kernels for 25%

profile of v6, /device:TPU:0, one launch (start us, length us, event | category | flops | bytes accessed | tf_op | source)
XLA Modules:
  0.0 36.6 jit_solution(15121193345194838028)
XLA Ops:
  0.0 0.0 copy-start
  0.0 0.9 %copy-done = bf16[16,64,64]{2,1,0:T(8,128)(2,1)S(1)} copy-done((bf16[16,64,64]{2,1,0:T(8,128)(2,1)S(1)}, bf16[16,64,64]{2,1,0:T(8,128)(2,1)}, u32[]{:S(2)}) %copy-start) | copy-done | bytes 131096
  1.0 0.1 shard_map.55.after_ref.rest_2_
  1.1 3.1 %collective-permute-start.2 = (bf16[64,1024]{1,0:T(8,128)(2,1)S(1)}, bf16[64,1024]{1,0:T(8,128)(2,1)S(1)}, u32[]{:S(2)}, u32[]{:S(2)}) collective-permute-start(bf16[64,1024]{1,0:T(8,128)(2,1)S(1)} %shard_map.55.after_ref.rest_2_), channel_id=1, source_target_pairs={{0,4},{2,6},{4,0},{6,2},{8,12},{10,14},{12,8},{14,10},{1,5},{3,7},... | collective-permute-start | bytes 393224 | tf_op jit(solution)/shard_map/ppermute | solution.py:68
  4.2 2.6 %collective-permute-start.3 = (bf16[64,1024]{1,0:T(8,128)(2,1)S(1)}, bf16[64,1024]{1,0:T(8,128)(2,1)S(1)}, u32[]{:S(2)}, u32[]{:S(2)}) collective-permute-start(bf16[64,1024]{1,0:T(8,128)(2,1)S(1)} %shard_map.55.after_ref.rest_2_), channel_id=1, source_target_pairs={{0,8},{2,10},{4,12},{6,14},{8,0},{10,2},{12,4},{14,6},{1,9},{3,11}... | collective-permute-start | bytes 393224 | tf_op jit(solution)/shard_map/ppermute | solution.py:68
  6.8 6.6 %shard_map.56 = (f32[128,128]{1,0:T(8,128)S(1)}, f32[128,128]{1,0:T(8,128)S(1)}) custom-call(bf16[256,4096]{1,0:T(8,128)(2,1)} %x_ref.1, bf16[256,14336]{1,0:T(8,128)(2,1)} %g_ref.1, bf16[64,4096]{1,0:T(8,128)(2,1)} %bitcast.3, bf16[64,14336]{1,0:T(8,128)(2,1)} %bitcast.2, bf16[64,1024]{1,0:T(8,128)(2,1)S(1)} %shard_map.55.after_ref.rest_2_), custom_call_target="tpu_custom_call" | custom-call | bytes 29600000 | tf_op jit(solution)/shard_map/pallas_call | solution.py:147
  13.4 0.1 collective-permute-start
  13.4 0.5 %collective-permute-start.1 = (f32[128,128]{1,0:T(8,128)S(1)}, f32[128,128]{1,0:T(8,128)S(1)}, u32[]{:S(2)}, u32[]{:S(2)}) collective-permute-start(f32[128,128]{1,0:T(8,128)S(1)} %get-tuple-element.18.refs_1_), channel_id=1, source_target_pairs={{0,1},{1,0},{2,3},{3,2},{4,5},{5,4},{6,7},{7,6},{8,9},{9,8},{10,11... | collective-permute-start | bytes 196616 | tf_op jit(solution)/shard_map/ppermute | solution.py:462
  13.9 0.7 %collective-permute-done.refs_2_ = f32[128,128]{1,0:T(8,128)S(1)} collective-permute-done((f32[128,128]{1,0:T(8,128)S(1)}, f32[128,128]{1,0:T(8,128)S(1)}, u32[]{:S(2)}, u32[]{:S(2)}) %collective-permute-start) | collective-permute-done | bytes 65568 | tf_op jit(solution)/shard_map/ppermute | solution.py:462
  14.7 0.2 collective-permute-done.1.refs_3_
  14.8 0.0 collective-permute-done.2.refs_4_
  14.8 0.0 collective-permute-done.3.refs_5_
  14.8 0.6 %shard_map.57 = (f32[40,128]{1,0:T(8,128)S(1)}, bf16[64,256]{1,0:T(8,128)(2,1)S(1)}, bf16[64,1024]{1,0:T(8,128)(2,1)S(1)}, bf16[64,1024]{1,0:T(8,128)(2,1)S(1)}) custom-call(f32[128,128]{1,0:T(8,128)S(1)} %get-tuple-element.17.refs_0_, f32[128,128]{1,0:T(8,128)S(1)} %get-tuple-element.18.refs_1_, ...), custom_call_target="tpu_custom_call", output_to_operand_aliasing={{2}: (4, {}), {3}: (5, {})} | custom-call | bytes 3700000 | tf_op jit(solution)/shard_map/pallas_call | solution.py:195
  15.4 0.5 %collective-permute-start.9 = (bf16[64,1024]{1,0:T(8,128)(2,1)S(1)}, bf16[64,1024]{1,0:T(8,128)(2,1)S(1)}, u32[]{:S(2)}, u32[]{:S(2)}) collective-permute-start(bf16[64,1024]{1,0:T(8,128)(2,1)S(1)} %get-tuple-element.24.rest_4_), channel_id=1, source_target_pairs={{0,4},{2,6},{4,0},{6,2},{8,12},{10,14},{12,8},{14,10},{1,5},{3,7},... | collective-permute-start | bytes 393224 | tf_op jit(solution)/shard_map/ppermute | solution.py:68
  15.9 1.5 %collective-permute-start.4 = (f32[40,128]{1,0:T(8,128)S(1)}, f32[40,128]{1,0:T(8,128)S(1)}, u32[]{:S(2)}, u32[]{:S(2)}) collective-permute-start(f32[40,128]{1,0:T(8,128)S(1)} %get-tuple-element.19.refs_0_), channel_id=1, source_target_pairs={{0,2},{2,0},{4,6},{6,4},{8,10},{10,8},{12,14},{14,12},{1,3},{3,1},... | collective-permute-start | bytes 61448 | tf_op jit(solution)/shard_map/ppermute | solution.py:68
  17.4 0.5 %collective-permute-start.8 = (bf16[64,256]{1,0:T(8,128)(2,1)S(1)}, bf16[64,256]{1,0:T(8,128)(2,1)S(1)}, u32[]{:S(2)}, u32[]{:S(2)}) collective-permute-start(bf16[64,256]{1,0:T(8,128)(2,1)S(1)} %get-tuple-element.22.rest_0_), channel_id=1, source_target_pairs={{0,2},{2,0},{4,6},{6,4},{8,10},{10,8},{12,14},{14,12},{1,3},{3,1},... | collective-permute-start | bytes 98312 | tf_op jit(solution)/shard_map/ppermute | solution.py:68
  17.9 1.8 %collective-permute-done.4.refs_1_ = f32[40,128]{1,0:T(8,128)S(1)} collective-permute-done((f32[40,128]{1,0:T(8,128)S(1)}, f32[40,128]{1,0:T(8,128)S(1)}, u32[]{:S(2)}, u32[]{:S(2)}) %collective-permute-start.4) | collective-permute-done | bytes 20512 | tf_op jit(solution)/shard_map/ppermute | solution.py:68
  19.7 1.4 %collective-permute-start.5 = (f32[40,128]{1,0:T(8,128)S(1)}, f32[40,128]{1,0:T(8,128)S(1)}, u32[]{:S(2)}, u32[]{:S(2)}) collective-permute-start(f32[40,128]{1,0:T(8,128)S(1)} %shard_map.58.refs_0_), channel_id=1, source_target_pairs={{0,12},{2,14},{4,8},{6,10},{8,4},{10,6},{12,0},{14,2},{1,13},{3,15... | collective-permute-start | bytes 61448 | tf_op jit(solution)/shard_map/ppermute | solution.py:68
  21.0 1.7 %collective-permute-start.6 = (f32[40,128]{1,0:T(8,128)S(1)}, f32[40,128]{1,0:T(8,128)S(1)}, u32[]{:S(2)}, u32[]{:S(2)}) collective-permute-start(f32[40,128]{1,0:T(8,128)S(1)} %shard_map.58.refs_0_), channel_id=1, source_target_pairs={{0,8},{2,10},{4,12},{6,14},{8,0},{10,2},{12,4},{14,6},{1,9},{3,11}... | collective-permute-start | bytes 61448 | tf_op jit(solution)/shard_map/ppermute | solution.py:68
  22.7 1.3 %collective-permute-start.7 = (f32[40,128]{1,0:T(8,128)S(1)}, f32[40,128]{1,0:T(8,128)S(1)}, u32[]{:S(2)}, u32[]{:S(2)}) collective-permute-start(f32[40,128]{1,0:T(8,128)S(1)} %shard_map.58.refs_0_), channel_id=1, source_target_pairs={{0,4},{2,6},{4,0},{6,2},{8,12},{10,14},{12,8},{14,10},{1,5},{3,7},... | collective-permute-start | bytes 61448 | tf_op jit(solution)/shard_map/ppermute | solution.py:68
  24.0 1.2 %collective-permute-done.5.refs_1_ = f32[40,128]{1,0:T(8,128)S(1)} collective-permute-done((f32[40,128]{1,0:T(8,128)S(1)}, f32[40,128]{1,0:T(8,128)S(1)}, u32[]{:S(2)}, u32[]{:S(2)}) %collective-permute-start.5) | collective-permute-done | bytes 20512 | tf_op jit(solution)/shard_map/ppermute | solution.py:68
  25.2 0.5 %collective-permute-done.6.refs_2_ = f32[40,128]{1,0:T(8,128)S(1)} collective-permute-done((f32[40,128]{1,0:T(8,128)S(1)}, f32[40,128]{1,0:T(8,128)S(1)}, u32[]{:S(2)}, u32[]{:S(2)}) %collective-permute-start.6) | collective-permute-done | bytes 20512 | tf_op jit(solution)/shard_map/ppermute | solution.py:68
  25.7 0.8 %collective-permute-done.7.refs_3_ = f32[40,128]{1,0:T(8,128)S(1)} collective-permute-done((f32[40,128]{1,0:T(8,128)S(1)}, f32[40,128]{1,0:T(8,128)S(1)}, u32[]{:S(2)}, u32[]{:S(2)}) %collective-permute-start.7) | collective-permute-done | bytes 20512 | tf_op jit(solution)/shard_map/ppermute | solution.py:68
  26.5 2.7 %shard_map.59 = (bf16[192,64]{1,0:T(8,128)(2,1)S(1)}, bf16[3,256,256]{2,1,0:T(8,128)(2,1)S(1)}) custom-call(f32[40,128]{1,0:T(8,128)S(1)} %shard_map.58.refs_0_, f32[40,128]{1,0:T(8,128)S(1)} %collective-permute-done.5.refs_1_, f32[40,128]{1,0:T(8,128)S(1)} %collective-permute-done.6.refs_2_, f32[40,128]{1,0:T(8,128)S(1)} %collective-permute-done.7.refs_3_), custom_call_target="tpu_custom_call" | custom-call | bytes 14800000 | tf_op jit(solution)/shard_map/pallas_call | solution.py:356
  29.2 0.0 collective-permute-done.8.rest_1_
  29.2 0.0 collective-permute-done.9.rest_5_
  29.2 2.2 %shard_map.60 = (f32[2,256]{1,0:T(2,128)S(1)}, f32[2,256]{1,0:T(2,128)S(1)}, f32[2,256]{1,0:T(2,128)S(1)}, f32[2,256]{1,0:T(2,128)S(1)}) custom-call(bf16[192,64]{1,0:T(8,128)(2,1)S(1)} %get-tuple-element.20.left_ref, bf16[3,256,256]{2,1,0:T(8,128)(2,1)S(1)} %get-tuple-element.21.weights, bf16[64,256]{1,0:T(8,128)(2,1)S(1)} %get-tuple-element.22.rest_0_, ...), custom_call_target="tpu_custom_call" | custom-call | bytes 14800000 | tf_op jit(solution)/shard_map/pallas_call | solution.py:441
  31.4 1.6 %collective-permute-start.11 = (f32[2,256]{1,0:T(2,128)S(1)}, f32[2,256]{1,0:T(2,128)S(1)}, u32[]{:S(2)}, u32[]{:S(2)}) collective-permute-start(f32[2,256]{1,0:T(2,128)S(1)} %get-tuple-element.27), channel_id=1, source_target_pairs={{0,2},{2,0},{4,6},{6,4},{8,10},{10,8},{12,14},{14,12},{1,3},{3,1},... | collective-permute-start | bytes 6152 | tf_op jit(solution)/shard_map/ppermute | solution.py:68
  33.0 0.0 collective-permute-start.12
  33.0 0.6 %collective-permute-start.10 = (f32[2,256]{1,0:T(2,128)S(1)}, f32[2,256]{1,0:T(2,128)S(1)}, u32[]{:S(2)}, u32[]{:S(2)}) collective-permute-start(f32[2,256]{1,0:T(2,128)S(1)} %get-tuple-element.26), channel_id=1, source_target_pairs={{0,1},{1,0},{2,3},{3,2},{4,5},{5,4},{6,7},{7,6},{8,9},{9,8},{10,11... | collective-permute-start | bytes 6152 | tf_op jit(solution)/shard_map/ppermute | solution.py:475
  33.6 1.4 %collective-permute-done.11 = f32[2,256]{1,0:T(2,128)S(1)} collective-permute-done((f32[2,256]{1,0:T(2,128)S(1)}, f32[2,256]{1,0:T(2,128)S(1)}, u32[]{:S(2)}, u32[]{:S(2)}) %collective-permute-start.11) | collective-permute-done | bytes 2080 | tf_op jit(solution)/shard_map/ppermute | solution.py:68
  35.1 1.0 %collective-permute-done.12 = f32[2,256]{1,0:T(2,128)S(1)} collective-permute-done((f32[2,256]{1,0:T(2,128)S(1)}, f32[2,256]{1,0:T(2,128)S(1)}, u32[]{:S(2)}, u32[]{:S(2)}) %collective-permute-start.12) | collective-permute-done | bytes 2080 | tf_op jit(solution)/shard_map/ppermute | solution.py:476
  36.0 0.0 collective-permute-done.10
  36.0 0.6 %add_add_fusion = f32[2,256]{1,0:T(2,128)} fusion(f32[2,256]{1,0:T(2,128)S(1)} %collective-permute-done.11, f32[2,256]{1,0:T(2,128)S(1)} %collective-permute-done.12, f32[2,256]{1,0:T(2,128)S(1)} %get-tuple-element.25, f32[2,256]{1,0:T(2,128)S(1)} %collective-permute-done.10), kind=kLoop, calls=%fused_computation | loop fusion | flops 1536 | bytes 10240 | tf_op jit(solution)/shard_map/add | solution.py:475
  (1 shorter events, 0.0 us)
Async XLA Ops:
  0.0 0.9 %copy-start = (bf16[16,64,64]{2,1,0:T(8,128)(2,1)S(1)}, bf16[16,64,64]{2,1,0:T(8,128)(2,1)}, u32[]{:S(2)}) copy-start(bf16[16,64,64]{2,1,0:T(8,128)(2,1)} %q_ref.1) | copy-start | bytes 393220
  1.1 13.8 %collective-permute-start.2 = (bf16[64,1024]{1,0:T(8,128)(2,1)S(1)}, bf16[64,1024]{1,0:T(8,128)(2,1)S(1)}, u32[]{:S(2)}, u32[]{:S(2)}) collective-permute-start(bf16[64,1024]{1,0:T(8,128)(2,1)S(1)} %shard_map.55.after_ref.rest_2_), channel_id=1, source_target_pairs={{0,4},{2,6},{4,0},{6,2},{8,12},{10,14},{12,8},{14,10},{1,5},{3,7},... | collective-permute-start | bytes 393224 | tf_op jit(solution)/shard_map/ppermute | solution.py:68
  4.2 10.7 %collective-permute-start.3 = (bf16[64,1024]{1,0:T(8,128)(2,1)S(1)}, bf16[64,1024]{1,0:T(8,128)(2,1)S(1)}, u32[]{:S(2)}, u32[]{:S(2)}) collective-permute-start(bf16[64,1024]{1,0:T(8,128)(2,1)S(1)} %shard_map.55.after_ref.rest_2_), channel_id=1, source_target_pairs={{0,8},{2,10},{4,12},{6,14},{8,0},{10,2},{12,4},{14,6},{1,9},{3,11}... | collective-permute-start | bytes 393224 | tf_op jit(solution)/shard_map/ppermute | solution.py:68
  13.4 1.3 %collective-permute-start = (f32[128,128]{1,0:T(8,128)S(1)}, f32[128,128]{1,0:T(8,128)S(1)}, u32[]{:S(2)}, u32[]{:S(2)}) collective-permute-start(f32[128,128]{1,0:T(8,128)S(1)} %get-tuple-element.17.refs_0_), channel_id=1, source_target_pairs={{0,1},{1,0},{2,3},{3,2},{4,5},{5,4},{6,7},{7,6},{8,9},{9,8},{10,11... | collective-permute-start | bytes 196616 | tf_op jit(solution)/shard_map/ppermute | solution.py:462
  13.4 1.4 %collective-permute-start.1 = (f32[128,128]{1,0:T(8,128)S(1)}, f32[128,128]{1,0:T(8,128)S(1)}, u32[]{:S(2)}, u32[]{:S(2)}) collective-permute-start(f32[128,128]{1,0:T(8,128)S(1)} %get-tuple-element.18.refs_1_), channel_id=1, source_target_pairs={{0,1},{1,0},{2,3},{3,2},{4,5},{5,4},{6,7},{7,6},{8,9},{9,8},{10,11... | collective-permute-start | bytes 196616 | tf_op jit(solution)/shard_map/ppermute | solution.py:462
  15.4 13.8 %collective-permute-start.9 = (bf16[64,1024]{1,0:T(8,128)(2,1)S(1)}, bf16[64,1024]{1,0:T(8,128)(2,1)S(1)}, u32[]{:S(2)}, u32[]{:S(2)}) collective-permute-start(bf16[64,1024]{1,0:T(8,128)(2,1)S(1)} %get-tuple-element.24.rest_4_), channel_id=1, source_target_pairs={{0,4},{2,6},{4,0},{6,2},{8,12},{10,14},{12,8},{14,10},{1,5},{3,7},... | collective-permute-start | bytes 393224 | tf_op jit(solution)/shard_map/ppermute | solution.py:68
  15.9 3.8 %collective-permute-start.4 = (f32[40,128]{1,0:T(8,128)S(1)}, f32[40,128]{1,0:T(8,128)S(1)}, u32[]{:S(2)}, u32[]{:S(2)}) collective-permute-start(f32[40,128]{1,0:T(8,128)S(1)} %get-tuple-element.19.refs_0_), channel_id=1, source_target_pairs={{0,2},{2,0},{4,6},{6,4},{8,10},{10,8},{12,14},{14,12},{1,3},{3,1},... | collective-permute-start | bytes 61448 | tf_op jit(solution)/shard_map/ppermute | solution.py:68
  17.4 11.8 %collective-permute-start.8 = (bf16[64,256]{1,0:T(8,128)(2,1)S(1)}, bf16[64,256]{1,0:T(8,128)(2,1)S(1)}, u32[]{:S(2)}, u32[]{:S(2)}) collective-permute-start(bf16[64,256]{1,0:T(8,128)(2,1)S(1)} %get-tuple-element.22.rest_0_), channel_id=1, source_target_pairs={{0,2},{2,0},{4,6},{6,4},{8,10},{10,8},{12,14},{14,12},{1,3},{3,1},... | collective-permute-start | bytes 98312 | tf_op jit(solution)/shard_map/ppermute | solution.py:68
  19.7 5.6 %collective-permute-start.5 = (f32[40,128]{1,0:T(8,128)S(1)}, f32[40,128]{1,0:T(8,128)S(1)}, u32[]{:S(2)}, u32[]{:S(2)}) collective-permute-start(f32[40,128]{1,0:T(8,128)S(1)} %shard_map.58.refs_0_), channel_id=1, source_target_pairs={{0,12},{2,14},{4,8},{6,10},{8,4},{10,6},{12,0},{14,2},{1,13},{3,15... | collective-permute-start | bytes 61448 | tf_op jit(solution)/shard_map/ppermute | solution.py:68
  21.0 4.7 %collective-permute-start.6 = (f32[40,128]{1,0:T(8,128)S(1)}, f32[40,128]{1,0:T(8,128)S(1)}, u32[]{:S(2)}, u32[]{:S(2)}) collective-permute-start(f32[40,128]{1,0:T(8,128)S(1)} %shard_map.58.refs_0_), channel_id=1, source_target_pairs={{0,8},{2,10},{4,12},{6,14},{8,0},{10,2},{12,4},{14,6},{1,9},{3,11}... | collective-permute-start | bytes 61448 | tf_op jit(solution)/shard_map/ppermute | solution.py:68
  22.7 3.8 %collective-permute-start.7 = (f32[40,128]{1,0:T(8,128)S(1)}, f32[40,128]{1,0:T(8,128)S(1)}, u32[]{:S(2)}, u32[]{:S(2)}) collective-permute-start(f32[40,128]{1,0:T(8,128)S(1)} %shard_map.58.refs_0_), channel_id=1, source_target_pairs={{0,4},{2,6},{4,0},{6,2},{8,12},{10,14},{12,8},{14,10},{1,5},{3,7},... | collective-permute-start | bytes 61448 | tf_op jit(solution)/shard_map/ppermute | solution.py:68
  31.4 3.7 %collective-permute-start.11 = (f32[2,256]{1,0:T(2,128)S(1)}, f32[2,256]{1,0:T(2,128)S(1)}, u32[]{:S(2)}, u32[]{:S(2)}) collective-permute-start(f32[2,256]{1,0:T(2,128)S(1)} %get-tuple-element.27), channel_id=1, source_target_pairs={{0,2},{2,0},{4,6},{6,4},{8,10},{10,8},{12,14},{14,12},{1,3},{3,1},... | collective-permute-start | bytes 6152 | tf_op jit(solution)/shard_map/ppermute | solution.py:68
  33.0 3.0 %collective-permute-start.12 = (f32[2,256]{1,0:T(2,128)S(1)}, f32[2,256]{1,0:T(2,128)S(1)}, u32[]{:S(2)}, u32[]{:S(2)}) collective-permute-start(f32[2,256]{1,0:T(2,128)S(1)} %get-tuple-element.28), channel_id=1, source_target_pairs={{0,3},{1,2},{2,1},{3,0},{4,7},{5,6},{6,5},{7,4},{8,11},{9,10},{10,... | collective-permute-start | bytes 6152 | tf_op jit(solution)/shard_map/ppermute | solution.py:476
  33.0 3.0 %collective-permute-start.10 = (f32[2,256]{1,0:T(2,128)S(1)}, f32[2,256]{1,0:T(2,128)S(1)}, u32[]{:S(2)}, u32[]{:S(2)}) collective-permute-start(f32[2,256]{1,0:T(2,128)S(1)} %get-tuple-element.26), channel_id=1, source_target_pairs={{0,1},{1,0},{2,3},{3,2},{4,5},{5,4},{6,7},{7,6},{8,9},{9,8},{10,11... | collective-permute-start | bytes 6152 | tf_op jit(solution)/shard_map/ppermute | solution.py:475

commit v7 on v6

--- a/solution.py
+++ b/solution.py
@@ -91,8 +91,8 @@
     x_ref, g_ref, pin_ref, pout_ref, after_ref, first_ref, second_ref, *scratch
 ):
     sides = (
+        (g_ref, pout_ref) + scratch[4:8],
         (x_ref, pin_ref) + scratch[:4],
-        (g_ref, pout_ref) + scratch[4:8],
     )
 
     def copies(side, i):
@@ -126,7 +126,7 @@
         lax.fori_loop(0, sems.shape[0], block, 0)
     half = first_ref.shape[0]
     for part, out_ref in enumerate((first_ref, second_ref)):
-        for i, side in enumerate(sides):
+        for i, side in enumerate(sides[::-1]):
             out_ref[:, i * RANK : (i + 1) * RANK] = side[4][part * half : (part + 1) * half]
 
 
@@ -135,8 +135,8 @@
     half = jax.ShapeDtypeStruct((tokens // 2, 2 * RANK), F32)
     scratch = []
     for source, factor, blocks in (
-        (train_inputs, proj_in, 2),
-        (train_grads, proj_out, 4),
+        (train_inputs, proj_in, 1),
+        (train_grads, proj_out, 2),
     ):
         scratch += [
             pltpu.VMEM(source.shape, BF16),
@@ -319,7 +319,7 @@
     bit = 1
     while bit < count:
         mine = summed(arrays)
-        group = [bit] if bit == 1 or 2 * bit == count else [3 * bit, 2 * bit, bit]
+        group = [bit] if bit == 1 or 2 * bit == count else [3 * bit, bit, 2 * bit]
         arrays = [mine] + [flipped(mine, count, flip) for flip in group]
         bit *= len(group) + 1
     return arrays
@@ -472,8 +472,8 @@
     )
     corner = [(i, i ^ 3) for i in range(2 * count)]
     return (
-        (keep + lax.ppermute(to_core, "tensor", swap))
-        + (flipped(to_chip, count, 1) + lax.ppermute(to_far, ("dp", "tensor"), corner))
+        (keep + lax.ppermute(to_far, ("dp", "tensor"), corner))
+        + (flipped(to_chip, count, 1) + lax.ppermute(to_core, "tensor", swap))
     )
 
 

time: 36.8 us -> 35.9 us (0.976)
  Pallas kernels: 12.2 us -> 11.2 us
    pallas_call x1, Pallas kernels: 6.59 us -> 5.58 us  [project(): pl.pallas_call(project_kernel, out_shape=(half, half), cost_estimate=cost...]
    ppermute x1, starting transfers between devices: 0.01 us -> 0.62 us  [local(): lax.ppermute(to_far, ('dp', 'tensor'), corner)]
    ppermute x1, starting transfers between devices: 0.61 us -> 0.01 us  [local(): lax.ppermute(to_core, 'tensor', swap)]
  transfers between devices with their start and end apart: 13 -> 13, of which waited for: 8 -> 7; matrix products, arithmetic and copies ran while one was open for 0% -> 0% of each run, Pallas kernels for 25% -> 23%
where the time goes in v7:
time: 35.9 us; the launch traced here: 35.7 us
  starting transfers between devices  15.3 us (43%)
  Pallas kernels  11.2 us (31%)
  waiting for transfers between devices  7.56 us (21%)
  local copies, waits for them, and re-layouts  0.95 us (3%)
  other arithmetic  0.58 us (2%)
    ppermute x9, starting transfers between devices, flipped(): return lax.ppermute(x, 'dp', [(i, i ^ flip) for i in range(count)])  14.1 us
    ppermute x9, waiting for transfers between devices, flipped(): return lax.ppermute(x, 'dp', [(i, i ^ flip) for i in range(count)])  5.71 us
    pallas_call x1, Pallas kernels, project(): pl.pallas_call(project_kernel, out_shape=(half, half), cost_estimate=cost...  5.58 us
    pallas_call x1, Pallas kernels, invert(): pl.pallas_call(functools.partial(invert_kernel, total), out_shape=(jax.Sh...  2.66 us
    pallas_call x1, Pallas kernels, score(): pl.pallas_call(functools.partial(score_kernel, held, count), out_shape=(s...  2.25 us
    unnamed x2, local copies, waits for them, and re-layouts  0.95 us
    ppermute x1, waiting for transfers between devices, local(): lax.ppermute(to_far, ('dp', 'tensor'), corner)  0.95 us
    ppermute x2, waiting for transfers between devices, local(): other = [lax.ppermute(part, 'tensor', swap) for part in mine]  0.9 us
  transfers between devices with their start and end apart: 13, of which 7 were waited for; matrix products, arithmetic and copies ran while one was open for 0% of the time, Pallas kernels for 23%

profile of v7, /device:TPU:0, one launch (start us, length us, event | category | flops | bytes accessed | tf_op | source)
XLA Modules:
  0.0 35.7 jit_solution(9203911608689785165)
XLA Ops:
  0.0 0.0 copy-start
  0.0 0.9 %copy-done = bf16[16,64,64]{2,1,0:T(8,128)(2,1)S(1)} copy-done((bf16[16,64,64]{2,1,0:T(8,128)(2,1)S(1)}, bf16[16,64,64]{2,1,0:T(8,128)(2,1)}, u32[]{:S(2)}) %copy-start) | copy-done | bytes 131096
  1.0 0.1 shard_map.55.after_ref.rest_2_
  1.1 3.1 %collective-permute-start.2 = (bf16[64,1024]{1,0:T(8,128)(2,1)S(1)}, bf16[64,1024]{1,0:T(8,128)(2,1)S(1)}, u32[]{:S(2)}, u32[]{:S(2)}) collective-permute-start(bf16[64,1024]{1,0:T(8,128)(2,1)S(1)} %shard_map.55.after_ref.rest_2_), channel_id=1, source_target_pairs={{0,4},{2,6},{4,0},{6,2},{8,12},{10,14},{12,8},{14,10},{1,5},{3,7},... | collective-permute-start | bytes 393224 | tf_op jit(solution)/shard_map/ppermute | solution.py:68
  4.2 2.6 %collective-permute-start.3 = (bf16[64,1024]{1,0:T(8,128)(2,1)S(1)}, bf16[64,1024]{1,0:T(8,128)(2,1)S(1)}, u32[]{:S(2)}, u32[]{:S(2)}) collective-permute-start(bf16[64,1024]{1,0:T(8,128)(2,1)S(1)} %shard_map.55.after_ref.rest_2_), channel_id=1, source_target_pairs={{0,8},{2,10},{4,12},{6,14},{8,0},{10,2},{12,4},{14,6},{1,9},{3,11}... | collective-permute-start | bytes 393224 | tf_op jit(solution)/shard_map/ppermute | solution.py:68
  6.8 5.6 %shard_map.56 = (f32[128,128]{1,0:T(8,128)S(1)}, f32[128,128]{1,0:T(8,128)S(1)}) custom-call(bf16[256,4096]{1,0:T(8,128)(2,1)} %x_ref.1, bf16[256,14336]{1,0:T(8,128)(2,1)} %g_ref.1, bf16[64,4096]{1,0:T(8,128)(2,1)} %bitcast.3, bf16[64,14336]{1,0:T(8,128)(2,1)} %bitcast.2, bf16[64,1024]{1,0:T(8,128)(2,1)S(1)} %shard_map.55.after_ref.rest_2_), custom_call_target="tpu_custom_call" | custom-call | bytes 29600000 | tf_op jit(solution)/shard_map/pallas_call | solution.py:147
  12.3 0.1 collective-permute-start
  12.4 0.5 %collective-permute-start.1 = (f32[128,128]{1,0:T(8,128)S(1)}, f32[128,128]{1,0:T(8,128)S(1)}, u32[]{:S(2)}, u32[]{:S(2)}) collective-permute-start(f32[128,128]{1,0:T(8,128)S(1)} %get-tuple-element.18.refs_1_), channel_id=1, source_target_pairs={{0,1},{1,0},{2,3},{3,2},{4,5},{5,4},{6,7},{7,6},{8,9},{9,8},{10,11... | collective-permute-start | bytes 196616 | tf_op jit(solution)/shard_map/ppermute | solution.py:462
  12.9 0.7 %collective-permute-done.refs_2_ = f32[128,128]{1,0:T(8,128)S(1)} collective-permute-done((f32[128,128]{1,0:T(8,128)S(1)}, f32[128,128]{1,0:T(8,128)S(1)}, u32[]{:S(2)}, u32[]{:S(2)}) %collective-permute-start) | collective-permute-done | bytes 65568 | tf_op jit(solution)/shard_map/ppermute | solution.py:462
  13.7 0.2 collective-permute-done.1.refs_3_
  13.8 0.0 collective-permute-done.2.refs_4_
  13.8 0.0 collective-permute-done.3.refs_5_
  13.8 0.6 %shard_map.57 = (f32[40,128]{1,0:T(8,128)S(1)}, bf16[64,256]{1,0:T(8,128)(2,1)S(1)}, bf16[64,1024]{1,0:T(8,128)(2,1)S(1)}, bf16[64,1024]{1,0:T(8,128)(2,1)S(1)}) custom-call(f32[128,128]{1,0:T(8,128)S(1)} %get-tuple-element.17.refs_0_, f32[128,128]{1,0:T(8,128)S(1)} %get-tuple-element.18.refs_1_, ...), custom_call_target="tpu_custom_call", output_to_operand_aliasing={{2}: (4, {}), {3}: (5, {})} | custom-call | bytes 3700000 | tf_op jit(solution)/shard_map/pallas_call | solution.py:195
  14.4 0.5 %collective-permute-start.9 = (bf16[64,1024]{1,0:T(8,128)(2,1)S(1)}, bf16[64,1024]{1,0:T(8,128)(2,1)S(1)}, u32[]{:S(2)}, u32[]{:S(2)}) collective-permute-start(bf16[64,1024]{1,0:T(8,128)(2,1)S(1)} %get-tuple-element.24.rest_4_), channel_id=1, source_target_pairs={{0,4},{2,6},{4,0},{6,2},{8,12},{10,14},{12,8},{14,10},{1,5},{3,7},... | collective-permute-start | bytes 393224 | tf_op jit(solution)/shard_map/ppermute | solution.py:68
  14.9 1.5 %collective-permute-start.4 = (f32[40,128]{1,0:T(8,128)S(1)}, f32[40,128]{1,0:T(8,128)S(1)}, u32[]{:S(2)}, u32[]{:S(2)}) collective-permute-start(f32[40,128]{1,0:T(8,128)S(1)} %get-tuple-element.19.refs_0_), channel_id=1, source_target_pairs={{0,2},{2,0},{4,6},{6,4},{8,10},{10,8},{12,14},{14,12},{1,3},{3,1},... | collective-permute-start | bytes 61448 | tf_op jit(solution)/shard_map/ppermute | solution.py:68
  16.4 0.5 %collective-permute-start.8 = (bf16[64,256]{1,0:T(8,128)(2,1)S(1)}, bf16[64,256]{1,0:T(8,128)(2,1)S(1)}, u32[]{:S(2)}, u32[]{:S(2)}) collective-permute-start(bf16[64,256]{1,0:T(8,128)(2,1)S(1)} %get-tuple-element.22.rest_0_), channel_id=1, source_target_pairs={{0,2},{2,0},{4,6},{6,4},{8,10},{10,8},{12,14},{14,12},{1,3},{3,1},... | collective-permute-start | bytes 98312 | tf_op jit(solution)/shard_map/ppermute | solution.py:68
  16.9 1.8 %collective-permute-done.4.refs_1_ = f32[40,128]{1,0:T(8,128)S(1)} collective-permute-done((f32[40,128]{1,0:T(8,128)S(1)}, f32[40,128]{1,0:T(8,128)S(1)}, u32[]{:S(2)}, u32[]{:S(2)}) %collective-permute-start.4) | collective-permute-done | bytes 20512 | tf_op jit(solution)/shard_map/ppermute | solution.py:68
  18.6 1.3 %collective-permute-start.5 = (f32[40,128]{1,0:T(8,128)S(1)}, f32[40,128]{1,0:T(8,128)S(1)}, u32[]{:S(2)}, u32[]{:S(2)}) collective-permute-start(f32[40,128]{1,0:T(8,128)S(1)} %shard_map.58.refs_0_), channel_id=1, source_target_pairs={{0,12},{2,14},{4,8},{6,10},{8,4},{10,6},{12,0},{14,2},{1,13},{3,15... | collective-permute-start | bytes 61448 | tf_op jit(solution)/shard_map/ppermute | solution.py:68
  20.0 0.9 %collective-permute-start.6 = (f32[40,128]{1,0:T(8,128)S(1)}, f32[40,128]{1,0:T(8,128)S(1)}, u32[]{:S(2)}, u32[]{:S(2)}) collective-permute-start(f32[40,128]{1,0:T(8,128)S(1)} %shard_map.58.refs_0_), channel_id=1, source_target_pairs={{0,4},{2,6},{4,0},{6,2},{8,12},{10,14},{12,8},{14,10},{1,5},{3,7},... | collective-permute-start | bytes 61448 | tf_op jit(solution)/shard_map/ppermute | solution.py:68
  20.9 2.2 %collective-permute-start.7 = (f32[40,128]{1,0:T(8,128)S(1)}, f32[40,128]{1,0:T(8,128)S(1)}, u32[]{:S(2)}, u32[]{:S(2)}) collective-permute-start(f32[40,128]{1,0:T(8,128)S(1)} %shard_map.58.refs_0_), channel_id=1, source_target_pairs={{0,8},{2,10},{4,12},{6,14},{8,0},{10,2},{12,4},{14,6},{1,9},{3,11}... | collective-permute-start | bytes 61448 | tf_op jit(solution)/shard_map/ppermute | solution.py:68
  23.0 1.2 %collective-permute-done.5.refs_1_ = f32[40,128]{1,0:T(8,128)S(1)} collective-permute-done((f32[40,128]{1,0:T(8,128)S(1)}, f32[40,128]{1,0:T(8,128)S(1)}, u32[]{:S(2)}, u32[]{:S(2)}) %collective-permute-start.5) | collective-permute-done | bytes 20512 | tf_op jit(solution)/shard_map/ppermute | solution.py:68
  24.2 0.0 collective-permute-done.6.refs_2_
  24.2 1.3 %collective-permute-done.7.refs_3_ = f32[40,128]{1,0:T(8,128)S(1)} collective-permute-done((f32[40,128]{1,0:T(8,128)S(1)}, f32[40,128]{1,0:T(8,128)S(1)}, u32[]{:S(2)}, u32[]{:S(2)}) %collective-permute-start.7) | collective-permute-done | bytes 20512 | tf_op jit(solution)/shard_map/ppermute | solution.py:68
  25.5 2.7 %shard_map.59 = (bf16[192,64]{1,0:T(8,128)(2,1)S(1)}, bf16[3,256,256]{2,1,0:T(8,128)(2,1)S(1)}) custom-call(f32[40,128]{1,0:T(8,128)S(1)} %shard_map.58.refs_0_, f32[40,128]{1,0:T(8,128)S(1)} %collective-permute-done.5.refs_1_, f32[40,128]{1,0:T(8,128)S(1)} %collective-permute-done.6.refs_2_, f32[40,128]{1,0:T(8,128)S(1)} %collective-permute-done.7.refs_3_), custom_call_target="tpu_custom_call" | custom-call | bytes 14800000 | tf_op jit(solution)/shard_map/pallas_call | solution.py:356
  28.2 0.0 collective-permute-done.8.rest_1_
  28.2 0.0 collective-permute-done.9.rest_5_
  28.2 2.2 %shard_map.60 = (f32[2,256]{1,0:T(2,128)S(1)}, f32[2,256]{1,0:T(2,128)S(1)}, f32[2,256]{1,0:T(2,128)S(1)}, f32[2,256]{1,0:T(2,128)S(1)}) custom-call(bf16[192,64]{1,0:T(8,128)(2,1)S(1)} %get-tuple-element.20.left_ref, bf16[3,256,256]{2,1,0:T(8,128)(2,1)S(1)} %get-tuple-element.21.weights, bf16[64,256]{1,0:T(8,128)(2,1)S(1)} %get-tuple-element.22.rest_0_, ...), custom_call_target="tpu_custom_call" | custom-call | bytes 14800000 | tf_op jit(solution)/shard_map/pallas_call | solution.py:441
  30.5 1.6 %collective-permute-start.11 = (f32[2,256]{1,0:T(2,128)S(1)}, f32[2,256]{1,0:T(2,128)S(1)}, u32[]{:S(2)}, u32[]{:S(2)}) collective-permute-start(f32[2,256]{1,0:T(2,128)S(1)} %get-tuple-element.27), channel_id=1, source_target_pairs={{0,2},{2,0},{4,6},{6,4},{8,10},{10,8},{12,14},{14,12},{1,3},{3,1},... | collective-permute-start | bytes 6152 | tf_op jit(solution)/shard_map/ppermute | solution.py:68
  32.1 0.0 collective-permute-start.12
  32.1 0.6 %collective-permute-start.10 = (f32[2,256]{1,0:T(2,128)S(1)}, f32[2,256]{1,0:T(2,128)S(1)}, u32[]{:S(2)}, u32[]{:S(2)}) collective-permute-start(f32[2,256]{1,0:T(2,128)S(1)} %get-tuple-element.26), channel_id=1, source_target_pairs={{0,3},{1,2},{2,1},{3,0},{4,7},{5,6},{6,5},{7,4},{8,11},{9,10},{10,... | collective-permute-start | bytes 6152 | tf_op jit(solution)/shard_map/ppermute | solution.py:475
  32.7 1.4 %collective-permute-done.11 = f32[2,256]{1,0:T(2,128)S(1)} collective-permute-done((f32[2,256]{1,0:T(2,128)S(1)}, f32[2,256]{1,0:T(2,128)S(1)}, u32[]{:S(2)}, u32[]{:S(2)}) %collective-permute-start.11) | collective-permute-done | bytes 2080 | tf_op jit(solution)/shard_map/ppermute | solution.py:68
  34.1 0.0 collective-permute-done.12
  34.1 0.9 %collective-permute-done.10 = f32[2,256]{1,0:T(2,128)S(1)} collective-permute-done((f32[2,256]{1,0:T(2,128)S(1)}, f32[2,256]{1,0:T(2,128)S(1)}, u32[]{:S(2)}, u32[]{:S(2)}) %collective-permute-start.10) | collective-permute-done | bytes 2080 | tf_op jit(solution)/shard_map/ppermute | solution.py:475
  35.1 0.6 %add_add_fusion = f32[2,256]{1,0:T(2,128)} fusion(f32[2,256]{1,0:T(2,128)S(1)} %collective-permute-done.11, f32[2,256]{1,0:T(2,128)S(1)} %collective-permute-done.12, f32[2,256]{1,0:T(2,128)S(1)} %get-tuple-element.25, f32[2,256]{1,0:T(2,128)S(1)} %collective-permute-done.10), kind=kLoop, calls=%fused_computation | loop fusion | flops 1536 | bytes 10240 | tf_op jit(solution)/shard_map/add | solution.py:475
  (1 shorter events, 0.0 us)
Async XLA Ops:
  0.0 0.9 %copy-start = (bf16[16,64,64]{2,1,0:T(8,128)(2,1)S(1)}, bf16[16,64,64]{2,1,0:T(8,128)(2,1)}, u32[]{:S(2)}) copy-start(bf16[16,64,64]{2,1,0:T(8,128)(2,1)} %q_ref.1) | copy-start | bytes 393220
  1.1 12.7 %collective-permute-start.2 = (bf16[64,1024]{1,0:T(8,128)(2,1)S(1)}, bf16[64,1024]{1,0:T(8,128)(2,1)S(1)}, u32[]{:S(2)}, u32[]{:S(2)}) collective-permute-start(bf16[64,1024]{1,0:T(8,128)(2,1)S(1)} %shard_map.55.after_ref.rest_2_), channel_id=1, source_target_pairs={{0,4},{2,6},{4,0},{6,2},{8,12},{10,14},{12,8},{14,10},{1,5},{3,7},... | collective-permute-start | bytes 393224 | tf_op jit(solution)/shard_map/ppermute | solution.py:68
  4.2 9.7 %collective-permute-start.3 = (bf16[64,1024]{1,0:T(8,128)(2,1)S(1)}, bf16[64,1024]{1,0:T(8,128)(2,1)S(1)}, u32[]{:S(2)}, u32[]{:S(2)}) collective-permute-start(bf16[64,1024]{1,0:T(8,128)(2,1)S(1)} %shard_map.55.after_ref.rest_2_), channel_id=1, source_target_pairs={{0,8},{2,10},{4,12},{6,14},{8,0},{10,2},{12,4},{14,6},{1,9},{3,11}... | collective-permute-start | bytes 393224 | tf_op jit(solution)/shard_map/ppermute | solution.py:68
  12.3 1.3 %collective-permute-start = (f32[128,128]{1,0:T(8,128)S(1)}, f32[128,128]{1,0:T(8,128)S(1)}, u32[]{:S(2)}, u32[]{:S(2)}) collective-permute-start(f32[128,128]{1,0:T(8,128)S(1)} %get-tuple-element.17.refs_0_), channel_id=1, source_target_pairs={{0,1},{1,0},{2,3},{3,2},{4,5},{5,4},{6,7},{7,6},{8,9},{9,8},{10,11... | collective-permute-start | bytes 196616 | tf_op jit(solution)/shard_map/ppermute | solution.py:462
  12.4 1.4 %collective-permute-start.1 = (f32[128,128]{1,0:T(8,128)S(1)}, f32[128,128]{1,0:T(8,128)S(1)}, u32[]{:S(2)}, u32[]{:S(2)}) collective-permute-start(f32[128,128]{1,0:T(8,128)S(1)} %get-tuple-element.18.refs_1_), channel_id=1, source_target_pairs={{0,1},{1,0},{2,3},{3,2},{4,5},{5,4},{6,7},{7,6},{8,9},{9,8},{10,11... | collective-permute-start | bytes 196616 | tf_op jit(solution)/shard_map/ppermute | solution.py:462
  14.4 13.8 %collective-permute-start.9 = (bf16[64,1024]{1,0:T(8,128)(2,1)S(1)}, bf16[64,1024]{1,0:T(8,128)(2,1)S(1)}, u32[]{:S(2)}, u32[]{:S(2)}) collective-permute-start(bf16[64,1024]{1,0:T(8,128)(2,1)S(1)} %get-tuple-element.24.rest_4_), channel_id=1, source_target_pairs={{0,4},{2,6},{4,0},{6,2},{8,12},{10,14},{12,8},{14,10},{1,5},{3,7},... | collective-permute-start | bytes 393224 | tf_op jit(solution)/shard_map/ppermute | solution.py:68
  14.9 3.8 %collective-permute-start.4 = (f32[40,128]{1,0:T(8,128)S(1)}, f32[40,128]{1,0:T(8,128)S(1)}, u32[]{:S(2)}, u32[]{:S(2)}) collective-permute-start(f32[40,128]{1,0:T(8,128)S(1)} %get-tuple-element.19.refs_0_), channel_id=1, source_target_pairs={{0,2},{2,0},{4,6},{6,4},{8,10},{10,8},{12,14},{14,12},{1,3},{3,1},... | collective-permute-start | bytes 61448 | tf_op jit(solution)/shard_map/ppermute | solution.py:68
  16.4 11.8 %collective-permute-start.8 = (bf16[64,256]{1,0:T(8,128)(2,1)S(1)}, bf16[64,256]{1,0:T(8,128)(2,1)S(1)}, u32[]{:S(2)}, u32[]{:S(2)}) collective-permute-start(bf16[64,256]{1,0:T(8,128)(2,1)S(1)} %get-tuple-element.22.rest_0_), channel_id=1, source_target_pairs={{0,2},{2,0},{4,6},{6,4},{8,10},{10,8},{12,14},{14,12},{1,3},{3,1},... | collective-permute-start | bytes 98312 | tf_op jit(solution)/shard_map/ppermute | solution.py:68
  18.6 5.6 %collective-permute-start.5 = (f32[40,128]{1,0:T(8,128)S(1)}, f32[40,128]{1,0:T(8,128)S(1)}, u32[]{:S(2)}, u32[]{:S(2)}) collective-permute-start(f32[40,128]{1,0:T(8,128)S(1)} %shard_map.58.refs_0_), channel_id=1, source_target_pairs={{0,12},{2,14},{4,8},{6,10},{8,4},{10,6},{12,0},{14,2},{1,13},{3,15... | collective-permute-start | bytes 61448 | tf_op jit(solution)/shard_map/ppermute | solution.py:68
  20.0 4.2 %collective-permute-start.6 = (f32[40,128]{1,0:T(8,128)S(1)}, f32[40,128]{1,0:T(8,128)S(1)}, u32[]{:S(2)}, u32[]{:S(2)}) collective-permute-start(f32[40,128]{1,0:T(8,128)S(1)} %shard_map.58.refs_0_), channel_id=1, source_target_pairs={{0,4},{2,6},{4,0},{6,2},{8,12},{10,14},{12,8},{14,10},{1,5},{3,7},... | collective-permute-start | bytes 61448 | tf_op jit(solution)/shard_map/ppermute | solution.py:68
  20.9 4.7 %collective-permute-start.7 = (f32[40,128]{1,0:T(8,128)S(1)}, f32[40,128]{1,0:T(8,128)S(1)}, u32[]{:S(2)}, u32[]{:S(2)}) collective-permute-start(f32[40,128]{1,0:T(8,128)S(1)} %shard_map.58.refs_0_), channel_id=1, source_target_pairs={{0,8},{2,10},{4,12},{6,14},{8,0},{10,2},{12,4},{14,6},{1,9},{3,11}... | collective-permute-start | bytes 61448 | tf_op jit(solution)/shard_map/ppermute | solution.py:68
  30.5 3.7 %collective-permute-start.11 = (f32[2,256]{1,0:T(2,128)S(1)}, f32[2,256]{1,0:T(2,128)S(1)}, u32[]{:S(2)}, u32[]{:S(2)}) collective-permute-start(f32[2,256]{1,0:T(2,128)S(1)} %get-tuple-element.27), channel_id=1, source_target_pairs={{0,2},{2,0},{4,6},{6,4},{8,10},{10,8},{12,14},{14,12},{1,3},{3,1},... | collective-permute-start | bytes 6152 | tf_op jit(solution)/shard_map/ppermute | solution.py:68
  32.1 2.1 %collective-permute-start.12 = (f32[2,256]{1,0:T(2,128)S(1)}, f32[2,256]{1,0:T(2,128)S(1)}, u32[]{:S(2)}, u32[]{:S(2)}) collective-permute-start(f32[2,256]{1,0:T(2,128)S(1)} %get-tuple-element.28), channel_id=1, source_target_pairs={{0,1},{1,0},{2,3},{3,2},{4,5},{5,4},{6,7},{7,6},{8,9},{9,8},{10,11... | collective-permute-start | bytes 6152 | tf_op jit(solution)/shard_map/ppermute | solution.py:476
  32.1 3.0 %collective-permute-start.10 = (f32[2,256]{1,0:T(2,128)S(1)}, f32[2,256]{1,0:T(2,128)S(1)}, u32[]{:S(2)}, u32[]{:S(2)}) collective-permute-start(f32[2,256]{1,0:T(2,128)S(1)} %get-tuple-element.26), channel_id=1, source_target_pairs={{0,3},{1,2},{2,1},{3,0},{4,7},{5,6},{6,5},{7,4},{8,11},{9,10},{10,... | collective-permute-start | bytes 6152 | tf_op jit(solution)/shard_map/ppermute | solution.py:475

commit v8 on v7

--- a/solution.py
+++ b/solution.py
@@ -70,7 +70,7 @@
 
 def first_from_peers(mine, count):
     known = {0: mine}
-    for bit in sorted(flips(count))[1:]:
+    for bit in sorted(flips(count))[:0:-1]:
         if bit & (bit - 1) == 0 and bit * 8 > count:
             known[bit] = flipped(mine, count, bit)
     return known
@@ -315,13 +315,14 @@
 
 
 def over_peers(mine, count):
+    groups, bit = [], 1
+    while bit < count:
+        groups.append([bit] if bit == 1 or 2 * bit == count else [3 * bit, bit, 2 * bit])
+        bit *= len(groups[-1]) + 1
     arrays = [mine]
-    bit = 1
-    while bit < count:
+    for group in reversed(groups):
         mine = summed(arrays)
-        group = [bit] if bit == 1 or 2 * bit == count else [3 * bit, bit, 2 * bit]
         arrays = [mine] + [flipped(mine, count, flip) for flip in group]
-        bit *= len(group) + 1
     return arrays
 
 
@@ -460,7 +461,7 @@
     known = first_from_peers(spread_queries, count)
     mine = project(train_inputs, train_grads, proj_in, proj_out, spread_queries)
     other = [lax.ppermute(part, "tensor", swap) for part in mine]
-    early = sorted(set(known) - {0})
+    early = sorted(set(known) - {0}, reverse=True)
     cov, grads, *arrived = grams(mine, other, [known[m] for m in early])
     known.update(zip(early, arrived))
     gathered = all_from_peers(known, count)

time: 35.9 us -> 35.6 us (level)
  waiting for transfers between devices: 7.56 us -> 6.28 us
  starting transfers between devices: 15.3 us -> 16.4 us
    ppermute x9, waiting for transfers between devices: 5.71 us -> 4.43 us  [flipped(): return lax.ppermute(x, 'dp', [(i, i ^ flip) for i in range(count)])]
    ppermute x9, starting transfers between devices: 14.1 us -> 15.2 us  [flipped(): return lax.ppermute(x, 'dp', [(i, i ^ flip) for i in range(count)])]
where the time goes in v8:
time: 35.6 us; the launch traced here: 35.5 us
  starting transfers between devices  16.4 us (46%)
  Pallas kernels  11.2 us (31%)
  waiting for transfers between devices  6.28 us (18%)
  local copies, waits for them, and re-layouts  0.95 us (3%)
  other arithmetic  0.58 us (2%)
    ppermute x9, starting transfers between devices, flipped(): return lax.ppermute(x, 'dp', [(i, i ^ flip) for i in range(count)])  15.2 us
    pallas_call x1, Pallas kernels, project(): pl.pallas_call(project_kernel, out_shape=(half, half), cost_estimate=cost...  5.58 us
    ppermute x9, waiting for transfers between devices, flipped(): return lax.ppermute(x, 'dp', [(i, i ^ flip) for i in range(count)])  4.43 us
    pallas_call x1, Pallas kernels, invert(): pl.pallas_call(functools.partial(invert_kernel, total), out_shape=(jax.Sh...  2.66 us
    pallas_call x1, Pallas kernels, score(): pl.pallas_call(functools.partial(score_kernel, held, count), out_shape=(s...  2.24 us
    unnamed x2, local copies, waits for them, and re-layouts  0.95 us
    ppermute x1, waiting for transfers between devices, local(): lax.ppermute(to_far, ('dp', 'tensor'), corner)  0.95 us
    ppermute x2, waiting for transfers between devices, local(): other = [lax.ppermute(part, 'tensor', swap) for part in mine]  0.9 us
  transfers between devices with their start and end apart: 13, of which 7 were waited for; matrix products, arithmetic and copies ran while one was open for 0% of the time, Pallas kernels for 23%

profile of v8, /device:TPU:0, one launch (start us, length us, event | category | flops | bytes accessed | tf_op | source)
XLA Modules:
  0.0 35.5 jit_solution(8875311713203833706)
XLA Ops:
  0.0 0.0 copy-start
  0.0 0.9 %copy-done = bf16[16,64,64]{2,1,0:T(8,128)(2,1)S(1)} copy-done((bf16[16,64,64]{2,1,0:T(8,128)(2,1)S(1)}, bf16[16,64,64]{2,1,0:T(8,128)(2,1)}, u32[]{:S(2)}) %copy-start) | copy-done | bytes 131096
  1.0 0.1 shard_map.55.after_ref.rest_2_
  1.1 4.1 %collective-permute-start.2 = (bf16[64,1024]{1,0:T(8,128)(2,1)S(1)}, bf16[64,1024]{1,0:T(8,128)(2,1)S(1)}, u32[]{:S(2)}, u32[]{:S(2)}) collective-permute-start(bf16[64,1024]{1,0:T(8,128)(2,1)S(1)} %shard_map.55.after_ref.rest_2_), channel_id=1, source_target_pairs={{0,8},{2,10},{4,12},{6,14},{8,0},{10,2},{12,4},{14,6},{1,9},{3,11}... | collective-permute-start | bytes 393224 | tf_op jit(solution)/shard_map/ppermute | solution.py:68
  5.2 1.6 %collective-permute-start.3 = (bf16[64,1024]{1,0:T(8,128)(2,1)S(1)}, bf16[64,1024]{1,0:T(8,128)(2,1)S(1)}, u32[]{:S(2)}, u32[]{:S(2)}) collective-permute-start(bf16[64,1024]{1,0:T(8,128)(2,1)S(1)} %shard_map.55.after_ref.rest_2_), channel_id=1, source_target_pairs={{0,4},{2,6},{4,0},{6,2},{8,12},{10,14},{12,8},{14,10},{1,5},{3,7},... | collective-permute-start | bytes 393224 | tf_op jit(solution)/shard_map/ppermute | solution.py:68
  6.8 5.6 %shard_map.56 = (f32[128,128]{1,0:T(8,128)S(1)}, f32[128,128]{1,0:T(8,128)S(1)}) custom-call(bf16[256,4096]{1,0:T(8,128)(2,1)} %x_ref.1, bf16[256,14336]{1,0:T(8,128)(2,1)} %g_ref.1, bf16[64,4096]{1,0:T(8,128)(2,1)} %bitcast.3, bf16[64,14336]{1,0:T(8,128)(2,1)} %bitcast.2, bf16[64,1024]{1,0:T(8,128)(2,1)S(1)} %shard_map.55.after_ref.rest_2_), custom_call_target="tpu_custom_call" | custom-call | bytes 29600000 | tf_op jit(solution)/shard_map/pallas_call | solution.py:147
  12.3 0.1 collective-permute-start
  12.4 0.5 %collective-permute-start.1 = (f32[128,128]{1,0:T(8,128)S(1)}, f32[128,128]{1,0:T(8,128)S(1)}, u32[]{:S(2)}, u32[]{:S(2)}) collective-permute-start(f32[128,128]{1,0:T(8,128)S(1)} %get-tuple-element.18.refs_1_), channel_id=1, source_target_pairs={{0,1},{1,0},{2,3},{3,2},{4,5},{5,4},{6,7},{7,6},{8,9},{9,8},{10,11... | collective-permute-start | bytes 196616 | tf_op jit(solution)/shard_map/ppermute | solution.py:463
  12.9 0.7 %collective-permute-done.refs_2_ = f32[128,128]{1,0:T(8,128)S(1)} collective-permute-done((f32[128,128]{1,0:T(8,128)S(1)}, f32[128,128]{1,0:T(8,128)S(1)}, u32[]{:S(2)}, u32[]{:S(2)}) %collective-permute-start) | collective-permute-done | bytes 65568 | tf_op jit(solution)/shard_map/ppermute | solution.py:463
  13.7 0.2 collective-permute-done.1.refs_3_
  13.8 0.0 collective-permute-done.2.refs_4_
  13.8 0.0 collective-permute-done.3.refs_5_
  13.8 0.6 %shard_map.57 = (f32[40,128]{1,0:T(8,128)S(1)}, bf16[64,256]{1,0:T(8,128)(2,1)S(1)}, bf16[64,1024]{1,0:T(8,128)(2,1)S(1)}, bf16[64,1024]{1,0:T(8,128)(2,1)S(1)}) custom-call(f32[128,128]{1,0:T(8,128)S(1)} %get-tuple-element.17.refs_0_, f32[128,128]{1,0:T(8,128)S(1)} %get-tuple-element.18.refs_1_, ...), custom_call_target="tpu_custom_call", output_to_operand_aliasing={{2}: (4, {}), {3}: (5, {})} | custom-call | bytes 3700000 | tf_op jit(solution)/shard_map/pallas_call | solution.py:195
  14.4 0.5 %collective-permute-start.9 = (bf16[64,1024]{1,0:T(8,128)(2,1)S(1)}, bf16[64,1024]{1,0:T(8,128)(2,1)S(1)}, u32[]{:S(2)}, u32[]{:S(2)}) collective-permute-start(bf16[64,1024]{1,0:T(8,128)(2,1)S(1)} %get-tuple-element.24.rest_4_), channel_id=1, source_target_pairs={{0,4},{2,6},{4,0},{6,2},{8,12},{10,14},{12,8},{14,10},{1,5},{3,7},... | collective-permute-start | bytes 393224 | tf_op jit(solution)/shard_map/ppermute | solution.py:68
  14.9 1.3 %collective-permute-start.4 = (f32[40,128]{1,0:T(8,128)S(1)}, f32[40,128]{1,0:T(8,128)S(1)}, u32[]{:S(2)}, u32[]{:S(2)}) collective-permute-start(f32[40,128]{1,0:T(8,128)S(1)} %get-tuple-element.19.refs_0_), channel_id=1, source_target_pairs={{0,12},{2,14},{4,8},{6,10},{8,4},{10,6},{12,0},{14,2},{1,13},{3,15... | collective-permute-start | bytes 61448 | tf_op jit(solution)/shard_map/ppermute | solution.py:68
  16.2 0.5 %collective-permute-start.5 = (f32[40,128]{1,0:T(8,128)S(1)}, f32[40,128]{1,0:T(8,128)S(1)}, u32[]{:S(2)}, u32[]{:S(2)}) collective-permute-start(f32[40,128]{1,0:T(8,128)S(1)} %get-tuple-element.19.refs_0_), channel_id=1, source_target_pairs={{0,4},{2,6},{4,0},{6,2},{8,12},{10,14},{12,8},{14,10},{1,5},{3,7},... | collective-permute-start | bytes 61448 | tf_op jit(solution)/shard_map/ppermute | solution.py:68
  16.7 2.5 %collective-permute-start.6 = (f32[40,128]{1,0:T(8,128)S(1)}, f32[40,128]{1,0:T(8,128)S(1)}, u32[]{:S(2)}, u32[]{:S(2)}) collective-permute-start(f32[40,128]{1,0:T(8,128)S(1)} %get-tuple-element.19.refs_0_), channel_id=1, source_target_pairs={{0,8},{2,10},{4,12},{6,14},{8,0},{10,2},{12,4},{14,6},{1,9},{3,11}... | collective-permute-start | bytes 61448 | tf_op jit(solution)/shard_map/ppermute | solution.py:68
  19.2 1.5 %collective-permute-start.8 = (bf16[64,256]{1,0:T(8,128)(2,1)S(1)}, bf16[64,256]{1,0:T(8,128)(2,1)S(1)}, u32[]{:S(2)}, u32[]{:S(2)}) collective-permute-start(bf16[64,256]{1,0:T(8,128)(2,1)S(1)} %get-tuple-element.22.rest_0_), channel_id=1, source_target_pairs={{0,2},{2,0},{4,6},{6,4},{8,10},{10,8},{12,14},{14,12},{1,3},{3,1},... | collective-permute-start | bytes 98312 | tf_op jit(solution)/shard_map/ppermute | solution.py:68
  20.8 0.0 collective-permute-done.4.refs_1_
  20.8 0.5 %collective-permute-done.5.refs_2_ = f32[40,128]{1,0:T(8,128)S(1)} collective-permute-done((f32[40,128]{1,0:T(8,128)S(1)}, f32[40,128]{1,0:T(8,128)S(1)}, u32[]{:S(2)}, u32[]{:S(2)}) %collective-permute-start.5) | collective-permute-done | bytes 20512 | tf_op jit(solution)/shard_map/ppermute | solution.py:68
  21.3 0.2 collective-permute-done.6.refs_3_
  21.5 1.6 %collective-permute-start.7 = (f32[40,128]{1,0:T(8,128)S(1)}, f32[40,128]{1,0:T(8,128)S(1)}, u32[]{:S(2)}, u32[]{:S(2)}) collective-permute-start(f32[40,128]{1,0:T(8,128)S(1)} %shard_map.58.refs_0_), channel_id=1, source_target_pairs={{0,2},{2,0},{4,6},{6,4},{8,10},{10,8},{12,14},{14,12},{1,3},{3,1},... | collective-permute-start | bytes 61448 | tf_op jit(solution)/shard_map/ppermute | solution.py:68
  23.1 2.3 %collective-permute-done.7.refs_1_ = f32[40,128]{1,0:T(8,128)S(1)} collective-permute-done((f32[40,128]{1,0:T(8,128)S(1)}, f32[40,128]{1,0:T(8,128)S(1)}, u32[]{:S(2)}, u32[]{:S(2)}) %collective-permute-start.7) | collective-permute-done | bytes 20512 | tf_op jit(solution)/shard_map/ppermute | solution.py:68
  25.3 2.7 %shard_map.59 = (bf16[192,64]{1,0:T(8,128)(2,1)S(1)}, bf16[3,256,256]{2,1,0:T(8,128)(2,1)S(1)}) custom-call(f32[40,128]{1,0:T(8,128)S(1)} %shard_map.58.refs_0_, f32[40,128]{1,0:T(8,128)S(1)} %collective-permute-done.7.refs_1_), custom_call_target="tpu_custom_call" | custom-call | bytes 14800000 | tf_op jit(solution)/shard_map/pallas_call | solution.py:357
  28.0 0.0 collective-permute-done.8.rest_1_
  28.0 0.0 collective-permute-done.9.rest_5_
  28.0 2.2 %shard_map.60 = (f32[2,256]{1,0:T(2,128)S(1)}, f32[2,256]{1,0:T(2,128)S(1)}, f32[2,256]{1,0:T(2,128)S(1)}, f32[2,256]{1,0:T(2,128)S(1)}) custom-call(bf16[192,64]{1,0:T(8,128)(2,1)S(1)} %get-tuple-element.20.left_ref, bf16[3,256,256]{2,1,0:T(8,128)(2,1)S(1)} %get-tuple-element.21.weights, bf16[64,256]{1,0:T(8,128)(2,1)S(1)} %get-tuple-element.22.rest_0_, ...), custom_call_target="tpu_custom_call" | custom-call | bytes 14800000 | tf_op jit(solution)/shard_map/pallas_call | solution.py:442
  30.3 1.6 %collective-permute-start.11 = (f32[2,256]{1,0:T(2,128)S(1)}, f32[2,256]{1,0:T(2,128)S(1)}, u32[]{:S(2)}, u32[]{:S(2)}) collective-permute-start(f32[2,256]{1,0:T(2,128)S(1)} %get-tuple-element.27), channel_id=1, source_target_pairs={{0,2},{2,0},{4,6},{6,4},{8,10},{10,8},{12,14},{14,12},{1,3},{3,1},... | collective-permute-start | bytes 6152 | tf_op jit(solution)/shard_map/ppermute | solution.py:68
  31.9 0.0 collective-permute-start.12
  31.9 0.6 %collective-permute-start.10 = (f32[2,256]{1,0:T(2,128)S(1)}, f32[2,256]{1,0:T(2,128)S(1)}, u32[]{:S(2)}, u32[]{:S(2)}) collective-permute-start(f32[2,256]{1,0:T(2,128)S(1)} %get-tuple-element.26), channel_id=1, source_target_pairs={{0,3},{1,2},{2,1},{3,0},{4,7},{5,6},{6,5},{7,4},{8,11},{9,10},{10,... | collective-permute-start | bytes 6152 | tf_op jit(solution)/shard_map/ppermute | solution.py:476
  32.5 1.4 %collective-permute-done.11 = f32[2,256]{1,0:T(2,128)S(1)} collective-permute-done((f32[2,256]{1,0:T(2,128)S(1)}, f32[2,256]{1,0:T(2,128)S(1)}, u32[]{:S(2)}, u32[]{:S(2)}) %collective-permute-start.11) | collective-permute-done | bytes 2080 | tf_op jit(solution)/shard_map/ppermute | solution.py:68
  33.9 0.0 collective-permute-done.12
  33.9 0.9 %collective-permute-done.10 = f32[2,256]{1,0:T(2,128)S(1)} collective-permute-done((f32[2,256]{1,0:T(2,128)S(1)}, f32[2,256]{1,0:T(2,128)S(1)}, u32[]{:S(2)}, u32[]{:S(2)}) %collective-permute-start.10) | collective-permute-done | bytes 2080 | tf_op jit(solution)/shard_map/ppermute | solution.py:476
  34.9 0.6 %add_add_fusion = f32[2,256]{1,0:T(2,128)} fusion(f32[2,256]{1,0:T(2,128)S(1)} %collective-permute-done.11, f32[2,256]{1,0:T(2,128)S(1)} %collective-permute-done.12, f32[2,256]{1,0:T(2,128)S(1)} %get-tuple-element.25, f32[2,256]{1,0:T(2,128)S(1)} %collective-permute-done.10), kind=kLoop, calls=%fused_computation | loop fusion | flops 1536 | bytes 10240 | tf_op jit(solution)/shard_map/add | solution.py:476
  (1 shorter events, 0.0 us)
Async XLA Ops:
  0.0 0.9 %copy-start = (bf16[16,64,64]{2,1,0:T(8,128)(2,1)S(1)}, bf16[16,64,64]{2,1,0:T(8,128)(2,1)}, u32[]{:S(2)}) copy-start(bf16[16,64,64]{2,1,0:T(8,128)(2,1)} %q_ref.1) | copy-start | bytes 393220
  1.1 12.7 %collective-permute-start.2 = (bf16[64,1024]{1,0:T(8,128)(2,1)S(1)}, bf16[64,1024]{1,0:T(8,128)(2,1)S(1)}, u32[]{:S(2)}, u32[]{:S(2)}) collective-permute-start(bf16[64,1024]{1,0:T(8,128)(2,1)S(1)} %shard_map.55.after_ref.rest_2_), channel_id=1, source_target_pairs={{0,8},{2,10},{4,12},{6,14},{8,0},{10,2},{12,4},{14,6},{1,9},{3,11}... | collective-permute-start | bytes 393224 | tf_op jit(solution)/shard_map/ppermute | solution.py:68
  5.2 8.6 %collective-permute-start.3 = (bf16[64,1024]{1,0:T(8,128)(2,1)S(1)}, bf16[64,1024]{1,0:T(8,128)(2,1)S(1)}, u32[]{:S(2)}, u32[]{:S(2)}) collective-permute-start(bf16[64,1024]{1,0:T(8,128)(2,1)S(1)} %shard_map.55.after_ref.rest_2_), channel_id=1, source_target_pairs={{0,4},{2,6},{4,0},{6,2},{8,12},{10,14},{12,8},{14,10},{1,5},{3,7},... | collective-permute-start | bytes 393224 | tf_op jit(solution)/shard_map/ppermute | solution.py:68
  12.3 1.3 %collective-permute-start = (f32[128,128]{1,0:T(8,128)S(1)}, f32[128,128]{1,0:T(8,128)S(1)}, u32[]{:S(2)}, u32[]{:S(2)}) collective-permute-start(f32[128,128]{1,0:T(8,128)S(1)} %get-tuple-element.17.refs_0_), channel_id=1, source_target_pairs={{0,1},{1,0},{2,3},{3,2},{4,5},{5,4},{6,7},{7,6},{8,9},{9,8},{10,11... | collective-permute-start | bytes 196616 | tf_op jit(solution)/shard_map/ppermute | solution.py:463
  12.4 1.4 %collective-permute-start.1 = (f32[128,128]{1,0:T(8,128)S(1)}, f32[128,128]{1,0:T(8,128)S(1)}, u32[]{:S(2)}, u32[]{:S(2)}) collective-permute-start(f32[128,128]{1,0:T(8,128)S(1)} %get-tuple-element.18.refs_1_), channel_id=1, source_target_pairs={{0,1},{1,0},{2,3},{3,2},{4,5},{5,4},{6,7},{7,6},{8,9},{9,8},{10,11... | collective-permute-start | bytes 196616 | tf_op jit(solution)/shard_map/ppermute | solution.py:463
  14.4 13.6 %collective-permute-start.9 = (bf16[64,1024]{1,0:T(8,128)(2,1)S(1)}, bf16[64,1024]{1,0:T(8,128)(2,1)S(1)}, u32[]{:S(2)}, u32[]{:S(2)}) collective-permute-start(bf16[64,1024]{1,0:T(8,128)(2,1)S(1)} %get-tuple-element.24.rest_4_), channel_id=1, source_target_pairs={{0,4},{2,6},{4,0},{6,2},{8,12},{10,14},{12,8},{14,10},{1,5},{3,7},... | collective-permute-start | bytes 393224 | tf_op jit(solution)/shard_map/ppermute | solution.py:68
  14.9 5.9 %collective-permute-start.4 = (f32[40,128]{1,0:T(8,128)S(1)}, f32[40,128]{1,0:T(8,128)S(1)}, u32[]{:S(2)}, u32[]{:S(2)}) collective-permute-start(f32[40,128]{1,0:T(8,128)S(1)} %get-tuple-element.19.refs_0_), channel_id=1, source_target_pairs={{0,12},{2,14},{4,8},{6,10},{8,4},{10,6},{12,0},{14,2},{1,13},{3,15... | collective-permute-start | bytes 61448 | tf_op jit(solution)/shard_map/ppermute | solution.py:68
  16.2 5.1 %collective-permute-start.5 = (f32[40,128]{1,0:T(8,128)S(1)}, f32[40,128]{1,0:T(8,128)S(1)}, u32[]{:S(2)}, u32[]{:S(2)}) collective-permute-start(f32[40,128]{1,0:T(8,128)S(1)} %get-tuple-element.19.refs_0_), channel_id=1, source_target_pairs={{0,4},{2,6},{4,0},{6,2},{8,12},{10,14},{12,8},{14,10},{1,5},{3,7},... | collective-permute-start | bytes 61448 | tf_op jit(solution)/shard_map/ppermute | solution.py:68
  16.7 4.7 %collective-permute-start.6 = (f32[40,128]{1,0:T(8,128)S(1)}, f32[40,128]{1,0:T(8,128)S(1)}, u32[]{:S(2)}, u32[]{:S(2)}) collective-permute-start(f32[40,128]{1,0:T(8,128)S(1)} %get-tuple-element.19.refs_0_), channel_id=1, source_target_pairs={{0,8},{2,10},{4,12},{6,14},{8,0},{10,2},{12,4},{14,6},{1,9},{3,11}... | collective-permute-start | bytes 61448 | tf_op jit(solution)/shard_map/ppermute | solution.py:68
  19.2 8.8 %collective-permute-start.8 = (bf16[64,256]{1,0:T(8,128)(2,1)S(1)}, bf16[64,256]{1,0:T(8,128)(2,1)S(1)}, u32[]{:S(2)}, u32[]{:S(2)}) collective-permute-start(bf16[64,256]{1,0:T(8,128)(2,1)S(1)} %get-tuple-element.22.rest_0_), channel_id=1, source_target_pairs={{0,2},{2,0},{4,6},{6,4},{8,10},{10,8},{12,14},{14,12},{1,3},{3,1},... | collective-permute-start | bytes 98312 | tf_op jit(solution)/shard_map/ppermute | solution.py:68
  21.5 3.8 %collective-permute-start.7 = (f32[40,128]{1,0:T(8,128)S(1)}, f32[40,128]{1,0:T(8,128)S(1)}, u32[]{:S(2)}, u32[]{:S(2)}) collective-permute-start(f32[40,128]{1,0:T(8,128)S(1)} %shard_map.58.refs_0_), channel_id=1, source_target_pairs={{0,2},{2,0},{4,6},{6,4},{8,10},{10,8},{12,14},{14,12},{1,3},{3,1},... | collective-permute-start | bytes 61448 | tf_op jit(solution)/shard_map/ppermute | solution.py:68
  30.3 3.7 %collective-permute-start.11 = (f32[2,256]{1,0:T(2,128)S(1)}, f32[2,256]{1,0:T(2,128)S(1)}, u32[]{:S(2)}, u32[]{:S(2)}) collective-permute-start(f32[2,256]{1,0:T(2,128)S(1)} %get-tuple-element.27), channel_id=1, source_target_pairs={{0,2},{2,0},{4,6},{6,4},{8,10},{10,8},{12,14},{14,12},{1,3},{3,1},... | collective-permute-start | bytes 6152 | tf_op jit(solution)/shard_map/ppermute | solution.py:68
  31.9 2.1 %collective-permute-start.12 = (f32[2,256]{1,0:T(2,128)S(1)}, f32[2,256]{1,0:T(2,128)S(1)}, u32[]{:S(2)}, u32[]{:S(2)}) collective-permute-start(f32[2,256]{1,0:T(2,128)S(1)} %get-tuple-element.28), channel_id=1, source_target_pairs={{0,1},{1,0},{2,3},{3,2},{4,5},{5,4},{6,7},{7,6},{8,9},{9,8},{10,11... | collective-permute-start | bytes 6152 | tf_op jit(solution)/shard_map/ppermute | solution.py:477
  31.9 3.0 %collective-permute-start.10 = (f32[2,256]{1,0:T(2,128)S(1)}, f32[2,256]{1,0:T(2,128)S(1)}, u32[]{:S(2)}, u32[]{:S(2)}) collective-permute-start(f32[2,256]{1,0:T(2,128)S(1)} %get-tuple-element.26), channel_id=1, source_target_pairs={{0,3},{1,2},{2,1},{3,0},{4,7},{5,6},{6,5},{7,4},{8,11},{9,10},{10,... | collective-permute-start | bytes 6152 | tf_op jit(solution)/shard_map/ppermute | solution.py:476

commit v9 on v7

--- a/solution.py
+++ b/solution.py
@@ -70,7 +70,7 @@
 
 def first_from_peers(mine, count):
     known = {0: mine}
-    for bit in sorted(flips(count))[1:]:
+    for bit in sorted(flips(count))[:0:-1]:
         if bit & (bit - 1) == 0 and bit * 8 > count:
             known[bit] = flipped(mine, count, bit)
     return known
@@ -460,7 +460,7 @@
     known = first_from_peers(spread_queries, count)
     mine = project(train_inputs, train_grads, proj_in, proj_out, spread_queries)
     other = [lax.ppermute(part, "tensor", swap) for part in mine]
-    early = sorted(set(known) - {0})
+    early = sorted(set(known) - {0}, reverse=True)
     cov, grads, *arrived = grams(mine, other, [known[m] for m in early])
     known.update(zip(early, arrived))
     gathered = all_from_peers(known, count)

time: 35.9 us -> 35.5 us (0.989)
  no operation moved by 1% of the time
where the time goes in v9:
time: 35.5 us; the launch traced here: 35.3 us
  starting transfers between devices  15.3 us (43%)
  Pallas kernels  11.2 us (32%)
  waiting for transfers between devices  7.22 us (20%)
  local copies, waits for them, and re-layouts  0.95 us (3%)
  other arithmetic  0.58 us (2%)
    ppermute x9, starting transfers between devices, flipped(): return lax.ppermute(x, 'dp', [(i, i ^ flip) for i in range(count)])  13.9 us
    ppermute x9, waiting for transfers between devices, flipped(): return lax.ppermute(x, 'dp', [(i, i ^ flip) for i in range(count)])  5.6 us
    pallas_call x1, Pallas kernels, project(): pl.pallas_call(project_kernel, out_shape=(half, half), cost_estimate=cost...  5.58 us
    pallas_call x1, Pallas kernels, invert(): pl.pallas_call(functools.partial(invert_kernel, total), out_shape=(jax.Sh...  2.66 us
    pallas_call x1, Pallas kernels, score(): pl.pallas_call(functools.partial(score_kernel, held, count), out_shape=(s...  2.25 us
    unnamed x2, local copies, waits for them, and re-layouts  0.95 us
    ppermute x2, waiting for transfers between devices, local(): other = [lax.ppermute(part, 'tensor', swap) for part in mine]  0.9 us
    ppermute x1, starting transfers between devices, local(): lax.ppermute(to_far, ('dp', 'tensor'), corner)  0.84 us
  transfers between devices with their start and end apart: 13, of which 7 were waited for; matrix products, arithmetic and copies ran while one was open for 0% of the time, Pallas kernels for 23%

profile of v9, /device:TPU:0, one launch (start us, length us, event | category | flops | bytes accessed | tf_op | source)
XLA Modules:
  0.0 35.3 jit_solution(7958420869623274716)
XLA Ops:
  0.0 0.0 copy-start
  0.0 0.9 %copy-done = bf16[16,64,64]{2,1,0:T(8,128)(2,1)S(1)} copy-done((bf16[16,64,64]{2,1,0:T(8,128)(2,1)S(1)}, bf16[16,64,64]{2,1,0:T(8,128)(2,1)}, u32[]{:S(2)}) %copy-start) | copy-done | bytes 131096
  1.0 0.1 shard_map.55.after_ref.rest_2_
  1.1 4.1 %collective-permute-start.2 = (bf16[64,1024]{1,0:T(8,128)(2,1)S(1)}, bf16[64,1024]{1,0:T(8,128)(2,1)S(1)}, u32[]{:S(2)}, u32[]{:S(2)}) collective-permute-start(bf16[64,1024]{1,0:T(8,128)(2,1)S(1)} %shard_map.55.after_ref.rest_2_), channel_id=1, source_target_pairs={{0,8},{2,10},{4,12},{6,14},{8,0},{10,2},{12,4},{14,6},{1,9},{3,11}... | collective-permute-start | bytes 393224 | tf_op jit(solution)/shard_map/ppermute | solution.py:68
  5.2 1.6 %collective-permute-start.3 = (bf16[64,1024]{1,0:T(8,128)(2,1)S(1)}, bf16[64,1024]{1,0:T(8,128)(2,1)S(1)}, u32[]{:S(2)}, u32[]{:S(2)}) collective-permute-start(bf16[64,1024]{1,0:T(8,128)(2,1)S(1)} %shard_map.55.after_ref.rest_2_), channel_id=1, source_target_pairs={{0,4},{2,6},{4,0},{6,2},{8,12},{10,14},{12,8},{14,10},{1,5},{3,7},... | collective-permute-start | bytes 393224 | tf_op jit(solution)/shard_map/ppermute | solution.py:68
  6.8 5.6 %shard_map.56 = (f32[128,128]{1,0:T(8,128)S(1)}, f32[128,128]{1,0:T(8,128)S(1)}) custom-call(bf16[256,4096]{1,0:T(8,128)(2,1)} %x_ref.1, bf16[256,14336]{1,0:T(8,128)(2,1)} %g_ref.1, bf16[64,4096]{1,0:T(8,128)(2,1)} %bitcast.3, bf16[64,14336]{1,0:T(8,128)(2,1)} %bitcast.2, bf16[64,1024]{1,0:T(8,128)(2,1)S(1)} %shard_map.55.after_ref.rest_2_), custom_call_target="tpu_custom_call" | custom-call | bytes 29600000 | tf_op jit(solution)/shard_map/pallas_call | solution.py:147
  12.3 0.1 collective-permute-start
  12.4 0.5 %collective-permute-start.1 = (f32[128,128]{1,0:T(8,128)S(1)}, f32[128,128]{1,0:T(8,128)S(1)}, u32[]{:S(2)}, u32[]{:S(2)}) collective-permute-start(f32[128,128]{1,0:T(8,128)S(1)} %get-tuple-element.18.refs_1_), channel_id=1, source_target_pairs={{0,1},{1,0},{2,3},{3,2},{4,5},{5,4},{6,7},{7,6},{8,9},{9,8},{10,11... | collective-permute-start | bytes 196616 | tf_op jit(solution)/shard_map/ppermute | solution.py:462
  12.9 0.7 %collective-permute-done.refs_2_ = f32[128,128]{1,0:T(8,128)S(1)} collective-permute-done((f32[128,128]{1,0:T(8,128)S(1)}, f32[128,128]{1,0:T(8,128)S(1)}, u32[]{:S(2)}, u32[]{:S(2)}) %collective-permute-start) | collective-permute-done | bytes 65568 | tf_op jit(solution)/shard_map/ppermute | solution.py:462
  13.7 0.2 collective-permute-done.1.refs_3_
  13.8 0.0 collective-permute-done.2.refs_4_
  13.8 0.0 collective-permute-done.3.refs_5_
  13.8 0.6 %shard_map.57 = (f32[40,128]{1,0:T(8,128)S(1)}, bf16[64,256]{1,0:T(8,128)(2,1)S(1)}, bf16[64,1024]{1,0:T(8,128)(2,1)S(1)}, bf16[64,1024]{1,0:T(8,128)(2,1)S(1)}) custom-call(f32[128,128]{1,0:T(8,128)S(1)} %get-tuple-element.17.refs_0_, f32[128,128]{1,0:T(8,128)S(1)} %get-tuple-element.18.refs_1_, ...), custom_call_target="tpu_custom_call", output_to_operand_aliasing={{2}: (4, {}), {3}: (5, {})} | custom-call | bytes 3700000 | tf_op jit(solution)/shard_map/pallas_call | solution.py:195
  14.4 0.5 %collective-permute-start.9 = (bf16[64,1024]{1,0:T(8,128)(2,1)S(1)}, bf16[64,1024]{1,0:T(8,128)(2,1)S(1)}, u32[]{:S(2)}, u32[]{:S(2)}) collective-permute-start(bf16[64,1024]{1,0:T(8,128)(2,1)S(1)} %get-tuple-element.24.rest_4_), channel_id=1, source_target_pairs={{0,4},{2,6},{4,0},{6,2},{8,12},{10,14},{12,8},{14,10},{1,5},{3,7},... | collective-permute-start | bytes 393224 | tf_op jit(solution)/shard_map/ppermute | solution.py:68
  14.9 1.5 %collective-permute-start.4 = (f32[40,128]{1,0:T(8,128)S(1)}, f32[40,128]{1,0:T(8,128)S(1)}, u32[]{:S(2)}, u32[]{:S(2)}) collective-permute-start(f32[40,128]{1,0:T(8,128)S(1)} %get-tuple-element.19.refs_0_), channel_id=1, source_target_pairs={{0,2},{2,0},{4,6},{6,4},{8,10},{10,8},{12,14},{14,12},{1,3},{3,1},... | collective-permute-start | bytes 61448 | tf_op jit(solution)/shard_map/ppermute | solution.py:68
  16.4 0.5 %collective-permute-start.8 = (bf16[64,256]{1,0:T(8,128)(2,1)S(1)}, bf16[64,256]{1,0:T(8,128)(2,1)S(1)}, u32[]{:S(2)}, u32[]{:S(2)}) collective-permute-start(bf16[64,256]{1,0:T(8,128)(2,1)S(1)} %get-tuple-element.22.rest_0_), channel_id=1, source_target_pairs={{0,2},{2,0},{4,6},{6,4},{8,10},{10,8},{12,14},{14,12},{1,3},{3,1},... | collective-permute-start | bytes 98312 | tf_op jit(solution)/shard_map/ppermute | solution.py:68
  16.9 1.8 %collective-permute-done.4.refs_1_ = f32[40,128]{1,0:T(8,128)S(1)} collective-permute-done((f32[40,128]{1,0:T(8,128)S(1)}, f32[40,128]{1,0:T(8,128)S(1)}, u32[]{:S(2)}, u32[]{:S(2)}) %collective-permute-start.4) | collective-permute-done | bytes 20512 | tf_op jit(solution)/shard_map/ppermute | solution.py:68
  18.6 1.3 %collective-permute-start.5 = (f32[40,128]{1,0:T(8,128)S(1)}, f32[40,128]{1,0:T(8,128)S(1)}, u32[]{:S(2)}, u32[]{:S(2)}) collective-permute-start(f32[40,128]{1,0:T(8,128)S(1)} %shard_map.58.refs_0_), channel_id=1, source_target_pairs={{0,12},{2,14},{4,8},{6,10},{8,4},{10,6},{12,0},{14,2},{1,13},{3,15... | collective-permute-start | bytes 61448 | tf_op jit(solution)/shard_map/ppermute | solution.py:68
  20.0 0.7 %collective-permute-start.6 = (f32[40,128]{1,0:T(8,128)S(1)}, f32[40,128]{1,0:T(8,128)S(1)}, u32[]{:S(2)}, u32[]{:S(2)}) collective-permute-start(f32[40,128]{1,0:T(8,128)S(1)} %shard_map.58.refs_0_), channel_id=1, source_target_pairs={{0,4},{2,6},{4,0},{6,2},{8,12},{10,14},{12,8},{14,10},{1,5},{3,7},... | collective-permute-start | bytes 61448 | tf_op jit(solution)/shard_map/ppermute | solution.py:68
  20.7 2.3 %collective-permute-start.7 = (f32[40,128]{1,0:T(8,128)S(1)}, f32[40,128]{1,0:T(8,128)S(1)}, u32[]{:S(2)}, u32[]{:S(2)}) collective-permute-start(f32[40,128]{1,0:T(8,128)S(1)} %shard_map.58.refs_0_), channel_id=1, source_target_pairs={{0,8},{2,10},{4,12},{6,14},{8,0},{10,2},{12,4},{14,6},{1,9},{3,11}... | collective-permute-start | bytes 61448 | tf_op jit(solution)/shard_map/ppermute | solution.py:68
  23.0 1.2 %collective-permute-done.5.refs_1_ = f32[40,128]{1,0:T(8,128)S(1)} collective-permute-done((f32[40,128]{1,0:T(8,128)S(1)}, f32[40,128]{1,0:T(8,128)S(1)}, u32[]{:S(2)}, u32[]{:S(2)}) %collective-permute-start.5) | collective-permute-done | bytes 20512 | tf_op jit(solution)/shard_map/ppermute | solution.py:68
  24.2 0.0 collective-permute-done.6.refs_2_
  24.2 1.2 %collective-permute-done.7.refs_3_ = f32[40,128]{1,0:T(8,128)S(1)} collective-permute-done((f32[40,128]{1,0:T(8,128)S(1)}, f32[40,128]{1,0:T(8,128)S(1)}, u32[]{:S(2)}, u32[]{:S(2)}) %collective-permute-start.7) | collective-permute-done | bytes 20512 | tf_op jit(solution)/shard_map/ppermute | solution.py:68
  25.4 2.7 %shard_map.59 = (bf16[192,64]{1,0:T(8,128)(2,1)S(1)}, bf16[3,256,256]{2,1,0:T(8,128)(2,1)S(1)}) custom-call(f32[40,128]{1,0:T(8,128)S(1)} %shard_map.58.refs_0_, f32[40,128]{1,0:T(8,128)S(1)} %collective-permute-done.5.refs_1_, f32[40,128]{1,0:T(8,128)S(1)} %collective-permute-done.6.refs_2_, f32[40,128]{1,0:T(8,128)S(1)} %collective-permute-done.7.refs_3_), custom_call_target="tpu_custom_call" | custom-call | bytes 14800000 | tf_op jit(solution)/shard_map/pallas_call | solution.py:356
  28.1 0.0 collective-permute-done.8.rest_1_
  28.1 0.0 collective-permute-done.9.rest_5_
  28.1 2.2 %shard_map.60 = (f32[2,256]{1,0:T(2,128)S(1)}, f32[2,256]{1,0:T(2,128)S(1)}, f32[2,256]{1,0:T(2,128)S(1)}, f32[2,256]{1,0:T(2,128)S(1)}) custom-call(bf16[192,64]{1,0:T(8,128)(2,1)S(1)} %get-tuple-element.20.left_ref, bf16[3,256,256]{2,1,0:T(8,128)(2,1)S(1)} %get-tuple-element.21.weights, bf16[64,256]{1,0:T(8,128)(2,1)S(1)} %get-tuple-element.22.rest_0_, ...), custom_call_target="tpu_custom_call" | custom-call | bytes 14800000 | tf_op jit(solution)/shard_map/pallas_call | solution.py:441
  30.4 1.4 %collective-permute-start.11 = (f32[2,256]{1,0:T(2,128)S(1)}, f32[2,256]{1,0:T(2,128)S(1)}, u32[]{:S(2)}, u32[]{:S(2)}) collective-permute-start(f32[2,256]{1,0:T(2,128)S(1)} %get-tuple-element.27), channel_id=1, source_target_pairs={{0,2},{2,0},{4,6},{6,4},{8,10},{10,8},{12,14},{14,12},{1,3},{3,1},... | collective-permute-start | bytes 6152 | tf_op jit(solution)/shard_map/ppermute | solution.py:68
  31.7 0.0 collective-permute-start.12
  31.7 0.8 %collective-permute-start.10 = (f32[2,256]{1,0:T(2,128)S(1)}, f32[2,256]{1,0:T(2,128)S(1)}, u32[]{:S(2)}, u32[]{:S(2)}) collective-permute-start(f32[2,256]{1,0:T(2,128)S(1)} %get-tuple-element.26), channel_id=1, source_target_pairs={{0,3},{1,2},{2,1},{3,0},{4,7},{5,6},{6,5},{7,4},{8,11},{9,10},{10,... | collective-permute-start | bytes 6152 | tf_op jit(solution)/shard_map/ppermute | solution.py:475
  32.6 1.4 %collective-permute-done.11 = f32[2,256]{1,0:T(2,128)S(1)} collective-permute-done((f32[2,256]{1,0:T(2,128)S(1)}, f32[2,256]{1,0:T(2,128)S(1)}, u32[]{:S(2)}, u32[]{:S(2)}) %collective-permute-start.11) | collective-permute-done | bytes 2080 | tf_op jit(solution)/shard_map/ppermute | solution.py:68
  34.0 0.0 collective-permute-done.12
  34.0 0.7 %collective-permute-done.10 = f32[2,256]{1,0:T(2,128)S(1)} collective-permute-done((f32[2,256]{1,0:T(2,128)S(1)}, f32[2,256]{1,0:T(2,128)S(1)}, u32[]{:S(2)}, u32[]{:S(2)}) %collective-permute-start.10) | collective-permute-done | bytes 2080 | tf_op jit(solution)/shard_map/ppermute | solution.py:475
  34.7 0.6 %add_add_fusion = f32[2,256]{1,0:T(2,128)} fusion(f32[2,256]{1,0:T(2,128)S(1)} %collective-permute-done.11, f32[2,256]{1,0:T(2,128)S(1)} %collective-permute-done.12, f32[2,256]{1,0:T(2,128)S(1)} %get-tuple-element.25, f32[2,256]{1,0:T(2,128)S(1)} %collective-permute-done.10), kind=kLoop, calls=%fused_computation | loop fusion | flops 1536 | bytes 10240 | tf_op jit(solution)/shard_map/add | solution.py:475
  (1 shorter events, 0.0 us)
Async XLA Ops:
  0.0 0.9 %copy-start = (bf16[16,64,64]{2,1,0:T(8,128)(2,1)S(1)}, bf16[16,64,64]{2,1,0:T(8,128)(2,1)}, u32[]{:S(2)}) copy-start(bf16[16,64,64]{2,1,0:T(8,128)(2,1)} %q_ref.1) | copy-start | bytes 393220
  1.1 12.7 %collective-permute-start.2 = (bf16[64,1024]{1,0:T(8,128)(2,1)S(1)}, bf16[64,1024]{1,0:T(8,128)(2,1)S(1)}, u32[]{:S(2)}, u32[]{:S(2)}) collective-permute-start(bf16[64,1024]{1,0:T(8,128)(2,1)S(1)} %shard_map.55.after_ref.rest_2_), channel_id=1, source_target_pairs={{0,8},{2,10},{4,12},{6,14},{8,0},{10,2},{12,4},{14,6},{1,9},{3,11}... | collective-permute-start | bytes 393224 | tf_op jit(solution)/shard_map/ppermute | solution.py:68
  5.2 8.6 %collective-permute-start.3 = (bf16[64,1024]{1,0:T(8,128)(2,1)S(1)}, bf16[64,1024]{1,0:T(8,128)(2,1)S(1)}, u32[]{:S(2)}, u32[]{:S(2)}) collective-permute-start(bf16[64,1024]{1,0:T(8,128)(2,1)S(1)} %shard_map.55.after_ref.rest_2_), channel_id=1, source_target_pairs={{0,4},{2,6},{4,0},{6,2},{8,12},{10,14},{12,8},{14,10},{1,5},{3,7},... | collective-permute-start | bytes 393224 | tf_op jit(solution)/shard_map/ppermute | solution.py:68
  12.3 1.3 %collective-permute-start = (f32[128,128]{1,0:T(8,128)S(1)}, f32[128,128]{1,0:T(8,128)S(1)}, u32[]{:S(2)}, u32[]{:S(2)}) collective-permute-start(f32[128,128]{1,0:T(8,128)S(1)} %get-tuple-element.17.refs_0_), channel_id=1, source_target_pairs={{0,1},{1,0},{2,3},{3,2},{4,5},{5,4},{6,7},{7,6},{8,9},{9,8},{10,11... | collective-permute-start | bytes 196616 | tf_op jit(solution)/shard_map/ppermute | solution.py:462
  12.4 1.4 %collective-permute-start.1 = (f32[128,128]{1,0:T(8,128)S(1)}, f32[128,128]{1,0:T(8,128)S(1)}, u32[]{:S(2)}, u32[]{:S(2)}) collective-permute-start(f32[128,128]{1,0:T(8,128)S(1)} %get-tuple-element.18.refs_1_), channel_id=1, source_target_pairs={{0,1},{1,0},{2,3},{3,2},{4,5},{5,4},{6,7},{7,6},{8,9},{9,8},{10,11... | collective-permute-start | bytes 196616 | tf_op jit(solution)/shard_map/ppermute | solution.py:462
  14.4 13.7 %collective-permute-start.9 = (bf16[64,1024]{1,0:T(8,128)(2,1)S(1)}, bf16[64,1024]{1,0:T(8,128)(2,1)S(1)}, u32[]{:S(2)}, u32[]{:S(2)}) collective-permute-start(bf16[64,1024]{1,0:T(8,128)(2,1)S(1)} %get-tuple-element.24.rest_4_), channel_id=1, source_target_pairs={{0,4},{2,6},{4,0},{6,2},{8,12},{10,14},{12,8},{14,10},{1,5},{3,7},... | collective-permute-start | bytes 393224 | tf_op jit(solution)/shard_map/ppermute | solution.py:68
  14.9 3.8 %collective-permute-start.4 = (f32[40,128]{1,0:T(8,128)S(1)}, f32[40,128]{1,0:T(8,128)S(1)}, u32[]{:S(2)}, u32[]{:S(2)}) collective-permute-start(f32[40,128]{1,0:T(8,128)S(1)} %get-tuple-element.19.refs_0_), channel_id=1, source_target_pairs={{0,2},{2,0},{4,6},{6,4},{8,10},{10,8},{12,14},{14,12},{1,3},{3,1},... | collective-permute-start | bytes 61448 | tf_op jit(solution)/shard_map/ppermute | solution.py:68
  16.4 11.7 %collective-permute-start.8 = (bf16[64,256]{1,0:T(8,128)(2,1)S(1)}, bf16[64,256]{1,0:T(8,128)(2,1)S(1)}, u32[]{:S(2)}, u32[]{:S(2)}) collective-permute-start(bf16[64,256]{1,0:T(8,128)(2,1)S(1)} %get-tuple-element.22.rest_0_), channel_id=1, source_target_pairs={{0,2},{2,0},{4,6},{6,4},{8,10},{10,8},{12,14},{14,12},{1,3},{3,1},... | collective-permute-start | bytes 98312 | tf_op jit(solution)/shard_map/ppermute | solution.py:68
  18.6 5.6 %collective-permute-start.5 = (f32[40,128]{1,0:T(8,128)S(1)}, f32[40,128]{1,0:T(8,128)S(1)}, u32[]{:S(2)}, u32[]{:S(2)}) collective-permute-start(f32[40,128]{1,0:T(8,128)S(1)} %shard_map.58.refs_0_), channel_id=1, source_target_pairs={{0,12},{2,14},{4,8},{6,10},{8,4},{10,6},{12,0},{14,2},{1,13},{3,15... | collective-permute-start | bytes 61448 | tf_op jit(solution)/shard_map/ppermute | solution.py:68
  20.0 4.2 %collective-permute-start.6 = (f32[40,128]{1,0:T(8,128)S(1)}, f32[40,128]{1,0:T(8,128)S(1)}, u32[]{:S(2)}, u32[]{:S(2)}) collective-permute-start(f32[40,128]{1,0:T(8,128)S(1)} %shard_map.58.refs_0_), channel_id=1, source_target_pairs={{0,4},{2,6},{4,0},{6,2},{8,12},{10,14},{12,8},{14,10},{1,5},{3,7},... | collective-permute-start | bytes 61448 | tf_op jit(solution)/shard_map/ppermute | solution.py:68
  20.7 4.7 %collective-permute-start.7 = (f32[40,128]{1,0:T(8,128)S(1)}, f32[40,128]{1,0:T(8,128)S(1)}, u32[]{:S(2)}, u32[]{:S(2)}) collective-permute-start(f32[40,128]{1,0:T(8,128)S(1)} %shard_map.58.refs_0_), channel_id=1, source_target_pairs={{0,8},{2,10},{4,12},{6,14},{8,0},{10,2},{12,4},{14,6},{1,9},{3,11}... | collective-permute-start | bytes 61448 | tf_op jit(solution)/shard_map/ppermute | solution.py:68
  30.4 3.7 %collective-permute-start.11 = (f32[2,256]{1,0:T(2,128)S(1)}, f32[2,256]{1,0:T(2,128)S(1)}, u32[]{:S(2)}, u32[]{:S(2)}) collective-permute-start(f32[2,256]{1,0:T(2,128)S(1)} %get-tuple-element.27), channel_id=1, source_target_pairs={{0,2},{2,0},{4,6},{6,4},{8,10},{10,8},{12,14},{14,12},{1,3},{3,1},... | collective-permute-start | bytes 6152 | tf_op jit(solution)/shard_map/ppermute | solution.py:68
  31.7 2.3 %collective-permute-start.12 = (f32[2,256]{1,0:T(2,128)S(1)}, f32[2,256]{1,0:T(2,128)S(1)}, u32[]{:S(2)}, u32[]{:S(2)}) collective-permute-start(f32[2,256]{1,0:T(2,128)S(1)} %get-tuple-element.28), channel_id=1, source_target_pairs={{0,1},{1,0},{2,3},{3,2},{4,5},{5,4},{6,7},{7,6},{8,9},{9,8},{10,11... | collective-permute-start | bytes 6152 | tf_op jit(solution)/shard_map/ppermute | solution.py:476
  31.7 3.0 %collective-permute-start.10 = (f32[2,256]{1,0:T(2,128)S(1)}, f32[2,256]{1,0:T(2,128)S(1)}, u32[]{:S(2)}, u32[]{:S(2)}) collective-permute-start(f32[2,256]{1,0:T(2,128)S(1)} %get-tuple-element.26), channel_id=1, source_target_pairs={{0,3},{1,2},{2,1},{3,0},{4,7},{5,6},{6,5},{7,4},{8,11},{9,10},{10,... | collective-permute-start | bytes 6152 | tf_op jit(solution)/shard_map/ppermute | solution.py:475
